TPU v7x, 256 devices: a whole 4x4x8 slice. The times are simulated.
256 devices in a mesh: batch: 32 (over x, y, core), tensor: 8 (over z).
Axes of the slice: x: 4, y: 4, z: 8, core: 2. Of those that a mesh axis runs over, the one named last changes fastest.
Arguments:
- residual: bfloat16 [256, 2, 4096], P('batch', None, 'tensor'), may hold values from -64 to 64
- new_queries: bfloat16 [256, 2, 2048], P('batch', None, 'tensor'), may hold values from -5 to 5
- new_keys: bfloat16 [256, 2, 2048], P('batch', None, 'tensor'), may hold values from -5 to 5
- new_values: bfloat16 [256, 2, 2048], P('batch', None, 'tensor'), may hold values from -5 to 5
- cache_keys: bfloat16 [256, 256, 2048], P('batch', None, 'tensor'), may hold values from -5 to 5
- cache_values: bfloat16 [256, 256, 2048], P('batch', None, 'tensor'), may hold values from -5 to 5
- lengths: int32 [256], P('batch'), may hold values from 2 to 256, as said below
- out_weight: bfloat16 [2048, 4096], P('tensor'), may hold values from -0.5 to 0.5
- temporal_gain: bfloat16 [4096], P('tensor'), may hold values from 0.099609375 to 1.8984375
- in_weight: bfloat16 [4096, 1024], P('tensor'), may hold values from -0.09375 to 0.09375
- tokens: int32 [256, 2, 8], P(('batch', 'tensor')), may hold values from 0 to 2047
- level_tables: bfloat16 [8, 2048, 1024], P(None, 'batch'), may hold values from -5 to 5
- depth_gain: bfloat16 [1024], replicated, may hold values from 0.099609375 to 1.8984375
- depth_qkv: bfloat16 [1024, 1536], replicated, may hold values from -0.1875 to 0.1875
- depth_out: bfloat16 [512, 1024], replicated, may hold values from -0.25 to 0.25
Outputs:
- temporal_out: bfloat16 [256, 2, 4096], P('batch', None, 'tensor')
- depth_states: bfloat16 [256, 2, 8, 1024], P(('batch', 'tensor'))
Inputs may be any that keep to these rules, and one draw needn't show every extreme that they name: `lengths`: each dialogue has between 2 and 256 live cache slots, the first ones; in every draw some dialogue has exactly 256.
All inputs are finite; a program needn't handle non-finite values.
Results may differ from a plain program's by a relative error of at most 0.02.
Values may be sent and summed in bfloat16 or wider, within the bound.
No kernel may reach another device: no remote copies, remote signals or barrier semaphores. Data moves between devices by JAX's collectives and lax.ppermute only.
A program may use at most 64 MiB of HBM per device.

v0:
```python
import math

import jax
import jax.numpy as jnp
from jax import lax
from jax.sharding import PartitionSpec as P

D = 4096
HD = 128
DHD = 64
DHEADS = 8
LEVELS = 8
FRAMES = 2


def inverse_rms(values, count):
    return lax.rsqrt(jnp.sum(values * values, axis=-1, keepdims=True) / count + 1e-05)


def per_device(
    residual,
    new_queries,
    new_keys,
    new_values,
    cache_keys,
    cache_values,
    lengths,
    out_weight,
    temporal_gain,
    in_weight,
    tokens,
    level_tables,
    depth_gain,
    depth_qkv,
    depth_out,
):
    held_dialogues = residual.shape[0]
    features = residual.shape[2]
    head_width = new_queries.shape[2]
    head_count = head_width // HD
    cache_len = cache_keys.shape[1]
    score_scale = 1.0 / math.sqrt(HD)
    queries = new_queries.reshape(held_dialogues, FRAMES, head_count, HD)
    fresh_keys = new_keys.reshape(held_dialogues, FRAMES, head_count, HD)
    fresh_values = new_values.reshape(held_dialogues, FRAMES, head_count, HD)
    past_keys = cache_keys.reshape(held_dialogues, cache_len, head_count, HD)
    past_values = cache_values.reshape(held_dialogues, cache_len, head_count, HD)
    live_slots = (jnp.arange(cache_len, dtype=jnp.int32)[None, :] < lengths[:, None])[
        :, None, None, :
    ]
    frame_mask = jnp.arange(FRAMES)[:, None] >= jnp.arange(FRAMES)[None, :]
    score_cache = (
        jnp.einsum("dfhe,dche->dhfc", queries, past_keys, preferred_element_type=jnp.float32)
        * score_scale
    )
    score_cache = jnp.where(live_slots, score_cache, -jnp.inf)
    score_fresh = (
        jnp.einsum("dfhe,dghe->dhfg", queries, fresh_keys, preferred_element_type=jnp.float32)
        * score_scale
    )
    score_fresh = jnp.where(frame_mask[None, None], score_fresh, -jnp.inf)
    largest = jnp.maximum(
        jnp.max(score_cache, axis=-1, keepdims=True), jnp.max(score_fresh, axis=-1, keepdims=True)
    )
    exp_cache = jnp.exp(score_cache - largest)
    exp_fresh = jnp.exp(score_fresh - largest)
    total = jnp.sum(exp_cache, axis=-1, keepdims=True) + jnp.sum(exp_fresh, axis=-1, keepdims=True)
    prob_cache = (exp_cache / total).astype(jnp.bfloat16)
    prob_fresh = (exp_fresh / total).astype(jnp.bfloat16)
    attended = jnp.einsum(
        "dhfc,dche->dfhe", prob_cache, past_values, preferred_element_type=jnp.float32
    )
    attended = attended + jnp.einsum(
        "dhfg,dghe->dfhe", prob_fresh, fresh_values, preferred_element_type=jnp.float32
    )
    attended = attended.astype(jnp.bfloat16).reshape(held_dialogues * FRAMES, head_width)
    head_terms = jnp.dot(attended, out_weight, preferred_element_type=jnp.float32).reshape(
        held_dialogues, FRAMES, -1
    )
    shares = lax.psum_scatter(
        head_terms.astype(jnp.bfloat16), "tensor", scatter_dimension=2, tiled=True
    ).astype(jnp.float32)
    hidden = residual.astype(jnp.float32) + shares
    squares = lax.psum(jnp.sum(hidden * hidden, axis=-1, keepdims=True), "tensor")
    inverse = lax.rsqrt(squares / D + 1e-05)
    temporal_out = hidden.astype(jnp.bfloat16)
    normed = (hidden * inverse * temporal_gain.astype(jnp.float32)).astype(jnp.bfloat16)
    owned_dialogues = held_dialogues // lax.axis_size("tensor")
    product = jnp.dot(
        normed.reshape(owned_dialogues * lax.axis_size("tensor") * FRAMES, features),
        in_weight,
        preferred_element_type=jnp.float32,
    )
    depth_proj = lax.psum_scatter(
        product.reshape(owned_dialogues * lax.axis_size("tensor"), FRAMES, -1).astype(jnp.bfloat16),
        "tensor",
        scatter_dimension=0,
        tiled=True,
    ).astype(jnp.float32)
    gathered_ids = lax.all_gather(tokens, "batch", axis=0, tiled=True)
    vocab_span = level_tables.shape[1]
    vocab_start = lax.axis_index("batch") * vocab_span
    one_hot = (
        gathered_ids[..., None] == vocab_start + jnp.arange(vocab_span, dtype=jnp.int32)
    ).astype(jnp.bfloat16)
    partial_value = jnp.einsum(
        "rflv,lve->rfle", one_hot, level_tables, preferred_element_type=jnp.float32
    )
    table_rows = lax.psum_scatter(
        partial_value.astype(jnp.bfloat16), "batch", scatter_dimension=0, tiled=True
    ).astype(jnp.float32)
    depth_input = depth_proj[:, :, None, :] + table_rows
    depth_width = depth_input.shape[3]
    depth_normed = (
        depth_input * inverse_rms(depth_input, depth_width) * depth_gain.astype(jnp.float32)
    ).astype(jnp.bfloat16)
    projected = jnp.dot(
        depth_normed.reshape(-1, depth_width), depth_qkv, preferred_element_type=jnp.float32
    ).astype(jnp.bfloat16)
    projected = projected.reshape(owned_dialogues, FRAMES, LEVELS, 3, DHEADS, DHD)
    depth_query = projected[:, :, :, 0]
    depth_key = projected[:, :, :, 1]
    depth_value = projected[:, :, :, 2]
    depth_scores = jnp.einsum(
        "aflhe,afmhe->afhlm", depth_query, depth_key, preferred_element_type=jnp.float32
    ) / math.sqrt(DHD)
    causal_mask = jnp.arange(LEVELS)[:, None] >= jnp.arange(LEVELS)[None, :]
    depth_exp = jnp.where(causal_mask, jnp.exp(depth_scores), 0.0)
    depth_probs = (depth_exp / jnp.sum(depth_exp, axis=-1, keepdims=True)).astype(jnp.bfloat16)
    depth_mixed = jnp.einsum(
        "afhlm,afmhe->aflhe", depth_probs, depth_value, preferred_element_type=jnp.float32
    )
    depth_mixed = depth_mixed.astype(jnp.bfloat16).reshape(-1, DHEADS * DHD)
    depth_states = depth_input + jnp.dot(
        depth_mixed, depth_out, preferred_element_type=jnp.float32
    ).reshape(owned_dialogues, FRAMES, LEVELS, depth_width)
    return (temporal_out, depth_states.astype(jnp.bfloat16))


def solution(mesh):
    placed = (
        P("batch", None, "tensor"),
        P("batch", None, "tensor"),
        P("batch", None, "tensor"),
        P("batch", None, "tensor"),
        P("batch", None, "tensor"),
        P("batch", None, "tensor"),
        P("batch"),
        P("tensor", None),
        P("tensor"),
        P("tensor", None),
        P(("batch", "tensor"), None, None),
        P(None, "batch", None),
        P(),
        P(),
        P(),
    )
    return jax.shard_map(
        per_device,
        mesh=mesh,
        in_specs=placed,
        out_specs=(P("batch", None, "tensor"), P(("batch", "tensor"), None, None, None)),
        check_vma=False,
    )
```

profile of v0, /device:TPU:4, one launch (start us, length us, event | category | flops | bytes accessed | tf_op | source)
XLA Modules:
  0.0 154.7 jit_solution(15553188211024825694)
XLA Ops:
  7.2 0.0 copy-start
  7.2 0.0 copy-start.6
  7.2 0.0 reduce-scatter.3.cloned.1.call-start
  7.2 0.9 iota_compare_fusion
  8.1 1.7 %fusion.46 = (f32[8,2,2]{2,1,0:T(2,128)S(1)}, f32[8,2,2,256]{3,2,1,0:T(2,128)S(1)}) fusion(bf16[8,2,256]{2,1,0:T(2,128)(2,1)} %param.16, pred[8,256]{1,0:T(8,128)(4,1)S(1)} %iota_compare_fusion, bf16[8,256,256]{2,1,0:T(8,128)(2,1)} %param.19), kind=kOutput, calls=%fused_computation.75 | convolution fusion | flops 2121696 | bytes 1091712 | tf_op jit(solution)/shard_map/dfhe,dche->dhfc/dot_general | solution.py:53
  9.9 0.9 fusion.47
  10.8 0.2 fusion.30
  11.0 0.0 copy-start.4
  11.0 1.5 fusion.11
  12.6 0.0 copy-done.6
  12.6 0.2 fusion.10
  12.8 2.6 %convolution_convert_fusion = bf16[8,2,4096]{2,0,1:T(8,128)(2,1)} fusion(bf16[8,2,256]{2,0,1:T(8,128)(2,1)S(1)} %dot_general.41, bf16[256,4096]{1,0:T(8,128)(2,1)} %param.22), kind=kOutput, calls=%fused_computation | convolution fusion | flops 33619968 | bytes 2236416 | tf_op jit(solution)/shard_map/dot_general | solution.py:77
  15.5 0.0 reduce-scatter.3.cloned.1.call-update
  15.5 0.0 reduce-scatter.5.cloned.1.call-start
  15.5 0.0 copy-done.4
  15.5 22.9 %all_gather.3 = s32[32,2,8]{2,1,0:T(2,128)S(1)} all-gather(s32[1,2,8]{2,1,0:T(2,128)S(1)} %copy-done.4), channel_id=1, replica_groups=mesh['batch'=32,'tensor'=8] {'batch'}, dimensions={0}, use_global_device_ids=true | all-gather | bytes 2112 | tf_op jit(solution)/shard_map/all_gather | solution.py:100
  38.4 0.1 copy.62
  38.5 1.7 %fusion.1 = bf16[32,2,8,1024]{3,0,1,2:T(8,128)(2,1)S(1)} fusion(bf16[8,64,1024]{2,1,0:T(8,128)(2,1)} %param.26, s32[64]{0:T(128)S(1)} %iota_add_fusion, s32[32,2,8]{0,1,2:T(2,128)S(1)} %copy.62), kind=kOutput, calls=%fused_computation.4 | convolution fusion | flops 67665920 | bytes 2099456 | tf_op jit(solution)/shard_map/rflv,lve->rfle/dot_general | solution.py:106
  40.2 0.0 copy-start.5
  40.2 0.0 copy-start.3
  40.3 0.0 copy-start.7
  40.3 0.0 copy-start.2
  40.3 1.6 %copy.63 = bf16[32,2,8,1024]{3,2,1,0:T(8,128)(2,1)} copy(bf16[32,2,8,1024]{3,0,1,2:T(8,128)(2,1)S(1)} %fusion.1) | data formatting | bytes 2097152 | tf_op jit(solution)/shard_map/convert_element_type | solution.py:110
  41.8 0.0 reduce-scatter.5.cloned.1.call-update
  41.9 0.0 copy-done.5
  41.9 0.0 copy-done.3
  41.9 0.0 copy-done.7
  41.9 0.6 dynamic-slice
  42.5 12.6 %reduce-scatter.3.cloned.1.call-done = bf16[8,2,512]{2,0,1:T(8,128)(2,1)} async-done(((bf16[8,2,4096]{2,0,1:T(8,128)(2,1)}), bf16[8,2,512]{2,0,1:T(8,128)(2,1)}) %reduce-scatter.3.cloned.1.call-update) | async-done | bytes 16400 | tf_op jit(solution)/shard_map/reduce_scatter | solution.py:80
  55.1 0.0 copy-done.2
  55.1 0.8 multiply_reduce_fusion.1
  55.9 15.5 %psum.7 = f32[8,2,1]{0,1,2:T(2,128)S(1)} all-reduce(f32[8,2,1]{0,1,2:T(2,128)S(1)} %bitcast.93), channel_id=1, replica_groups=mesh['batch'=32,'tensor'=8] {'tensor'}, use_global_device_ids=true, to_apply=%region_6.7 | all-reduce | flops 16 | bytes 128 | tf_op jit(solution)/shard_map/psum | solution.py:84
  71.4 1.5 convolution_convert_fusion.4
  73.0 0.6 copy.69
  73.6 27.6 %all-reduce = bf16[8,2,1024]{2,1,0:T(2,128)(2,1)S(1)} all-reduce(bf16[8,2,1024]{2,1,0:T(2,128)(2,1)S(1)} %copy.61), channel_id=3, replica_groups=mesh['batch'=32,'tensor'=8] {'tensor'}, use_global_device_ids=true, to_apply=%region_7.8.clone | all-reduce | flops 16384 | bytes 65536
  101.2 0.7 bitcast_convert_fusion
  101.8 41.0 %reduce-scatter.5.cloned.1.call-done = bf16[1,2,8,1024]{3,2,1,0:T(8,128)(2,1)} async-done(((bf16[32,2,8,1024]{3,2,1,0:T(8,128)(2,1)}), bf16[1,2,8,1024]{3,2,1,0:T(8,128)(2,1)}) %reduce-scatter.5.cloned.1.call-update) | async-done | bytes 32784 | tf_op jit(solution)/shard_map/reduce_scatter | solution.py:109
  142.8 0.9 multiply_reduce_fusion
  143.7 0.0 copy-start.1
  143.7 0.0 copy-done
  143.7 1.4 convolution_convert_fusion.1
  145.1 0.1 reshape.142
  145.2 0.1 fusion.4
  145.4 0.2 fusion.6
  145.6 0.1 reshape.146
  145.7 0.0 copy-done.1
  145.7 2.1 %fusion.5 = bf16[1,2,8,1024]{3,2,1,0:T(8,128)(2,1)} fusion(bf16[2,8,512]{2,1,0:T(8,128)(2,1)S(1)} %reshape.146, bf16[512,1024]{1,0:T(8,128)(2,1)} %param.29, bf16[1,2,8,1024]{3,2,1,0:T(8,128)(2,1)S(1)} %copy-done.1, f32[2,1024]{1,0:T(2,128)S(1)} %bitcast_convert_fusion), kind=kOutput, calls=%fused_computation.10 | convolution fusion | flops 16842752 | bytes 1138688 | tf_op jit(solution)/shard_map/dot_general | solution.py:134
  (15 shorter events, 0.2 us)
Async XLA Ops:
  7.2 136.5 %copy-start = (bf16[1024,1536]{1,0:T(8,128)(2,1)S(1)}, bf16[1024,1536]{1,0:T(8,128)(2,1)}, u32[]{:S(2)}) copy-start(bf16[1024,1536]{1,0:T(8,128)(2,1)} %param.28) | copy-start | bytes 9437188
  7.2 5.4 %copy-start.6 = (bf16[8,2,256]{2,1,0:T(2,128)(2,1)S(1)}, bf16[8,2,256]{2,1,0:T(2,128)(2,1)}, u32[]{:S(2)}) copy-start(bf16[8,2,256]{2,1,0:T(2,128)(2,1)} %param.18) | copy-start | bytes 24580
  7.2 47.9 %reduce-scatter.3.cloned.1.call-start = ((), (), s32[]{:S(2)}) async-start(), calls=%async_computation.2 | async-start | bytes 147456 | tf_op jit(solution)/shard_map/reduce_scatter | solution.py:80
  11.0 4.5 %copy-start.4 = (s32[1,2,8]{2,1,0:T(2,128)S(1)}, s32[1,2,8]{2,1,0:T(2,128)}, u32[]{:S(2)}) copy-start(s32[1,2,8]{2,1,0:T(2,128)} %param.25) | copy-start | bytes 196
  15.5 127.4 %reduce-scatter.5.cloned.1.call-start = ((), (), s32[]{:S(2)}) async-start(), calls=%async_computation.3 | async-start | bytes 1081344 | tf_op jit(solution)/shard_map/reduce_scatter | solution.py:109
  40.2 1.7 %copy-start.5 = (bf16[512]{0:T(512)(128)(2,1)S(1)}, bf16[512]{0:T(512)(128)(2,1)}, u32[]{:S(2)}) copy-start(bf16[512]{0:T(512)(128)(2,1)} %param.23) | copy-start | bytes 3076
  40.2 1.7 %copy-start.3 = (bf16[1024]{0:T(1024)(128)(2,1)S(1)}, bf16[1024]{0:T(1024)(128)(2,1)}, u32[]{:S(2)}) copy-start(bf16[1024]{0:T(1024)(128)(2,1)} %param.27) | copy-start | bytes 6148
  40.3 1.7 %copy-start.7 = (u32[256]{0:T(256)S(1)}, u32[256]{0:T(256)}, u32[]{:S(2)}) copy-start(u32[256]{0:T(256)} %constant.37) | copy-start | bytes 3076
  40.3 14.8 %copy-start.2 = (bf16[8,2,512]{2,1,0:T(2,128)(2,1)S(1)}, bf16[8,2,512]{2,1,0:T(2,128)(2,1)}, u32[]{:S(2)}) copy-start(bf16[8,2,512]{2,1,0:T(2,128)(2,1)} %param.15) | copy-start | bytes 49156
  143.7 2.0 %copy-start.1 = (bf16[1,2,8,1024]{3,2,1,0:T(8,128)(2,1)S(1)}, bf16[1,2,8,1024]{3,2,1,0:T(8,128)(2,1)}, u32[]{:S(2)}) copy-start(bf16[1,2,8,1024]{3,2,1,0:T(8,128)(2,1)} %reduce-scatter.5.cloned.1.call-done) | copy-start | bytes 98308
Sparse Core Ops, SparseCore 0:
  15.6 39.4 reduce-scatter.2
  59.3 83.4 reduce-scatter.4
where the time goes:
time: 155 us
  blocking collectives  65.9 us (43%)
  waiting for transfers between devices  53.6 us (35%)
  between operations  14.3 us (9%)
  matrix products  14.1 us (9%)
  other arithmetic  3.47 us (2%)
  local copies, waits for them, and re-layouts  3.22 us (2%)
    reduce_scatter x1, waiting for transfers between devices, per_device(): lax.psum_scatter(partial_value.astype(jnp.bfloat16), 'batch', scatter_dim...  41 us
    unnamed x1, blocking collectives  27.6 us
    all_gather x1, blocking collectives, per_device(): gathered_ids = lax.all_gather(tokens, 'batch', axis=0, tiled=True)  22.9 us
    psum x1, blocking collectives, per_device(): lax.psum(jnp.sum(hidden * hidden, axis=-1, keepdims=True), 'tensor')  15.5 us
    reduce_scatter x1, waiting for transfers between devices, per_device(): lax.psum_scatter(head_terms.astype(jnp.bfloat16), 'tensor', scatter_dimen...  12.6 us
  transfers between devices with their start and end apart: 2, of which 2 were waited for; matrix products, arithmetic and copies ran while one was open for 5% of the time, Pallas kernels for 0%

commit v1 on v0

--- a/solution.py
+++ b/solution.py
@@ -74,42 +74,54 @@
         "dhfg,dghe->dfhe", prob_fresh, fresh_values, preferred_element_type=jnp.float32
     )
     attended = attended.astype(jnp.bfloat16).reshape(held_dialogues * FRAMES, head_width)
-    head_terms = jnp.dot(attended, out_weight, preferred_element_type=jnp.float32).reshape(
-        held_dialogues, FRAMES, -1
-    )
-    shares = lax.psum_scatter(
-        head_terms.astype(jnp.bfloat16), "tensor", scatter_dimension=2, tiled=True
-    ).astype(jnp.float32)
-    hidden = residual.astype(jnp.float32) + shares
-    squares = lax.psum(jnp.sum(hidden * hidden, axis=-1, keepdims=True), "tensor")
-    inverse = lax.rsqrt(squares / D + 1e-05)
-    temporal_out = hidden.astype(jnp.bfloat16)
-    normed = (hidden * inverse * temporal_gain.astype(jnp.float32)).astype(jnp.bfloat16)
-    owned_dialogues = held_dialogues // lax.axis_size("tensor")
-    product = jnp.dot(
-        normed.reshape(owned_dialogues * lax.axis_size("tensor") * FRAMES, features),
-        in_weight,
-        preferred_element_type=jnp.float32,
-    )
-    depth_proj = lax.psum_scatter(
-        product.reshape(owned_dialogues * lax.axis_size("tensor"), FRAMES, -1).astype(jnp.bfloat16),
-        "tensor",
-        scatter_dimension=0,
-        tiled=True,
-    ).astype(jnp.float32)
-    gathered_ids = lax.all_gather(tokens, "batch", axis=0, tiled=True)
+    tensor_size = lax.axis_size("tensor")
+    batch_size = lax.axis_size("batch")
+    rows = held_dialogues * FRAMES
+    owned_dialogues = held_dialogues // tensor_size
+
+    token_count = owned_dialogues * FRAMES * LEVELS
+    sent_ids = jnp.broadcast_to(tokens.reshape(1, token_count), (batch_size, token_count))
+    gathered_ids = lax.all_to_all(sent_ids, "batch", 0, 0, tiled=True)
     vocab_span = level_tables.shape[1]
     vocab_start = lax.axis_index("batch") * vocab_span
-    one_hot = (
-        gathered_ids[..., None] == vocab_start + jnp.arange(vocab_span, dtype=jnp.int32)
+    levels = jnp.arange(token_count, dtype=jnp.int32) % LEVELS
+    local_ids = gathered_ids - vocab_start
+    entry = jnp.where(
+        (local_ids >= 0) & (local_ids < vocab_span), local_ids + levels * vocab_span, -1
+    ).reshape(-1, 1)
+    one_hot = (entry == jnp.arange(LEVELS * vocab_span, dtype=jnp.int32)[None, :]).astype(
+        jnp.bfloat16
+    )
+    partial_rows = jnp.dot(
+        one_hot,
+        level_tables.reshape(LEVELS * vocab_span, -1),
+        preferred_element_type=jnp.float32,
     ).astype(jnp.bfloat16)
-    partial_value = jnp.einsum(
-        "rflv,lve->rfle", one_hot, level_tables, preferred_element_type=jnp.float32
+    received_rows = lax.all_to_all(
+        partial_rows.reshape(batch_size, token_count, -1), "batch", 0, 0, tiled=True
     )
-    table_rows = lax.psum_scatter(
-        partial_value.astype(jnp.bfloat16), "batch", scatter_dimension=0, tiled=True
-    ).astype(jnp.float32)
-    depth_input = depth_proj[:, :, None, :] + table_rows
+    table_rows = jnp.sum(received_rows.astype(jnp.float32), axis=0)
+
+    head_terms = jnp.dot(attended, out_weight, preferred_element_type=jnp.float32)
+    head_terms = head_terms.astype(jnp.bfloat16).reshape(rows, tensor_size, features)
+    head_terms = head_terms.transpose(1, 0, 2)
+    shares = lax.all_to_all(head_terms, "tensor", 0, 0, tiled=True)
+    shares = jnp.sum(shares.astype(jnp.float32), axis=0)
+    hidden = residual.astype(jnp.float32).reshape(rows, features) + shares
+    temporal_out = hidden.astype(jnp.bfloat16).reshape(held_dialogues, FRAMES, features)
+    squares = jnp.sum(hidden * hidden, axis=-1, keepdims=True)
+    scaled = (hidden * temporal_gain.astype(jnp.float32)).astype(jnp.bfloat16)
+    product = jnp.dot(scaled, in_weight, preferred_element_type=jnp.float32)
+    payload = jnp.concatenate([product, jnp.broadcast_to(squares, (rows, 128))], axis=1)
+    payload = payload.reshape(tensor_size, owned_dialogues * FRAMES, -1)
+    received = lax.all_to_all(payload, "tensor", 0, 0, tiled=True)
+    received = jnp.sum(received, axis=0)
+    depth_proj = received[:, :-128]
+    inverse = lax.rsqrt(received[:, -128:-127] / D + 1e-05)
+    depth_proj = (depth_proj * inverse).reshape(owned_dialogues, FRAMES, -1)
+    depth_input = depth_proj[:, :, None, :] + table_rows.reshape(
+        owned_dialogues, FRAMES, LEVELS, -1
+    )
     depth_width = depth_input.shape[3]
     depth_normed = (
         depth_input * inverse_rms(depth_input, depth_width) * depth_gain.astype(jnp.float32)

time: 155 us -> 80.1 us (0.52)
  the two profiles are of different devices: /device:TPU:4 before, /device:TPU:1 now
where the time goes in v1:
time: 80.1 us; the launch traced here: 79.5 us
  starting transfers between devices  30.5 us (38%)
  waiting for transfers between devices  28.7 us (36%)
  matrix products  12.2 us (15%)
  local copies, waits for them, and re-layouts  3.61 us (5%)
  other arithmetic  3.59 us (4%)
  between operations  0.86 us (1%)
    all_to_all x1, waiting for transfers between devices, per_device(): lax.all_to_all(partial_rows.reshape(batch_size, token_count, -1), 'batch'...  16.7 us
    all_to_all x1, starting transfers between devices, per_device(): lax.all_to_all(partial_rows.reshape(batch_size, token_count, -1), 'batch'...  10.4 us
    all_to_all x1, starting transfers between devices, per_device(): gathered_ids = lax.all_to_all(sent_ids, 'batch', 0, 0, tiled=True)  8.59 us
    all_to_all x1, starting transfers between devices, per_device(): shares = lax.all_to_all(head_terms, 'tensor', 0, 0, tiled=True)  8.19 us
    all_to_all x1, waiting for transfers between devices, per_device(): shares = lax.all_to_all(head_terms, 'tensor', 0, 0, tiled=True)  7.63 us
    all_to_all x1, waiting for transfers between devices, per_device(): received = lax.all_to_all(payload, 'tensor', 0, 0, tiled=True)  4.24 us
    all_to_all x1, starting transfers between devices, per_device(): received = lax.all_to_all(payload, 'tensor', 0, 0, tiled=True)  3.35 us
    dot_general x1, matrix products, per_device(): jnp.dot(one_hot, level_tables.reshape(LEVELS * vocab_span, -1), preferred...  2.98 us
  transfers between devices with their start and end apart: 4, of which 4 were waited for; matrix products, arithmetic and copies ran while one was open for 13% of the time, Pallas kernels for 0%

profile of v1, /device:TPU:1, one launch (start us, length us, event | category | flops | bytes accessed | tf_op | source)
XLA Modules:
  0.0 79.5 jit_solution(14460446623678268434)
XLA Ops:
  0.6 0.0 copy-start
  0.6 0.0 copy-start.5
  0.7 0.9 %broadcast_in_dim.75 = s32[16]{0:T(128)S(1)} reshape(s32[1,2,8]{2,1,0:T(2,128)} %param.25) | data formatting | bytes 128 | tf_op jit(solution)/shard_map/broadcast_in_dim | solution.py:83
  1.6 0.6 broadcast_in_dim.76
  2.2 8.6 %all-to-all-start.2 = ((s32[32,1,16]{2,1,0:T(1,128)}), s32[32,1,16]{2,1,0:T(1,128)S(1)}, u32[]{:S(2)}, u32[]{:S(2)}) async-start(s32[32,1,16]{2,1,0:T(1,128)} %broadcast_in_dim.76), calls=%async_computation.2 | async-start | bytes 32768 | tf_op jit(solution)/shard_map/all_to_all | solution.py:84
  10.8 0.0 copy-start.1
  10.8 0.9 %iota_compare_fusion.2 = pred[8,256]{1,0:T(8,128)(4,1)S(1)} fusion(s32[8]{0:T(128)} %param.21), kind=kLoop, calls=%fused_computation.63 | loop fusion | flops 2048 | bytes 2080 | tf_op jit(solution)/shard_map/lt | solution.py:48
  11.7 1.7 %fusion.46 = (f32[8,2,2]{2,1,0:T(2,128)S(1)}, f32[8,2,2,256]{3,2,1,0:T(2,128)S(1)}) fusion(bf16[8,2,256]{2,1,0:T(2,128)(2,1)} %param.16, pred[8,256]{1,0:T(8,128)(4,1)S(1)} %iota_compare_fusion.2, bf16[8,256,256]{2,1,0:T(8,128)(2,1)} %param.19), kind=kOutput, calls=%fused_computation.81 | convolution fusion | flops 2121696 | bytes 1091712 | tf_op jit(solution)/shard_map/dfhe,dche->dhfc/dot_general | solution.py:53
  13.4 0.9 %fusion.47 = (f32[8,2,2]{2,1,0:T(2,128)S(1)}, f32[8,2,2,2]{2,3,1,0:T(2,128)S(1)}) fusion(bf16[8,2,256]{2,1,0:T(2,128)(2,1)} %param.17, bf16[8,2,256]{2,1,0:T(2,128)(2,1)} %param.16, pred[2,2]{0,1:T(4,128)(4,1)S(1)} %iota_compare_fusion.4), kind=kOutput, calls=%fused_computation.82 | convolution fusion | flops 16544 | bytes 16772 | tf_op jit(solution)/shard_map/dfhe,dghe->dhfg/dot_general | solution.py:58
  14.3 0.2 fusion.25
  14.5 0.0 copy-start.2
  14.6 0.0 copy-start.4
  14.6 1.5 %fusion.9 = f32[8,2,2,128]{3,2,1,0:T(2,128)S(1)} fusion(f32[8,2,2,256]{3,2,1,0:T(2,128)S(1)} %get-tuple-element.8, f32[8,2,2]{2,1,0:T(2,128)S(1)} %add.79, f32[8,2,2]{2,1,0:T(2,128)S(1)} %max.8, bf16[8,256,256]{2,1,0:T(8,128)(2,1)} %param.20), kind=kOutput, calls=%fused_computation.19 | convolution fusion | flops 2121728 | bytes 1097984 | tf_op jit(solution)/shard_map/dhfc,dche->dfhe/dot_general | solution.py:70
  16.1 0.0 copy-done.5
  16.1 0.2 fusion.8
  16.3 0.0 copy-done.1
  16.4 0.4 convolution_convert_fusion
  16.7 0.7 copy.105
  17.4 0.0 copy-done.2
  17.4 0.0 copy-done.4
  17.4 0.1 add.87
  17.5 0.1 all-to-all-done.2
  17.7 8.2 %all-to-all-start = ((bf16[8,16,512]{2,1,0:T(8,128)(2,1)}), bf16[8,16,512]{2,1,0:T(8,128)(2,1)S(1)}, u32[]{:S(2)}, u32[]{:S(2)}) async-start(bf16[8,16,512]{2,1,0:T(8,128)(2,1)} %bitcast.94), calls=%async_computation | async-start | bytes 262144 | tf_op jit(solution)/shard_map/all_to_all | solution.py:108
  25.9 0.1 sub.35
  26.0 7.6 %all-to-all-done = bf16[8,16,512]{2,1,0:T(8,128)(2,1)S(1)} async-done(((bf16[8,16,512]{2,1,0:T(8,128)(2,1)}), bf16[8,16,512]{2,1,0:T(8,128)(2,1)S(1)}, u32[]{:S(2)}, u32[]{:S(2)}) %all-to-all-start) | async-done | bytes 131104 | tf_op jit(solution)/shard_map/all_to_all | solution.py:108
  33.7 0.6 multiply_reduce_fusion.1
  34.3 0.1 broadcast_in_dim.73
  34.4 1.5 %fusion.26 = f32[16,1024]{1,0:T(8,128)S(1)} fusion(bf16[512,1024]{1,0:T(8,128)(2,1)} %param.24, f32[16,512]{1,0:T(8,128)S(1)} %reshape.215, f32[16,512]{1,0:T(8,128)S(1)} %convert_reduce_fusion.1, f32[512]{0:T(512)S(1)} %convert_element_type.77), kind=kOutput, calls=%fused_computation.49 | convolution fusion | flops 16801792 | bytes 1181696 | tf_op jit(solution)/shard_map/dot_general | solution.py:114
  35.9 0.1 broadcast_in_dim.74
  35.9 0.7 reshape.216
  36.6 3.4 %all-to-all-start.1 = ((f32[8,2,1152]{2,1,0:T(2,128)}), f32[8,2,1152]{2,1,0:T(2,128)S(1)}, u32[]{:S(2)}, u32[]{:S(2)}) async-start(f32[8,2,1152]{2,1,0:T(2,128)} %reshape.216), calls=%async_computation.1 | async-start | bytes 147456 | tf_op jit(solution)/shard_map/all_to_all | solution.py:117
  40.0 0.0 copy-start.3
  40.0 3.0 %convolution_convert_fusion.2 = bf16[512,1024]{1,0:T(8,128)(2,1)} fusion(bf16[512,1024]{1,0:T(8,128)(2,1)} %bitcast.98, s32[512]{0:T(512)S(1)} %add_select_fusion), kind=kOutput, calls=%fused_computation.3 | convolution fusion | flops 537657344 | bytes 2099200 | tf_op jit(solution)/shard_map/dot_general | solution.py:95
  43.0 4.2 %all-to-all-done.1 = f32[8,2,1152]{2,1,0:T(2,128)S(1)} async-done(((f32[8,2,1152]{2,1,0:T(2,128)}), f32[8,2,1152]{2,1,0:T(2,128)S(1)}, u32[]{:S(2)}, u32[]{:S(2)}) %all-to-all-start.1) | async-done | bytes 73760 | tf_op jit(solution)/shard_map/all_to_all | solution.py:117
  47.2 10.4 %all-to-all-start.3 = ((bf16[32,16,1024]{2,1,0:T(8,128)(2,1)}), bf16[32,16,1024]{2,1,0:T(8,128)(2,1)}, u32[]{:S(2)}, u32[]{:S(2)}) async-start(bf16[32,16,1024]{2,1,0:T(8,128)(2,1)} %bitcast.95), calls=%async_computation.3 | async-start | bytes 2097152 | tf_op jit(solution)/shard_map/all_to_all | solution.py:100
  57.6 0.0 copy-done.3
  57.7 0.1 fusion.41
  57.8 0.1 slice_multiply_fusion
  57.9 16.7 %all-to-all-done.3 = bf16[32,16,1024]{2,1,0:T(8,128)(2,1)} async-done(((bf16[32,16,1024]{2,1,0:T(8,128)(2,1)}), bf16[32,16,1024]{2,1,0:T(8,128)(2,1)}, u32[]{:S(2)}, u32[]{:S(2)}) %all-to-all-start.3) | async-done | bytes 1048608 | tf_op jit(solution)/shard_map/all_to_all | solution.py:100
  74.6 1.4 %convert_reduce_fusion = f32[16,1024]{1,0:T(8,128)S(1)} fusion(bf16[32,16,1024]{2,1,0:T(8,128)(2,1)} %all-to-all-done.3), kind=kLoop, calls=%fused_computation.2 | loop fusion | flops 1032192 | bytes 1114112 | tf_op jit(solution)/shard_map/reduce_sum | solution.py:103
  76.0 0.1 multiply_reduce_fusion
  76.1 0.1 rsqrt.16
  76.1 0.0 copy-done
  76.1 0.6 convolution_convert_fusion.1
  76.7 0.1 reshape.220
  76.9 0.1 fusion.1
  77.0 0.2 fusion.3
  77.3 0.1 dot_general.45
  77.4 2.1 %fusion.4 = bf16[1,2,8,1024]{3,2,1,0:T(8,128)(2,1)} fusion(bf16[2,8,512]{2,1,0:T(8,128)(2,1)S(1)} %dot_general.45, bf16[512,1024]{1,0:T(8,128)(2,1)} %param.29, f32[16,1024]{1,0:T(8,128)S(1)} %convert_reduce_fusion, f32[2,1024]{1,0:T(2,128)S(1)} %slice_multiply_fusion), kind=kOutput, calls=%fused_computation.11 | convolution fusion | flops 16826368 | bytes 1171456 | tf_op jit(solution)/shard_map/dot_general | solution.py:146
  (20 shorter events, 0.3 us)
Async XLA Ops:
  0.6 75.5 %copy-start = (bf16[1024,1536]{1,0:T(8,128)(2,1)S(1)}, bf16[1024,1536]{1,0:T(8,128)(2,1)}, u32[]{:S(2)}) copy-start(bf16[1024,1536]{1,0:T(8,128)(2,1)} %param.28) | copy-start | bytes 9437188
  0.6 15.5 %copy-start.5 = (bf16[8,2,256]{2,1,0:T(2,128)(2,1)S(1)}, bf16[8,2,256]{2,1,0:T(2,128)(2,1)}, u32[]{:S(2)}) copy-start(bf16[8,2,256]{2,1,0:T(2,128)(2,1)} %param.18) | copy-start | bytes 24580
  2.2 15.5 %all-to-all-start.2 = ((s32[32,1,16]{2,1,0:T(1,128)}), s32[32,1,16]{2,1,0:T(1,128)S(1)}, u32[]{:S(2)}, u32[]{:S(2)}) async-start(s32[32,1,16]{2,1,0:T(1,128)} %broadcast_in_dim.76), calls=%async_computation.2 | async-start | bytes 32768 | tf_op jit(solution)/shard_map/all_to_all | solution.py:84
  10.8 5.6 %copy-start.1 = (bf16[256,4096]{1,0:T(8,128)(2,1)S(1)}, bf16[256,4096]{1,0:T(8,128)(2,1)}, u32[]{:S(2)}) copy-start(bf16[256,4096]{1,0:T(8,128)(2,1)} %param.22) | copy-start | bytes 6291460
  14.5 2.9 %copy-start.2 = (bf16[8,2,512]{2,1,0:T(2,128)(2,1)S(1)}, bf16[8,2,512]{2,1,0:T(2,128)(2,1)}, u32[]{:S(2)}) copy-start(bf16[8,2,512]{2,1,0:T(2,128)(2,1)} %param.15) | copy-start | bytes 49156
  14.6 2.9 %copy-start.4 = (bf16[512]{0:T(512)(128)(2,1)S(1)}, bf16[512]{0:T(512)(128)(2,1)}, u32[]{:S(2)}) copy-start(bf16[512]{0:T(512)(128)(2,1)} %param.23) | copy-start | bytes 3076
  17.7 16.0 %all-to-all-start = ((bf16[8,16,512]{2,1,0:T(8,128)(2,1)}), bf16[8,16,512]{2,1,0:T(8,128)(2,1)S(1)}, u32[]{:S(2)}, u32[]{:S(2)}) async-start(bf16[8,16,512]{2,1,0:T(8,128)(2,1)} %bitcast.94), calls=%async_computation | async-start | bytes 262144 | tf_op jit(solution)/shard_map/all_to_all | solution.py:108
  36.6 10.6 %all-to-all-start.1 = ((f32[8,2,1152]{2,1,0:T(2,128)}), f32[8,2,1152]{2,1,0:T(2,128)S(1)}, u32[]{:S(2)}, u32[]{:S(2)}) async-start(f32[8,2,1152]{2,1,0:T(2,128)} %reshape.216), calls=%async_computation.1 | async-start | bytes 147456 | tf_op jit(solution)/shard_map/all_to_all | solution.py:117
  40.0 17.6 %copy-start.3 = (bf16[1024]{0:T(1024)(128)(2,1)S(1)}, bf16[1024]{0:T(1024)(128)(2,1)}, u32[]{:S(2)}) copy-start(bf16[1024]{0:T(1024)(128)(2,1)} %param.27) | copy-start | bytes 6148
  47.2 27.3 %all-to-all-start.3 = ((bf16[32,16,1024]{2,1,0:T(8,128)(2,1)}), bf16[32,16,1024]{2,1,0:T(8,128)(2,1)}, u32[]{:S(2)}, u32[]{:S(2)}) async-start(bf16[32,16,1024]{2,1,0:T(8,128)(2,1)} %bitcast.95), calls=%async_computation.3 | async-start | bytes 2097152 | tf_op jit(solution)/shard_map/all_to_all | solution.py:100

commit v2 on v0

v2 whole, which is shorter than its diff:
```python
import functools
import math

import jax
import jax.numpy as jnp
from jax import lax
from jax.experimental import pallas as pl
from jax.experimental.pallas import tpu as pltpu
from jax.sharding import PartitionSpec as P

D = 4096
HD = 128
DD = 1024
DHD = 64
DHEADS = 8
LEVELS = 8
FRAMES = 2
CORES = 2
SIDE = 4
EXTRA = 128
MIB = 2**20
NT = (((1,), (1,)), ((), ()))


def dot_nt(a, b):
    return lax.dot_general(a, b, NT, preferred_element_type=jnp.float32)


def dot_nn(a, b):
    return jnp.dot(a, b, preferred_element_type=jnp.float32)


def iota(shape, axis):
    return lax.broadcasted_iota(jnp.int32, shape, axis)


def attend_kernel(
    lengths_ref, q_ref, nk_ref, nv_ref, k_hbm, v_hbm, w_hbm, out_ref, k_buf, v_buf, w_buf, small, sems
):
    dialogues = q_ref.shape[0]
    width = q_ref.shape[2]
    rows = dialogues * FRAMES
    heads = width // HD
    stacked = heads * rows
    half = dialogues // 2
    slots = k_buf.shape[1]
    copies = []
    for i in range(2):
        part = pl.ds(i * half, half)
        copies.append(pltpu.make_async_copy(k_hbm.at[part], k_buf.at[part], sems.at[i]))
    for i in range(2):
        part = pl.ds(i * half, half)
        copies.append(pltpu.make_async_copy(v_hbm.at[part], v_buf.at[part], sems.at[2 + i]))
    copies.append(pltpu.make_async_copy(w_hbm, w_buf, sems.at[4]))
    for copy in copies:
        copy.start()
    for i, ref in enumerate((q_ref, nk_ref, nv_ref)):
        for d in range(dialogues):
            small[i, FRAMES * d : FRAMES * (d + 1), :] = ref[d].astype(jnp.float32)
    query = small[0]
    fresh_key = small[1].astype(jnp.bfloat16)
    fresh_value = small[2].astype(jnp.bfloat16)
    head_of = iota((rows, width), 1) // HD
    spread = jnp.concatenate(
        [jnp.where(head_of == h, query, 0.0) for h in range(heads)], axis=0
    ).astype(jnp.bfloat16)
    scale = 1.0 / math.sqrt(HD)

    row = iota((stacked, slots), 0)
    slot = iota((stacked, slots), 1)
    dialogue = (row % rows) // FRAMES
    scores = jnp.zeros((stacked, slots), jnp.float32)
    live = jnp.zeros((stacked, slots), jnp.int32)
    for d in range(dialogues):
        if d % half == 0:
            copies[d // half].wait()
        scores = jnp.where(dialogue == d, dot_nt(spread, k_buf[d]), scores)
        live = jnp.where(dialogue == d, lengths_ref[d], live)
    scores = jnp.where(slot < live, scores * scale, -jnp.inf)

    row_n = iota((stacked, rows), 0) % rows
    col_n = iota((stacked, rows), 1)
    seen = (row_n // FRAMES == col_n // FRAMES) & (col_n <= row_n)
    fresh = jnp.where(seen, dot_nt(spread, fresh_key) * scale, -jnp.inf)
    largest = jnp.maximum(
        jnp.max(scores, axis=-1, keepdims=True), jnp.max(fresh, axis=-1, keepdims=True)
    )
    exp_cache = jnp.exp(scores - largest)
    exp_fresh = jnp.exp(fresh - largest)
    total = jnp.sum(exp_cache, axis=-1, keepdims=True) + jnp.sum(
        exp_fresh, axis=-1, keepdims=True
    )
    prob_cache = exp_cache / total
    prob_fresh = (exp_fresh / total).astype(jnp.bfloat16)
    mixed = dot_nn(prob_fresh, fresh_value)
    for d in range(dialogues):
        if d % half == 0:
            copies[2 + d // half].wait()
        own = jnp.where(dialogue == d, prob_cache, 0.0).astype(jnp.bfloat16)
        mixed = mixed + dot_nn(own, v_buf[d])
    attended = mixed[:rows]
    for h in range(1, heads):
        attended = jnp.where(head_of == h, mixed[h * rows : (h + 1) * rows], attended)
    attended = attended.astype(jnp.bfloat16)
    copies[4].wait()
    peers, _, features = out_ref.shape
    for t in range(peers):
        out_ref[t] = dot_nn(attended, w_buf[:, t * features : (t + 1) * features]).astype(
            jnp.bfloat16
        )


def lookup_kernel(ids_ref, own_hbm, other_ref, *refs):
    out_refs, (done_ref, own_buf, found_buf, sem) = refs[:SIDE], refs[SIDE:]
    first = pltpu.make_async_copy(own_hbm, own_buf, sem)
    first.start()
    members = ids_ref.shape[0]
    span = own_buf.shape[1]
    width = own_buf.shape[2]
    entries = LEVELS * span
    count = FRAMES * LEVELS
    rows = members * count
    me = lax.axis_index("batch")

    pick = (iota((rows, members), 0) // count == iota((rows, members), 1)).astype(jnp.bfloat16)
    row = iota((rows, LEVELS), 0)
    lane = iota((rows, LEVELS), 1)
    block = jnp.zeros((rows, LEVELS), jnp.float32)
    inner = jnp.zeros((rows, LEVELS), jnp.float32)
    for f in range(FRAMES):
        ids = ids_ref[:, f, :]
        mine = (lane == row % LEVELS) & ((row // LEVELS) % FRAMES == f)
        high = (ids // span).astype(jnp.float32).astype(jnp.bfloat16)
        low = (ids % span).astype(jnp.float32).astype(jnp.bfloat16)
        block = jnp.where(mine, dot_nn(pick, high), block)
        inner = jnp.where(mine, dot_nn(pick, low), inner)
    block = jnp.sum(block, axis=1, keepdims=True).astype(jnp.int32)
    inner = jnp.sum(inner, axis=1, keepdims=True).astype(jnp.int32)
    level = iota((rows, 1), 0) % LEVELS
    place = inner + level * span
    at_own = jnp.where(block == me, place, -1)
    at_other = jnp.where(block == (me ^ 1), place, -1)
    entry = iota((rows, entries), 1)
    hot_own = jnp.where(entry == at_own, 1.0, 0.0).astype(jnp.bfloat16)
    hot_other = jnp.where(entry == at_other, 1.0, 0.0).astype(jnp.bfloat16)
    first.wait()
    found = dot_nn(hot_own, own_buf[...].reshape(entries, width))
    found = found + dot_nn(hot_other, other_ref[...].reshape(entries, width))
    found_buf[...] = found.astype(jnp.bfloat16).reshape(found_buf.shape)
    mine = me // (SIDE * CORES)
    for s in range(SIDE):
        out_refs[s][...] = found_buf[pl.ds((mine + s) % SIDE * SIDE, SIDE)]
    done_ref[...] = jnp.zeros_like(done_ref)


def collect_kernel(own_ref, *refs):
    arrived, out_refs = refs[: SIDE - 1], refs[SIDE - 1 :]
    mine = lax.axis_index("batch") // CORES % SIDE
    for s in range(SIDE):
        place = (mine + s) % SIDE
        value = own_ref[place]
        for ref in arrived:
            value = value + ref[place]
        out_refs[s][...] = value


def middle_kernel(
    shares_ref, residual_ref, gain_ref, w_hbm, order_hbm, stream_ref, sent_ref, w_buf, rows_buf, sent_buf, sem
):
    copy = pltpu.make_async_copy(w_hbm, w_buf, sem)
    copy.start()
    dialogues = residual_ref.shape[0]
    for d in range(dialogues):
        rows_buf[FRAMES * d : FRAMES * (d + 1), :] = residual_ref[d].astype(jnp.float32)
    hidden = rows_buf[...]
    share = shares_ref[0].astype(jnp.float32)
    for t in range(1, shares_ref.shape[0]):
        share = share + shares_ref[t].astype(jnp.float32)
    hidden = hidden + share
    rows_buf[...] = hidden
    squares = jnp.sum(hidden * hidden, axis=-1, keepdims=True)
    scaled = (hidden * gain_ref[...]).astype(jnp.bfloat16)
    width = w_buf.shape[1]
    sent_buf[:, width:] = jnp.broadcast_to(squares, (hidden.shape[0], EXTRA))
    for d in range(dialogues):
        stream_ref[d] = rows_buf[FRAMES * d : FRAMES * (d + 1), :].astype(jnp.bfloat16)
    copy.wait()
    sent_buf[:, :width] = dot_nn(scaled, w_buf[...])
    for d in range(dialogues):
        sent_ref[d] = sent_buf[FRAMES * d : FRAMES * (d + 1), :]


def depth_kernel(
    terms_ref, *refs
):
    table_refs = refs[:SIDE]
    gain_ref, qkv_hbm, o_hbm, out_ref, qkv_buf, o_buf, sems = refs[SIDE:]
    first = pltpu.make_async_copy(qkv_hbm, qkv_buf, sems.at[0])
    second = pltpu.make_async_copy(o_hbm, o_buf, sems.at[1])
    first.start()
    second.start()
    count, width = table_refs[0].shape
    terms = terms_ref[0]
    for t in range(1, terms_ref.shape[0]):
        terms = terms + terms_ref[t]
    inverse = lax.rsqrt(terms[:, width : width + 1] / D + 1e-05)
    proj = terms[:, :width] * inverse
    values = table_refs[0][...].astype(jnp.float32)
    for ref in table_refs[1:]:
        values = values + ref[...].astype(jnp.float32)
    frame = iota((count, width), 0) // LEVELS
    depth_input = values + jnp.where(frame == 0, proj[0:1], proj[1:2])
    mean = jnp.sum(depth_input * depth_input, axis=-1, keepdims=True) / width
    normed = (depth_input * lax.rsqrt(mean + 1e-05) * gain_ref[...]).astype(jnp.bfloat16)
    first.wait()
    heads_width = DHEADS * DHD
    query = dot_nn(normed, qkv_buf[:, :heads_width]).astype(jnp.bfloat16).astype(jnp.float32)
    key = dot_nn(normed, qkv_buf[:, heads_width : 2 * heads_width]).astype(jnp.bfloat16)
    value = dot_nn(normed, qkv_buf[:, 2 * heads_width :]).astype(jnp.bfloat16)
    head_of = iota((count, heads_width), 1) // DHD
    spread = jnp.concatenate(
        [jnp.where(head_of == h, query, 0.0) for h in range(DHEADS)], axis=0
    ).astype(jnp.bfloat16)
    scores = dot_nt(spread, key) * (1.0 / math.sqrt(DHD))
    row = iota(scores.shape, 0) % count
    col = iota(scores.shape, 1)
    seen = (row // LEVELS == col // LEVELS) & (col <= row)
    exps = jnp.where(seen, jnp.exp(scores), 0.0)
    probs = (exps / jnp.sum(exps, axis=-1, keepdims=True)).astype(jnp.bfloat16)
    spread_out = dot_nn(probs, value)
    mixed = spread_out[:count]
    for h in range(1, DHEADS):
        mixed = jnp.where(head_of == h, spread_out[h * count : (h + 1) * count], mixed)
    second.wait()
    out_ref[...] = (depth_input + dot_nn(mixed.astype(jnp.bfloat16), o_buf[...])).astype(
        jnp.bfloat16
    )


VMEM = pl.BlockSpec(memory_space=pltpu.VMEM)
SMEM = pl.BlockSpec(memory_space=pltpu.SMEM)
ANY = pl.BlockSpec(memory_space=pl.ANY)


def hbm(*arrays):
    return tuple(pltpu.with_memory_space_constraint(a, pltpu.HBM) for a in arrays)


def call(kernel, name, outs, ins, out_specs, scratch, limit, flops, moved):
    return pl.pallas_call(
        kernel,
        name=name,
        out_shape=outs,
        in_specs=ins,
        out_specs=out_specs,
        scratch_shapes=scratch,
        compiler_params=pltpu.CompilerParams(vmem_limit_bytes=limit * MIB),
        cost_estimate=pl.CostEstimate(flops=flops, bytes_accessed=moved, transcendentals=0),
    )


def shifted(size, step, s):
    span = SIDE * step
    return [(b, b // span * span + (b + s * step) % span) for b in range(size)]


def per_device(
    residual,
    new_queries,
    new_keys,
    new_values,
    cache_keys,
    cache_values,
    lengths,
    out_weight,
    temporal_gain,
    in_weight,
    tokens,
    level_tables,
    depth_gain,
    depth_qkv,
    depth_out,
):
    shape = jax.ShapeDtypeStruct
    bf16, f32 = jnp.bfloat16, jnp.float32
    held, _, features = residual.shape
    tensor_size = lax.axis_size("tensor")
    batch_size = lax.axis_size("batch")
    rows = held * FRAMES
    width = in_weight.shape[1]
    members = batch_size // CORES
    groups = [[b for b in range(batch_size) if b % CORES == c] for c in range(CORES)]
    count = FRAMES * LEVELS

    other_tables = lax.ppermute(level_tables, "batch", [(b, b ^ 1) for b in range(batch_size)])
    sent_ids = jnp.broadcast_to(tokens, (members, FRAMES, LEVELS))
    ids = lax.all_to_all(sent_ids, "batch", 0, 0, axis_index_groups=groups, tiled=True)

    head_terms = call(
        attend_kernel,
        "attend",
        pltpu.HBM((tensor_size, rows, features), bf16),
        [SMEM, VMEM, VMEM, VMEM, ANY, ANY, ANY],
        VMEM,
        [
            pltpu.VMEM(cache_keys.shape, bf16),
            pltpu.VMEM(cache_values.shape, bf16),
            pltpu.VMEM(out_weight.shape, bf16),
            pltpu.VMEM((3, rows, new_queries.shape[2]), f32),
            pltpu.SemaphoreType.DMA((5,)),
        ],
        24,
        10**8,
        4 * 2**20,
    )(*hbm(lengths, new_queries, new_keys, new_values, cache_keys, cache_values, out_weight))
    shares = lax.all_to_all(head_terms, "tensor", 0, 0, tiled=True)

    *partial_rows, order = call(
        lookup_kernel,
        "lookup",
        (*[shape((SIDE, count, width), bf16)] * SIDE, shape((8, 128), f32)),
        [VMEM, ANY, VMEM],
        (*[VMEM] * SIDE, VMEM),
        [
            pltpu.VMEM(level_tables.shape, bf16),
            pltpu.VMEM((members, count, width), bf16),
            pltpu.SemaphoreType.DMA,
        ],
        24,
        6 * 10**8,
        1,
    )(ids, *hbm(level_tables), other_tables)
    across = [
        lax.ppermute(partial_rows[s], "batch", shifted(batch_size, SIDE * CORES, s))
        for s in (2, 1, 3)
    ]
    own_rows, *side_rows = call(
        collect_kernel,
        "collect",
        [shape((count, width), bf16)] * SIDE,
        [VMEM] * SIDE,
        [VMEM] * SIDE,
        [],
        24,
        10**6,
        1,
    )(partial_rows[0], *across)
    along = [
        lax.ppermute(side_rows[s - 1], "batch", shifted(batch_size, CORES, s)) for s in (2, 1, 3)
    ]

    temporal_out, sent = call(
        middle_kernel,
        "middle",
        (pltpu.HBM(residual.shape, bf16), pltpu.HBM((held, FRAMES, width + EXTRA), f32)),
        [VMEM, VMEM, VMEM, ANY, ANY],
        (VMEM, VMEM),
        [
            pltpu.VMEM(in_weight.shape, bf16),
            pltpu.VMEM((rows, features), f32),
            pltpu.VMEM((rows, width + EXTRA), f32),
            pltpu.SemaphoreType.DMA,
        ],
        24,
        10**9,
        1,
    )(shares, residual, temporal_gain.astype(f32).reshape(1, features), *hbm(in_weight), order)
    terms = lax.all_to_all(sent, "tensor", 0, 0, tiled=True)

    states = call(
        depth_kernel,
        "depth",
        pltpu.HBM((count, width), bf16),
        [VMEM] * (SIDE + 2) + [ANY, ANY],
        VMEM,
        [
            pltpu.VMEM(depth_qkv.shape, bf16),
            pltpu.VMEM(depth_out.shape, bf16),
            pltpu.SemaphoreType.DMA((2,)),
        ],
        24,
        10**9,
        1,
    )(terms, own_rows, *along, depth_gain.astype(f32).reshape(1, width), *hbm(depth_qkv, depth_out))
    return (temporal_out, states.reshape(1, FRAMES, LEVELS, width))


def solution(mesh):
    placed = (
        P("batch", None, "tensor"),
        P("batch", None, "tensor"),
        P("batch", None, "tensor"),
        P("batch", None, "tensor"),
        P("batch", None, "tensor"),
        P("batch", None, "tensor"),
        P("batch"),
        P("tensor", None),
        P("tensor"),
        P("tensor", None),
        P(("batch", "tensor"), None, None),
        P(None, "batch", None),
        P(),
        P(),
        P(),
    )
    return jax.shard_map(
        per_device,
        mesh=mesh,
        in_specs=placed,
        out_specs=(P("batch", None, "tensor"), P(("batch", "tensor"), None, None, None)),
        check_vma=False,
    )
```

time: 155 us -> 52.7 us (0.34)
  the two profiles are of different devices: /device:TPU:4 before, /device:TPU:56 now
where the time goes in v2:
time: 52.7 us; the launch traced here: 52.3 us
  starting transfers between devices  31.1 us (59%)
  Pallas kernels  12.1 us (23%)
  waiting for transfers between devices  7.01 us (13%)
  local copies, waits for them, and re-layouts  1.3 us (2%)
  between operations  0.72 us (1%)
    all_to_all x1, starting transfers between devices, per_device(): shares = lax.all_to_all(head_terms, 'tensor', 0, 0, tiled=True)  8.57 us
    all_to_all x1, starting transfers between devices, per_device(): lax.all_to_all(sent_ids, 'batch', 0, 0, axis_index_groups=groups, tiled=T...  7.17 us
    all_to_all x1, starting transfers between devices, per_device(): terms = lax.all_to_all(sent, 'tensor', 0, 0, tiled=True)  6.6 us
    ppermute x3, starting transfers between devices, per_device(): lax.ppermute(partial_rows[s], 'batch', shifted(batch_size, SIDE * CORES, s))  4.97 us
    pallas_call x1, Pallas kernels, per_device(): call(attend_kernel, 'attend', pltpu.HBM((tensor_size, rows, features), bf...  4.29 us
    ppermute x3, starting transfers between devices, per_device(): lax.ppermute(side_rows[s - 1], 'batch', shifted(batch_size, CORES, s))  3.69 us
    pallas_call x1, Pallas kernels, per_device(): call(depth_kernel, 'depth', pltpu.HBM((count, width), bf16), [VMEM] * (SI...  3.64 us
    all_to_all x1, waiting for transfers between devices, per_device(): terms = lax.all_to_all(sent, 'tensor', 0, 0, tiled=True)  3.22 us
  transfers between devices with their start and end apart: 10, of which 4 were waited for; matrix products, arithmetic and copies ran while one was open for 2% of the time, Pallas kernels for 16%

profile of v2, /device:TPU:56, one launch (start us, length us, event | category | flops | bytes accessed | tf_op | source)
XLA Modules:
  0.0 52.3 jit_solution(44612604167769558)
XLA Ops:
  0.6 0.0 copy-start.2
  0.6 0.1 collective-permute-start
  0.7 1.3 %broadcast_in_dim.8 = s32[16,2,8]{2,1,0:T(2,128)} broadcast(s32[2,8]{1,0:T(2,128)} %bitcast.7), dimensions={1,2} | broadcast | bytes 1088 | tf_op jit(solution)/shard_map/broadcast_in_dim | solution.py:296
  2.0 7.2 %all-to-all-start.1 = ((s32[16,2,8]{2,1,0:T(2,128)}), s32[16,2,8]{2,1,0:T(2,128)S(1)}, u32[]{:S(2)}, u32[]{:S(2)}) async-start(s32[16,2,8]{2,1,0:T(2,128)} %broadcast_in_dim.8), calls=%async_computation.1 | async-start | bytes 32768 | tf_op jit(solution)/shard_map/all_to_all | solution.py:297
  9.2 0.0 copy-start
  9.2 4.3 %attend.1 = bf16[8,16,512]{2,1,0:T(8,128)(2,1)} custom-call(s32[8]{0:T(128)} %lengths_ref.1, bf16[8,2,256]{2,1,0:T(2,128)(2,1)} %q_ref.1, bf16[8,2,256]{2,1,0:T(2,128)(2,1)} %nk_ref.1, bf16[8,2,256]{2,1,0:T(2,128)(2,1)} %nv_ref.1, bf16[8,256,256]{2,1,0:T(8,128)(2,1)} %k_hbm.1, bf16[8,256,256]{2,1,0:T(8,128)(2,1)} %v_hbm.1, bf16[256,4096]{1,0:T(8,128)(2,1)} %w_hbm.2), custom_call_target="tpu_custom_call" | custom-call | flops 100000000 | bytes 4194304 | tf_op jit(solution)/shard_map/attend/pallas_call | solution.py:299
  13.5 1.3 %all-to-all-done.1.ids_ref = s32[16,2,8]{2,1,0:T(2,128)S(1)} async-done(((s32[16,2,8]{2,1,0:T(2,128)}), s32[16,2,8]{2,1,0:T(2,128)S(1)}, u32[]{:S(2)}, u32[]{:S(2)}) %all-to-all-start.1) | async-done | bytes 1056 | tf_op jit(solution)/shard_map/all_to_all | solution.py:297
  14.8 8.6 %all-to-all-start = ((bf16[8,16,512]{2,1,0:T(8,128)(2,1)}), bf16[8,16,512]{2,1,0:T(8,128)(2,1)S(1)}, u32[]{:S(2)}, u32[]{:S(2)}) async-start(bf16[8,16,512]{2,1,0:T(8,128)(2,1)} %attend.1), calls=%async_computation | async-start | bytes 262144 | tf_op jit(solution)/shard_map/all_to_all | solution.py:316
  23.4 0.0 copy-done.2
  23.4 0.0 copy-start.1
  23.4 0.0 collective-permute-done.other_ref
  23.4 2.0 %lookup.1 = (bf16[4,16,1024]{2,1,0:T(8,128)(2,1)S(1)}, bf16[4,16,1024]{2,1,0:T(8,128)(2,1)S(1)}, bf16[4,16,1024]{2,1,0:T(8,128)(2,1)S(1)}, bf16[4,16,1024]{2,1,0:T(8,128)(2,1)S(1)}, f32[8,128]{1,0:T(8,128)S(1)}) custom-call(s32[16,2,8]{2,1,0:T(2,128)S(1)} %all-to-all-done.1.ids_ref, bf16[8,64,1024]{2,1,0:T(8,128)(2,1)} %own_hbm.1, ...), custom_call_target="tpu_custom_call" | custom-call | flops 600000000 | bytes 1 | tf_op jit(solution)/shard_map/lookup/pallas_call | solution.py:318
  25.4 1.7 %collective-permute-start.1 = (bf16[4,16,1024]{2,1,0:T(8,128)(2,1)S(1)}, bf16[4,16,1024]{2,1,0:T(8,128)(2,1)S(1)}, u32[]{:S(2)}, u32[]{:S(2)}) collective-permute-start(bf16[4,16,1024]{2,1,0:T(8,128)(2,1)S(1)} %get-tuple-element.17), channel_id=1, source_target_pairs={{0,128},{8,136},{16,144},{24,152},{32,160},{40,168},{48,176},{56,1... | collective-permute-start | bytes 393224 | tf_op jit(solution)/shard_map/ppermute | solution.py:334
  27.2 0.6 %collective-permute-start.2 = (bf16[4,16,1024]{2,1,0:T(8,128)(2,1)S(1)}, bf16[4,16,1024]{2,1,0:T(8,128)(2,1)S(1)}, u32[]{:S(2)}, u32[]{:S(2)}) collective-permute-start(bf16[4,16,1024]{2,1,0:T(8,128)(2,1)S(1)} %get-tuple-element.18), channel_id=1, source_target_pairs={{0,64},{8,72},{16,80},{24,88},{32,96},{40,104},{48,112},{56,120},{... | collective-permute-start | bytes 393224 | tf_op jit(solution)/shard_map/ppermute | solution.py:334
  27.7 2.7 %collective-permute-start.3 = (bf16[4,16,1024]{2,1,0:T(8,128)(2,1)S(1)}, bf16[4,16,1024]{2,1,0:T(8,128)(2,1)S(1)}, u32[]{:S(2)}, u32[]{:S(2)}) collective-permute-start(bf16[4,16,1024]{2,1,0:T(8,128)(2,1)S(1)} %get-tuple-element.19), channel_id=1, source_target_pairs={{0,192},{8,200},{16,208},{24,216},{32,224},{40,232},{48,240},{56,2... | collective-permute-start | bytes 393224 | tf_op jit(solution)/shard_map/ppermute | solution.py:334
  30.4 0.6 %all-to-all-done.shares_ref = bf16[8,16,512]{2,1,0:T(8,128)(2,1)S(1)} async-done(((bf16[8,16,512]{2,1,0:T(8,128)(2,1)}), bf16[8,16,512]{2,1,0:T(8,128)(2,1)S(1)}, u32[]{:S(2)}, u32[]{:S(2)}) %all-to-all-start) | async-done | bytes 131104 | tf_op jit(solution)/shard_map/all_to_all | solution.py:316
  31.0 0.0 copy-done
  31.0 2.2 %middle.1 = (bf16[8,2,512]{2,1,0:T(2,128)(2,1)}, f32[8,2,1152]{2,1,0:T(2,128)}) custom-call(bf16[8,16,512]{2,1,0:T(8,128)(2,1)S(1)} %all-to-all-done.shares_ref, bf16[8,2,512]{2,1,0:T(2,128)(2,1)S(1)} %copy-done, f32[1,512]{1,0:T(1,128)S(1)} %bitcast.5, bf16[512,1024]{1,0:T(8,128)(2,1)} %w_hbm.3, f32[8,128]{1,0:T(8,128)S(1)} %get-tuple-element.13.order_hbm), custom_call_target="tpu_custom_call" | custom-call | flops 1000000000 | bytes 1 | tf_op jit(solution)/shard_map/middle/pallas_call | solution.py:352
  33.2 6.6 %all-to-all-start.2 = ((f32[8,2,1152]{2,1,0:T(2,128)}), f32[8,2,1152]{2,1,0:T(2,128)S(1)}, u32[]{:S(2)}, u32[]{:S(2)}) async-start(f32[8,2,1152]{2,1,0:T(2,128)} %get-tuple-element.15), calls=%async_computation.2 | async-start | bytes 147456 | tf_op jit(solution)/shard_map/all_to_all | solution.py:368
  39.8 0.0 collective-permute-done.1.refs_0_
  39.8 0.0 collective-permute-done.2.refs_1_
  39.8 0.0 collective-permute-done.3.refs_2_
  39.8 0.1 collect.1
  39.9 1.7 %collective-permute-start.4 = (bf16[16,1024]{1,0:T(8,128)(2,1)S(1)}, bf16[16,1024]{1,0:T(8,128)(2,1)S(1)}, u32[]{:S(2)}, u32[]{:S(2)}) collective-permute-start(bf16[16,1024]{1,0:T(8,128)(2,1)S(1)} %get-tuple-element.21), channel_id=1, source_target_pairs={{0,32},{8,40},{16,48},{24,56},{32,0},{40,8},{48,16},{56,24},{64,96... | collective-permute-start | bytes 98312 | tf_op jit(solution)/shard_map/ppermute | solution.py:349
  41.6 1.9 %collective-permute-start.5 = (bf16[16,1024]{1,0:T(8,128)(2,1)S(1)}, bf16[16,1024]{1,0:T(8,128)(2,1)S(1)}, u32[]{:S(2)}, u32[]{:S(2)}) collective-permute-start(bf16[16,1024]{1,0:T(8,128)(2,1)S(1)} %get-tuple-element.22), channel_id=1, source_target_pairs={{0,16},{8,24},{16,32},{24,40},{32,48},{40,56},{48,0},{56,8},{64,80... | collective-permute-start | bytes 98312 | tf_op jit(solution)/shard_map/ppermute | solution.py:349
  43.5 0.1 collective-permute-start.6
  43.6 0.0 copy-done.1
  43.6 3.2 %all-to-all-done.2.terms_ref = f32[8,2,1152]{2,1,0:T(2,128)S(1)} async-done(((f32[8,2,1152]{2,1,0:T(2,128)}), f32[8,2,1152]{2,1,0:T(2,128)S(1)}, u32[]{:S(2)}, u32[]{:S(2)}) %all-to-all-start.2) | async-done | bytes 73760 | tf_op jit(solution)/shard_map/all_to_all | solution.py:368
  46.8 0.0 collective-permute-done.4.refs_1_
  46.8 0.0 collective-permute-done.5.refs_2_
  46.8 1.8 %collective-permute-done.6.refs_3_ = bf16[16,1024]{1,0:T(8,128)(2,1)S(1)} collective-permute-done((bf16[16,1024]{1,0:T(8,128)(2,1)S(1)}, bf16[16,1024]{1,0:T(8,128)(2,1)S(1)}, u32[]{:S(2)}, u32[]{:S(2)}) %collective-permute-start.6) | collective-permute-done | bytes 32800 | tf_op jit(solution)/shard_map/ppermute | solution.py:349
  48.6 3.6 %depth.1 = bf16[16,1024]{1,0:T(8,128)(2,1)} custom-call(f32[8,2,1152]{2,1,0:T(2,128)S(1)} %all-to-all-done.2.terms_ref, bf16[16,1024]{1,0:T(8,128)(2,1)S(1)} %get-tuple-element.20.refs_0_, bf16[16,1024]{1,0:T(8,128)(2,1)S(1)} %collective-permute-done.4.refs_1_, bf16[16,1024]{1,0:T(8,128)(2,1)S(1)} %collective-permute-done.5.refs_2_, ...), custom_call_target="tpu_custom_call" | custom-call | flops 1000000000 | bytes 1 | tf_op jit(solution)/shard_map/depth/pallas_call | solution.py:370
  (2 shorter events, 0.0 us)
Async XLA Ops:
  0.6 22.8 %copy-start.2 = (bf16[512]{0:T(512)(128)(2,1)S(1)}, bf16[512]{0:T(512)(128)(2,1)}, u32[]{:S(2)}) copy-start(bf16[512]{0:T(512)(128)(2,1)} %param.23) | copy-start | bytes 3076
  0.6 22.8 %collective-permute-start = (bf16[8,64,1024]{2,1,0:T(8,128)(2,1)}, bf16[8,64,1024]{2,1,0:T(8,128)(2,1)S(1)}, u32[]{:S(2)}, u32[]{:S(2)}) collective-permute-start(bf16[8,64,1024]{2,1,0:T(8,128)(2,1)} %own_hbm.1), channel_id=1, source_target_pairs={{0,8},{8,0},{16,24},{24,16},{32,40},{40,32},{48,56},{56,48},{64,72... | collective-permute-start | bytes 3145736 | tf_op jit(solution)/shard_map/ppermute | solution.py:295
  2.0 12.8 %all-to-all-start.1 = ((s32[16,2,8]{2,1,0:T(2,128)}), s32[16,2,8]{2,1,0:T(2,128)S(1)}, u32[]{:S(2)}, u32[]{:S(2)}) async-start(s32[16,2,8]{2,1,0:T(2,128)} %broadcast_in_dim.8), calls=%async_computation.1 | async-start | bytes 32768 | tf_op jit(solution)/shard_map/all_to_all | solution.py:297
  9.2 21.8 %copy-start = (bf16[8,2,512]{2,1,0:T(2,128)(2,1)S(1)}, bf16[8,2,512]{2,1,0:T(2,128)(2,1)}, u32[]{:S(2)}) copy-start(bf16[8,2,512]{2,1,0:T(2,128)(2,1)} %residual_ref.1) | copy-start | bytes 49156
  14.8 16.2 %all-to-all-start = ((bf16[8,16,512]{2,1,0:T(8,128)(2,1)}), bf16[8,16,512]{2,1,0:T(8,128)(2,1)S(1)}, u32[]{:S(2)}, u32[]{:S(2)}) async-start(bf16[8,16,512]{2,1,0:T(8,128)(2,1)} %attend.1), calls=%async_computation | async-start | bytes 262144 | tf_op jit(solution)/shard_map/all_to_all | solution.py:316
  23.4 20.2 %copy-start.1 = (bf16[1024]{0:T(1024)(128)(2,1)S(1)}, bf16[1024]{0:T(1024)(128)(2,1)}, u32[]{:S(2)}) copy-start(bf16[1024]{0:T(1024)(128)(2,1)} %param.27) | copy-start | bytes 6148
  25.4 14.4 %collective-permute-start.1 = (bf16[4,16,1024]{2,1,0:T(8,128)(2,1)S(1)}, bf16[4,16,1024]{2,1,0:T(8,128)(2,1)S(1)}, u32[]{:S(2)}, u32[]{:S(2)}) collective-permute-start(bf16[4,16,1024]{2,1,0:T(8,128)(2,1)S(1)} %get-tuple-element.17), channel_id=1, source_target_pairs={{0,128},{8,136},{16,144},{24,152},{32,160},{40,168},{48,176},{56,1... | collective-permute-start | bytes 393224 | tf_op jit(solution)/shard_map/ppermute | solution.py:334
  27.2 12.6 %collective-permute-start.2 = (bf16[4,16,1024]{2,1,0:T(8,128)(2,1)S(1)}, bf16[4,16,1024]{2,1,0:T(8,128)(2,1)S(1)}, u32[]{:S(2)}, u32[]{:S(2)}) collective-permute-start(bf16[4,16,1024]{2,1,0:T(8,128)(2,1)S(1)} %get-tuple-element.18), channel_id=1, source_target_pairs={{0,64},{8,72},{16,80},{24,88},{32,96},{40,104},{48,112},{56,120},{... | collective-permute-start | bytes 393224 | tf_op jit(solution)/shard_map/ppermute | solution.py:334
  27.7 12.1 %collective-permute-start.3 = (bf16[4,16,1024]{2,1,0:T(8,128)(2,1)S(1)}, bf16[4,16,1024]{2,1,0:T(8,128)(2,1)S(1)}, u32[]{:S(2)}, u32[]{:S(2)}) collective-permute-start(bf16[4,16,1024]{2,1,0:T(8,128)(2,1)S(1)} %get-tuple-element.19), channel_id=1, source_target_pairs={{0,192},{8,200},{16,208},{24,216},{32,224},{40,232},{48,240},{56,2... | collective-permute-start | bytes 393224 | tf_op jit(solution)/shard_map/ppermute | solution.py:334
  33.2 13.6 %all-to-all-start.2 = ((f32[8,2,1152]{2,1,0:T(2,128)}), f32[8,2,1152]{2,1,0:T(2,128)S(1)}, u32[]{:S(2)}, u32[]{:S(2)}) async-start(f32[8,2,1152]{2,1,0:T(2,128)} %get-tuple-element.15), calls=%async_computation.2 | async-start | bytes 147456 | tf_op jit(solution)/shard_map/all_to_all | solution.py:368
  39.9 6.9 %collective-permute-start.4 = (bf16[16,1024]{1,0:T(8,128)(2,1)S(1)}, bf16[16,1024]{1,0:T(8,128)(2,1)S(1)}, u32[]{:S(2)}, u32[]{:S(2)}) collective-permute-start(bf16[16,1024]{1,0:T(8,128)(2,1)S(1)} %get-tuple-element.21), channel_id=1, source_target_pairs={{0,32},{8,40},{16,48},{24,56},{32,0},{40,8},{48,16},{56,24},{64,96... | collective-permute-start | bytes 98312 | tf_op jit(solution)/shard_map/ppermute | solution.py:349
  41.6 5.3 %collective-permute-start.5 = (bf16[16,1024]{1,0:T(8,128)(2,1)S(1)}, bf16[16,1024]{1,0:T(8,128)(2,1)S(1)}, u32[]{:S(2)}, u32[]{:S(2)}) collective-permute-start(bf16[16,1024]{1,0:T(8,128)(2,1)S(1)} %get-tuple-element.22), channel_id=1, source_target_pairs={{0,16},{8,24},{16,32},{24,40},{32,48},{40,56},{48,0},{56,8},{64,80... | collective-permute-start | bytes 98312 | tf_op jit(solution)/shard_map/ppermute | solution.py:349
  43.5 5.1 %collective-permute-start.6 = (bf16[16,1024]{1,0:T(8,128)(2,1)S(1)}, bf16[16,1024]{1,0:T(8,128)(2,1)S(1)}, u32[]{:S(2)}, u32[]{:S(2)}) collective-permute-start(bf16[16,1024]{1,0:T(8,128)(2,1)S(1)} %get-tuple-element.23), channel_id=1, source_target_pairs={{0,48},{8,56},{16,0},{24,8},{32,16},{40,24},{48,32},{56,40},{64,11... | collective-permute-start | bytes 98312 | tf_op jit(solution)/shard_map/ppermute | solution.py:349

commit v3 on v2

v3 whole, which is shorter than its diff:
```python
import functools
import math

import jax
import jax.numpy as jnp
from jax import lax
from jax.experimental import pallas as pl
from jax.experimental.pallas import tpu as pltpu
from jax.sharding import PartitionSpec as P

D = 4096
HD = 128
DD = 1024
DHD = 64
DHEADS = 8
LEVELS = 8
FRAMES = 2
CORES = 2
SIDE = 4
STEPS = (2, 1, 3)
EXTRA = 128
MIB = 2**20
LIMIT = 16
WARM_FLOPS = 10**10
NT = (((1,), (1,)), ((), ()))


def dot_nt(a, b):
    return lax.dot_general(a, b, NT, preferred_element_type=jnp.float32)


def dot_nn(a, b):
    return jnp.dot(a, b, preferred_element_type=jnp.float32)


def iota(shape, axis):
    return lax.broadcasted_iota(jnp.int32, shape, axis)


def warm_kernel(out_ref):
    out_ref[...] = jnp.zeros_like(out_ref)


def attend_kernel(
    lengths_hbm, q_ref, nk_ref, nv_ref, k_ref, v_hbm, w_ref, own_hbm, order_ref, out_hbm, own_ref,
    lengths_buf, v_buf, small, sent_buf, sems
):
    get_lengths = pltpu.make_async_copy(lengths_hbm, lengths_buf, sems.at[0])
    get_values = pltpu.make_async_copy(v_hbm, v_buf, sems.at[1])
    get_own = pltpu.make_async_copy(own_hbm, own_ref, sems.at[2])
    get_lengths.start()
    get_values.start()
    get_own.start()
    dialogues = q_ref.shape[0]
    width = q_ref.shape[2]
    rows = dialogues * FRAMES
    heads = width // HD
    stacked = heads * rows
    slots = k_ref.shape[1]
    for i, ref in enumerate((q_ref, nk_ref, nv_ref)):
        for d in range(dialogues):
            small[i, FRAMES * d : FRAMES * (d + 1), :] = ref[d].astype(jnp.float32)
    query = small[0]
    fresh_key = small[1].astype(jnp.bfloat16)
    fresh_value = small[2].astype(jnp.bfloat16)
    head_of = iota((rows, width), 1) // HD
    spread = jnp.concatenate(
        [jnp.where(head_of == h, query, 0.0) for h in range(heads)], axis=0
    ).astype(jnp.bfloat16)
    scale = 1.0 / math.sqrt(HD)

    row = iota((stacked, slots), 0)
    slot = iota((stacked, slots), 1)
    dialogue = (row % rows) // FRAMES
    scores = jnp.zeros((stacked, slots), jnp.float32)
    for d in range(dialogues):
        scores = jnp.where(dialogue == d, dot_nt(spread, k_ref[d]), scores)
    row_n = iota((stacked, rows), 0) % rows
    col_n = iota((stacked, rows), 1)
    seen = (row_n // FRAMES == col_n // FRAMES) & (col_n <= row_n)
    fresh = jnp.where(seen, dot_nt(spread, fresh_key) * scale, -jnp.inf)
    get_lengths.wait()
    live = jnp.zeros((stacked, slots), jnp.int32)
    for d in range(dialogues):
        live = jnp.where(dialogue == d, lengths_buf[d], live)
    scores = jnp.where(slot < live, scores * scale, -jnp.inf)
    largest = jnp.maximum(
        jnp.max(scores, axis=-1, keepdims=True), jnp.max(fresh, axis=-1, keepdims=True)
    )
    exp_cache = jnp.exp(scores - largest)
    exp_fresh = jnp.exp(fresh - largest)
    total = jnp.sum(exp_cache, axis=-1, keepdims=True) + jnp.sum(
        exp_fresh, axis=-1, keepdims=True
    )
    prob_cache = exp_cache / total
    prob_fresh = (exp_fresh / total).astype(jnp.bfloat16)
    mixed = dot_nn(prob_fresh, fresh_value)
    get_values.wait()
    for d in range(dialogues):
        own = jnp.where(dialogue == d, prob_cache, 0.0).astype(jnp.bfloat16)
        mixed = mixed + dot_nn(own, v_buf[d])
    attended = mixed[:rows]
    for h in range(1, heads):
        attended = jnp.where(head_of == h, mixed[h * rows : (h + 1) * rows], attended)
    attended = attended.astype(jnp.bfloat16)
    peers, _, features = sent_buf.shape
    sends = []
    for t in range(peers):
        sent_buf[t] = dot_nn(attended, w_ref[:, t * features : (t + 1) * features]).astype(
            jnp.bfloat16
        )
        sends.append(pltpu.make_async_copy(sent_buf.at[t], out_hbm.at[t], sems.at[3 + t]))
        sends[t].start()
    get_own.wait()
    for send in sends:
        send.wait()


def gather_kernel(*refs):
    out_ref = refs[-1]
    for i in range(SIDE):
        out_ref[i] = refs[i][0]


def lookup_kernel(*refs):
    ids_refs, (own_ref, other_ref) = refs[:SIDE], refs[SIDE : SIDE + 2]
    out_refs, (done_ref, found_buf) = refs[SIDE + 2 : 2 * SIDE + 2], refs[2 * SIDE + 2 :]
    span = own_ref.shape[1]
    width = own_ref.shape[2]
    entries = LEVELS * span
    count = FRAMES * LEVELS
    members = SIDE * SIDE
    rows = members * count
    me = lax.axis_index("batch")

    pick = (iota((rows, members), 0) // count == iota((rows, members), 1)).astype(jnp.bfloat16)
    row = iota((rows, LEVELS), 0)
    lane = iota((rows, LEVELS), 1)
    block = jnp.zeros((rows, LEVELS), jnp.float32)
    inner = jnp.zeros((rows, LEVELS), jnp.float32)
    for f in range(FRAMES):
        ids = jnp.concatenate([ref[:, f, :] for ref in ids_refs], axis=0)
        mine = (lane == row % LEVELS) & ((row // LEVELS) % FRAMES == f)
        high = (ids // span).astype(jnp.float32).astype(jnp.bfloat16)
        low = (ids % span).astype(jnp.float32).astype(jnp.bfloat16)
        block = jnp.where(mine, dot_nn(pick, high), block)
        inner = jnp.where(mine, dot_nn(pick, low), inner)
    block = jnp.sum(block, axis=1, keepdims=True).astype(jnp.int32)
    inner = jnp.sum(inner, axis=1, keepdims=True).astype(jnp.int32)
    level = iota((rows, 1), 0) % LEVELS
    place = inner + level * span
    at_own = jnp.where(block == me, place, -1)
    at_other = jnp.where(block == (me ^ 1), place, -1)
    entry = iota((rows, entries), 1)
    hot_own = jnp.where(entry == at_own, 1.0, 0.0).astype(jnp.bfloat16)
    hot_other = jnp.where(entry == at_other, 1.0, 0.0).astype(jnp.bfloat16)
    found = dot_nn(hot_own, own_ref[...].reshape(entries, width))
    found = found + dot_nn(hot_other, other_ref[...].reshape(entries, width))
    found_buf[...] = found.astype(jnp.bfloat16).reshape(found_buf.shape)
    for s in range(SIDE):
        out_refs[s][...] = found_buf[s * SIDE : (s + 1) * SIDE]
    done_ref[...] = jnp.zeros_like(done_ref)


def collect_kernel(own_ref, *refs):
    arrived, out_refs = refs[: SIDE - 1], refs[SIDE - 1 :]
    for s in range(SIDE):
        value = own_ref[s]
        for ref in arrived:
            value = value + ref[s]
        out_refs[s][...] = value


def fetch_kernel(w_hbm, order_ref, out_ref, sem):
    copy = pltpu.make_async_copy(w_hbm, out_ref, sem)
    copy.start()
    copy.wait()


def middle_kernel(
    shares_ref, residual_ref, gain_ref, w_hbm, order_ref, stream_ref, sent_ref,
    w_ref, rows_buf, sent_buf, sem
):
    get_weight = pltpu.make_async_copy(w_hbm, w_ref, sem)
    get_weight.start()
    dialogues = residual_ref.shape[0]
    for d in range(dialogues):
        rows_buf[FRAMES * d : FRAMES * (d + 1), :] = residual_ref[d].astype(jnp.float32)
    hidden = rows_buf[...]
    share = shares_ref[0].astype(jnp.float32)
    for t in range(1, shares_ref.shape[0]):
        share = share + shares_ref[t].astype(jnp.float32)
    hidden = hidden + share
    rows_buf[...] = hidden
    squares = jnp.sum(hidden * hidden, axis=-1, keepdims=True)
    scaled = (hidden * gain_ref[...]).astype(jnp.bfloat16)
    width = w_ref.shape[1]
    sent_buf[:, width:] = jnp.broadcast_to(squares, (hidden.shape[0], EXTRA))
    for d in range(dialogues):
        stream_ref[d] = rows_buf[FRAMES * d : FRAMES * (d + 1), :].astype(jnp.bfloat16)
    get_weight.wait()
    sent_buf[:, :width] = dot_nn(scaled, w_ref[...])
    for d in range(dialogues):
        sent_ref[d] = sent_buf[FRAMES * d : FRAMES * (d + 1), :]


def depth_kernel(
    terms_ref, *refs
):
    table_refs = refs[:SIDE]
    gain_ref, qkv_ref, o_hbm, out_ref, o_ref, sem = refs[SIDE:]
    get_weight = pltpu.make_async_copy(o_hbm, o_ref, sem)
    get_weight.start()
    count, width = table_refs[0].shape
    terms = terms_ref[0]
    for t in range(1, terms_ref.shape[0]):
        terms = terms + terms_ref[t]
    inverse = lax.rsqrt(terms[:, width : width + 1] / D + 1e-05)
    proj = terms[:, :width] * inverse
    values = table_refs[0][...].astype(jnp.float32)
    for ref in table_refs[1:]:
        values = values + ref[...].astype(jnp.float32)
    frame = iota((count, width), 0) // LEVELS
    depth_input = values + jnp.where(frame == 0, proj[0:1], proj[1:2])
    mean = jnp.sum(depth_input * depth_input, axis=-1, keepdims=True) / width
    normed = (depth_input * lax.rsqrt(mean + 1e-05) * gain_ref[...]).astype(jnp.bfloat16)
    heads_width = DHEADS * DHD
    query = dot_nn(normed, qkv_ref[:, :heads_width]).astype(jnp.bfloat16).astype(jnp.float32)
    key = dot_nn(normed, qkv_ref[:, heads_width : 2 * heads_width]).astype(jnp.bfloat16)
    value = dot_nn(normed, qkv_ref[:, 2 * heads_width :]).astype(jnp.bfloat16)
    head_of = iota((count, heads_width), 1) // DHD
    spread = jnp.concatenate(
        [jnp.where(head_of == h, query, 0.0) for h in range(DHEADS)], axis=0
    ).astype(jnp.bfloat16)
    scores = dot_nt(spread, key) * (1.0 / math.sqrt(DHD))
    row = iota(scores.shape, 0) % count
    col = iota(scores.shape, 1)
    seen = (row // LEVELS == col // LEVELS) & (col <= row)
    exps = jnp.where(seen, jnp.exp(scores), 0.0)
    probs = (exps / jnp.sum(exps, axis=-1, keepdims=True)).astype(jnp.bfloat16)
    spread_out = dot_nn(probs, value)
    mixed = spread_out[:count]
    for h in range(1, DHEADS):
        mixed = jnp.where(head_of == h, spread_out[h * count : (h + 1) * count], mixed)
    get_weight.wait()
    out_ref[...] = (depth_input + dot_nn(mixed.astype(jnp.bfloat16), o_ref[...])).astype(
        jnp.bfloat16
    )


VMEM = pl.BlockSpec(memory_space=pltpu.VMEM)
SMEM = pl.BlockSpec(memory_space=pltpu.SMEM)
ANY = pl.BlockSpec(memory_space=pl.ANY)


def hbm(*arrays):
    return tuple(pltpu.with_memory_space_constraint(a, pltpu.HBM) for a in arrays)


def call(kernel, name, outs, ins, out_specs, scratch, limit, flops, moved):
    return pl.pallas_call(
        kernel,
        name=name,
        out_shape=outs,
        in_specs=ins,
        out_specs=out_specs,
        scratch_shapes=scratch,
        compiler_params=pltpu.CompilerParams(vmem_limit_bytes=limit * MIB),
        cost_estimate=pl.CostEstimate(flops=flops, bytes_accessed=moved, transcendentals=0),
    )


def flipped(size, step, s):
    span = SIDE * step
    return [(b, b // span * span + (b % span // step ^ s) * step + b % step) for b in range(size)]


def sorted_steps(arrays):
    return [arrays[STEPS.index(s)] for s in range(1, SIDE)]


def per_device(
    residual,
    new_queries,
    new_keys,
    new_values,
    cache_keys,
    cache_values,
    lengths,
    out_weight,
    temporal_gain,
    in_weight,
    tokens,
    level_tables,
    depth_gain,
    depth_qkv,
    depth_out,
):
    shape = jax.ShapeDtypeStruct
    bf16, f32 = jnp.bfloat16, jnp.float32
    held, _, features = residual.shape
    tensor_size = lax.axis_size("tensor")
    batch_size = lax.axis_size("batch")
    rows = held * FRAMES
    width = in_weight.shape[1]
    members = batch_size // CORES
    count = FRAMES * LEVELS

    other_tables = lax.ppermute(level_tables, "batch", flipped(batch_size, 1, 1))
    order = call(
        warm_kernel, "warm", pltpu.VMEM((8, 128), f32), [], VMEM, [], LIMIT, WARM_FLOPS, 1
    )()
    near = [lax.ppermute(tokens, "batch", flipped(batch_size, CORES, s)) for s in STEPS]
    head_terms, own_tables = call(
        attend_kernel,
        "attend",
        (
            pltpu.HBM((tensor_size, rows, features), bf16),
            pltpu.VMEM(level_tables.shape, bf16),
        ),
        [ANY] + [VMEM] * 4 + [ANY, VMEM, ANY, VMEM],
        (ANY, VMEM),
        [
            pltpu.SMEM((held,), jnp.int32),
            pltpu.VMEM(cache_values.shape, bf16),
            pltpu.VMEM((3, rows, new_queries.shape[2]), f32),
            pltpu.VMEM((tensor_size, rows, features), bf16),
            pltpu.SemaphoreType.DMA((3 + tensor_size,)),
        ],
        LIMIT,
        10**8,
        4 * 2**20,
    )(
        *hbm(lengths),
        new_queries,
        new_keys,
        new_values,
        cache_keys,
        *hbm(cache_values),
        out_weight,
        *hbm(level_tables),
        order,
    )
    column = call(
        gather_kernel,
        "gather",
        pltpu.VMEM((SIDE, FRAMES, LEVELS), jnp.int32),
        [VMEM] * (SIDE + 1),
        VMEM,
        [],
        LIMIT,
        10**6,
        1,
    )(tokens, *sorted_steps(near), own_tables)
    ids = [lax.ppermute(column, "batch", flipped(batch_size, CORES * SIDE, s)) for s in STEPS]

    shares = lax.all_to_all(head_terms, "tensor", 0, 0, tiled=True)

    *partial_rows, looked = call(
        lookup_kernel,
        "lookup",
        (
            *[pltpu.VMEM((SIDE, count, width), bf16)] * SIDE,
            pltpu.VMEM((8, 128), f32),
        ),
        [VMEM] * (SIDE + 2),
        (VMEM,) * (SIDE + 1),
        [
            pltpu.VMEM((members, count, width), bf16),
        ],
        LIMIT,
        10**11,
        1,
    )(column, *sorted_steps(ids), own_tables, other_tables)
    across = [
        lax.ppermute(partial_rows[s], "batch", flipped(batch_size, CORES * SIDE, s))
        for s in STEPS
    ]
    own_rows, *side_rows = call(
        collect_kernel,
        "collect",
        [pltpu.VMEM((count, width), bf16)] * SIDE,
        [VMEM] * SIDE,
        [VMEM] * SIDE,
        [],
        LIMIT,
        10**6,
        1,
    )(partial_rows[0], *across)
    along = [
        lax.ppermute(side_rows[s - 1], "batch", flipped(batch_size, CORES, s)) for s in STEPS
    ]

    temporal_out, sent = call(
        middle_kernel,
        "middle",
        (pltpu.HBM(residual.shape, bf16), pltpu.HBM((held, FRAMES, width + EXTRA), f32)),
        [VMEM] * 3 + [ANY, VMEM],
        (VMEM, VMEM),
        [
            pltpu.VMEM(in_weight.shape, bf16),
            pltpu.VMEM((rows, features), f32),
            pltpu.VMEM((rows, width + EXTRA), f32),
            pltpu.SemaphoreType.DMA,
        ],
        LIMIT,
        10**9,
        1,
    )(shares, residual, temporal_gain.astype(f32).reshape(1, features), *hbm(in_weight), looked)
    terms = lax.all_to_all(sent, "tensor", 0, 0, tiled=True)

    qkv_near = call(
        fetch_kernel,
        "fetch",
        pltpu.VMEM(depth_qkv.shape, bf16),
        [ANY, VMEM],
        VMEM,
        [pltpu.SemaphoreType.DMA],
        LIMIT,
        10**9,
        1,
    )(*hbm(depth_qkv), own_rows)
    states = call(
        depth_kernel,
        "depth",
        pltpu.HBM((count, width), bf16),
        [VMEM] * (SIDE + 3) + [ANY],
        VMEM,
        [pltpu.VMEM(depth_out.shape, bf16), pltpu.SemaphoreType.DMA],
        LIMIT,
        10**9,
        1,
    )(terms, own_rows, *along, depth_gain.astype(f32).reshape(1, width), qkv_near, *hbm(depth_out))
    return (temporal_out, states.reshape(1, FRAMES, LEVELS, width))


def solution(mesh):
    placed = (
        P("batch", None, "tensor"),
        P("batch", None, "tensor"),
        P("batch", None, "tensor"),
        P("batch", None, "tensor"),
        P("batch", None, "tensor"),
        P("batch", None, "tensor"),
        P("batch"),
        P("tensor", None),
        P("tensor"),
        P("tensor", None),
        P(("batch", "tensor"), None, None),
        P(None, "batch", None),
        P(),
        P(),
        P(),
    )
    return jax.shard_map(
        per_device,
        mesh=mesh,
        in_specs=placed,
        out_specs=(P("batch", None, "tensor"), P(("batch", "tensor"), None, None, None)),
        check_vma=False,
    )
```

time: 52.7 us -> 48.4 us (0.918)
  the two profiles are of different devices: /device:TPU:56 before, /device:TPU:4 now
where the time goes in v3:
time: 48.4 us; the launch traced here: 48.1 us
  starting transfers between devices  28.7 us (59%)
  Pallas kernels  10.8 us (22%)
  waiting for transfers between devices  7.58 us (16%)
  between operations  0.86 us (2%)
    all_to_all x1, starting transfers between devices, per_device(): shares = lax.all_to_all(head_terms, 'tensor', 0, 0, tiled=True)  8.47 us
    ppermute x3, starting transfers between devices, per_device(): lax.ppermute(tokens, 'batch', flipped(batch_size, CORES, s))  4.34 us
    ppermute x3, starting transfers between devices, per_device(): lax.ppermute(partial_rows[s], 'batch', flipped(batch_size, CORES * SIDE, s))  4.18 us
    ppermute x3, starting transfers between devices, per_device(): lax.ppermute(side_rows[s - 1], 'batch', flipped(batch_size, CORES, s))  4.18 us
    ppermute x3, starting transfers between devices, per_device(): lax.ppermute(column, 'batch', flipped(batch_size, CORES * SIDE, s))  4.09 us
    all_to_all x1, waiting for transfers between devices, per_device(): shares = lax.all_to_all(head_terms, 'tensor', 0, 0, tiled=True)  3.82 us
    all_to_all x1, starting transfers between devices, per_device(): terms = lax.all_to_all(sent, 'tensor', 0, 0, tiled=True)  3.39 us
    pallas_call x1, Pallas kernels, per_device(): call(attend_kernel, 'attend', (pltpu.HBM((tensor_size, rows, features), b...  3.1 us
  transfers between devices with their start and end apart: 15, of which 3 were waited for; matrix products, arithmetic and copies ran while one was open for 0% of the time, Pallas kernels for 17%

profile of v3, /device:TPU:4, one launch (start us, length us, event | category | flops | bytes accessed | tf_op | source)
XLA Modules:
  0.0 48.1 jit_solution(1332924605950880481)
XLA Ops:
  0.6 0.0 copy-start
  0.6 0.0 copy-start.1
  0.7 0.0 copy-start.4
  0.7 0.0 copy-start.3
  0.7 0.0 copy-start.2
  0.7 0.1 collective-permute-start.6
  0.8 3.3 %collective-permute-start.1 = (s32[1,2,8]{2,1,0:T(2,128)}, s32[1,2,8]{2,1,0:T(2,128)S(1)}, u32[]{:S(2)}, u32[]{:S(2)}) collective-permute-start(s32[1,2,8]{2,1,0:T(2,128)} %refs_0_.1), channel_id=1, source_target_pairs={{0,32},{8,40},{16,48},{24,56},{32,0},{40,8},{48,16},{56,24},{64,96... | collective-permute-start | bytes 200 | tf_op jit(solution)/shard_map/ppermute | solution.py:313
  4.1 0.7 %collective-permute-start = (s32[1,2,8]{2,1,0:T(2,128)}, s32[1,2,8]{2,1,0:T(2,128)S(1)}, u32[]{:S(2)}, u32[]{:S(2)}) collective-permute-start(s32[1,2,8]{2,1,0:T(2,128)} %refs_0_.1), channel_id=1, source_target_pairs={{0,16},{8,24},{16,0},{24,8},{32,48},{40,56},{48,32},{56,40},{64,80... | collective-permute-start | bytes 200 | tf_op jit(solution)/shard_map/ppermute | solution.py:313
  4.7 0.4 collective-permute-start.2
  5.1 0.0 copy-done
  5.1 0.0 copy-done.1
  5.1 0.0 copy-done.4
  5.1 0.0 copy-done.3
  5.1 0.0 copy-done.2
  5.2 0.0 copy-start.5
  5.2 3.1 %attend.1 = (bf16[8,16,512]{2,1,0:T(8,128)(2,1)}, bf16[8,64,1024]{2,1,0:T(8,128)(2,1)S(1)}) custom-call(s32[8]{0:T(128)} %lengths_hbm.1, bf16[8,2,256]{2,1,0:T(2,128)(2,1)S(1)} %copy-done.2, bf16[8,2,256]{2,1,0:T(2,128)(2,1)S(1)} %copy-done.3, bf16[8,2,256]{2,1,0:T(2,128)(2,1)S(1)} %copy-done.4, bf16[8,256,256]{2,1,0:T(8,128)(2,1)S(1)} %copy-done.1, ...), custom_call_target="tpu_custom_call" | custom-call | flops 100000000 | bytes 4194304 | tf_op jit(solution)/shard_map/attend/pallas_call | solution.py:314
  8.3 0.0 collective-permute-done.1.refs_2_
  8.3 0.0 collective-permute-done.refs_1_
  8.3 1.4 %collective-permute-done.2.refs_3_ = s32[1,2,8]{2,1,0:T(2,128)S(1)} collective-permute-done((s32[1,2,8]{2,1,0:T(2,128)}, s32[1,2,8]{2,1,0:T(2,128)S(1)}, u32[]{:S(2)}, u32[]{:S(2)}) %collective-permute-start.2) | collective-permute-done | bytes 96 | tf_op jit(solution)/shard_map/ppermute | solution.py:313
  9.7 0.0 copy-done.5
  9.7 0.5 %collective-permute-start.5 = (s32[4,2,8]{2,1,0:T(2,128)S(1)}, s32[4,2,8]{2,1,0:T(2,128)S(1)}, u32[]{:S(2)}, u32[]{:S(2)}) collective-permute-start(s32[4,2,8]{2,1,0:T(2,128)S(1)} %gather.1.refs_0_), channel_id=1, source_target_pairs={{0,192},{8,200},{16,208},{24,216},{32,224},{40,232},{48,240},{56,2... | collective-permute-start | bytes 776 | tf_op jit(solution)/shard_map/ppermute | solution.py:355
  10.3 2.7 %collective-permute-start.4 = (s32[4,2,8]{2,1,0:T(2,128)S(1)}, s32[4,2,8]{2,1,0:T(2,128)S(1)}, u32[]{:S(2)}, u32[]{:S(2)}) collective-permute-start(s32[4,2,8]{2,1,0:T(2,128)S(1)} %gather.1.refs_0_), channel_id=1, source_target_pairs={{0,128},{8,136},{16,144},{24,152},{32,160},{40,168},{48,176},{56,1... | collective-permute-start | bytes 776 | tf_op jit(solution)/shard_map/ppermute | solution.py:355
  13.0 0.8 %collective-permute-start.3 = (s32[4,2,8]{2,1,0:T(2,128)S(1)}, s32[4,2,8]{2,1,0:T(2,128)S(1)}, u32[]{:S(2)}, u32[]{:S(2)}) collective-permute-start(s32[4,2,8]{2,1,0:T(2,128)S(1)} %gather.1.refs_0_), channel_id=1, source_target_pairs={{0,64},{8,72},{16,80},{24,88},{32,96},{40,104},{48,112},{56,120},{... | collective-permute-start | bytes 776 | tf_op jit(solution)/shard_map/ppermute | solution.py:355
  13.8 8.5 %all-to-all-start = ((bf16[8,16,512]{2,1,0:T(8,128)(2,1)}), bf16[8,16,512]{2,1,0:T(8,128)(2,1)S(1)}, u32[]{:S(2)}, u32[]{:S(2)}) async-start(bf16[8,16,512]{2,1,0:T(8,128)(2,1)} %get-tuple-element.15), calls=%async_computation | async-start | bytes 262144 | tf_op jit(solution)/shard_map/all_to_all | solution.py:357
  22.3 0.0 copy-start.8
  22.3 0.0 copy-start.6
  22.3 0.0 collective-permute-done.5.refs_3_
  22.3 0.0 collective-permute-done.4.refs_2_
  22.3 0.0 collective-permute-done.3.refs_1_
  22.4 0.0 collective-permute-done.6.refs_5_
  22.4 1.0 %lookup.1 = (bf16[4,16,1024]{2,1,0:T(8,128)(2,1)S(1)}, bf16[4,16,1024]{2,1,0:T(8,128)(2,1)S(1)}, bf16[4,16,1024]{2,1,0:T(8,128)(2,1)S(1)}, bf16[4,16,1024]{2,1,0:T(8,128)(2,1)S(1)}, f32[8,128]{1,0:T(8,128)S(1)}) custom-call(s32[4,2,8]{2,1,0:T(2,128)S(1)} %gather.1.refs_0_, s32[4,2,8]{2,1,0:T(2,128)S(1)} %collective-permute-done.3.refs_1_, ...), custom_call_target="tpu_custom_call" | custom-call | flops 99999997952 | bytes 1 | tf_op jit(solution)/shard_map/lookup/pallas_call | solution.py:359
  23.4 0.0 copy-start.7
  23.4 0.6 %collective-permute-start.7 = (bf16[4,16,1024]{2,1,0:T(8,128)(2,1)S(1)}, bf16[4,16,1024]{2,1,0:T(8,128)(2,1)S(1)}, u32[]{:S(2)}, u32[]{:S(2)}) collective-permute-start(bf16[4,16,1024]{2,1,0:T(8,128)(2,1)S(1)} %get-tuple-element.21), channel_id=1, source_target_pairs={{0,128},{8,136},{16,144},{24,152},{32,160},{40,168},{48,176},{56,1... | collective-permute-start | bytes 393224 | tf_op jit(solution)/shard_map/ppermute | solution.py:376
  24.0 2.1 %collective-permute-start.8 = (bf16[4,16,1024]{2,1,0:T(8,128)(2,1)S(1)}, bf16[4,16,1024]{2,1,0:T(8,128)(2,1)S(1)}, u32[]{:S(2)}, u32[]{:S(2)}) collective-permute-start(bf16[4,16,1024]{2,1,0:T(8,128)(2,1)S(1)} %get-tuple-element.22), channel_id=1, source_target_pairs={{0,64},{8,72},{16,80},{24,88},{32,96},{40,104},{48,112},{56,120},{... | collective-permute-start | bytes 393224 | tf_op jit(solution)/shard_map/ppermute | solution.py:376
  26.1 1.5 %collective-permute-start.9 = (bf16[4,16,1024]{2,1,0:T(8,128)(2,1)S(1)}, bf16[4,16,1024]{2,1,0:T(8,128)(2,1)S(1)}, u32[]{:S(2)}, u32[]{:S(2)}) collective-permute-start(bf16[4,16,1024]{2,1,0:T(8,128)(2,1)S(1)} %get-tuple-element.23), channel_id=1, source_target_pairs={{0,192},{8,200},{16,208},{24,216},{32,224},{40,232},{48,240},{56,2... | collective-permute-start | bytes 393224 | tf_op jit(solution)/shard_map/ppermute | solution.py:376
  27.6 0.0 copy-done.8
  27.6 3.8 %all-to-all-done.shares_ref = bf16[8,16,512]{2,1,0:T(8,128)(2,1)S(1)} async-done(((bf16[8,16,512]{2,1,0:T(8,128)(2,1)}), bf16[8,16,512]{2,1,0:T(8,128)(2,1)S(1)}, u32[]{:S(2)}, u32[]{:S(2)}) %all-to-all-start) | async-done | bytes 131104 | tf_op jit(solution)/shard_map/all_to_all | solution.py:357
  31.4 0.0 copy-done.6
  31.4 2.1 %middle.1 = (bf16[8,2,512]{2,1,0:T(2,128)(2,1)}, f32[8,2,1152]{2,1,0:T(2,128)}) custom-call(bf16[8,16,512]{2,1,0:T(8,128)(2,1)S(1)} %all-to-all-done.shares_ref, bf16[8,2,512]{2,1,0:T(2,128)(2,1)S(1)} %copy-done.6, f32[1,512]{1,0:T(1,128)S(1)} %bitcast.4, bf16[512,1024]{1,0:T(8,128)(2,1)} %w_hbm.2, f32[8,128]{1,0:T(8,128)S(1)} %get-tuple-element.17.order_ref), custom_call_target="tpu_custom_call" | custom-call | flops 1000000000 | bytes 1 | tf_op jit(solution)/shard_map/middle/pallas_call | solution.py:394
  33.5 3.4 %all-to-all-start.1 = ((f32[8,2,1152]{2,1,0:T(2,128)}), f32[8,2,1152]{2,1,0:T(2,128)S(1)}, u32[]{:S(2)}, u32[]{:S(2)}) async-start(f32[8,2,1152]{2,1,0:T(2,128)} %get-tuple-element.19), calls=%async_computation.1 | async-start | bytes 147456 | tf_op jit(solution)/shard_map/all_to_all | solution.py:410
  36.9 0.0 copy-done.7
  36.9 0.0 collective-permute-done.7.refs_0_
  36.9 0.0 collective-permute-done.8.refs_1_
  37.0 0.0 collective-permute-done.9.refs_2_
  37.0 1.8 %collective-permute-start.10 = (bf16[16,1024]{1,0:T(8,128)(2,1)S(1)}, bf16[16,1024]{1,0:T(8,128)(2,1)S(1)}, u32[]{:S(2)}, u32[]{:S(2)}) collective-permute-start(bf16[16,1024]{1,0:T(8,128)(2,1)S(1)} %get-tuple-element.25), channel_id=1, source_target_pairs={{0,32},{8,40},{16,48},{24,56},{32,0},{40,8},{48,16},{56,24},{64,96... | collective-permute-start | bytes 98312 | tf_op jit(solution)/shard_map/ppermute | solution.py:391
  38.8 0.7 %collective-permute-start.11 = (bf16[16,1024]{1,0:T(8,128)(2,1)S(1)}, bf16[16,1024]{1,0:T(8,128)(2,1)S(1)}, u32[]{:S(2)}, u32[]{:S(2)}) collective-permute-start(bf16[16,1024]{1,0:T(8,128)(2,1)S(1)} %get-tuple-element.26), channel_id=1, source_target_pairs={{0,16},{8,24},{16,0},{24,8},{32,48},{40,56},{48,32},{56,40},{64,80... | collective-permute-start | bytes 98312 | tf_op jit(solution)/shard_map/ppermute | solution.py:391
  39.5 1.7 %collective-permute-start.12 = (bf16[16,1024]{1,0:T(8,128)(2,1)S(1)}, bf16[16,1024]{1,0:T(8,128)(2,1)S(1)}, u32[]{:S(2)}, u32[]{:S(2)}) collective-permute-start(bf16[16,1024]{1,0:T(8,128)(2,1)S(1)} %get-tuple-element.27), channel_id=1, source_target_pairs={{0,48},{8,56},{16,32},{24,40},{32,16},{40,24},{48,0},{56,8},{64,11... | collective-permute-start | bytes 98312 | tf_op jit(solution)/shard_map/ppermute | solution.py:391
  41.2 1.9 %fetch.1.refs_5_ = bf16[1024,1536]{1,0:T(8,128)(2,1)S(1)} custom-call(bf16[1024,1536]{1,0:T(8,128)(2,1)} %w_hbm.3, bf16[16,1024]{1,0:T(8,128)(2,1)S(1)} %get-tuple-element.24.order_ref.refs_0_), custom_call_target="tpu_custom_call" | custom-call | flops 1000000000 | bytes 1 | tf_op jit(solution)/shard_map/fetch/pallas_call | solution.py:412
  43.1 2.3 %all-to-all-done.1.terms_ref = f32[8,2,1152]{2,1,0:T(2,128)S(1)} async-done(((f32[8,2,1152]{2,1,0:T(2,128)}), f32[8,2,1152]{2,1,0:T(2,128)S(1)}, u32[]{:S(2)}, u32[]{:S(2)}) %all-to-all-start.1) | async-done | bytes 73760 | tf_op jit(solution)/shard_map/all_to_all | solution.py:410
  45.4 0.0 collective-permute-done.10.refs_1_
  45.4 0.0 collective-permute-done.11.refs_2_
  45.4 0.0 collective-permute-done.12.refs_3_
  45.4 2.7 %depth.1 = bf16[16,1024]{1,0:T(8,128)(2,1)} custom-call(f32[8,2,1152]{2,1,0:T(2,128)S(1)} %all-to-all-done.1.terms_ref, bf16[16,1024]{1,0:T(8,128)(2,1)S(1)} %get-tuple-element.24.order_ref.refs_0_, bf16[16,1024]{1,0:T(8,128)(2,1)S(1)} %collective-permute-done.10.refs_1_, bf16[16,1024]{1,0:T(8,128)(2,1)S(1)} %collective-permute-done.11.refs_2_, ...), custom_call_target="tpu_custom_call" | custom-call | flops 1000000000 | bytes 1 | tf_op jit(solution)/shard_map/depth/pallas_call | solution.py:423
  (5 shorter events, 0.0 us)
Async XLA Ops:
  0.6 4.5 %copy-start = (bf16[256,4096]{1,0:T(8,128)(2,1)S(1)}, bf16[256,4096]{1,0:T(8,128)(2,1)}, u32[]{:S(2)}) copy-start(bf16[256,4096]{1,0:T(8,128)(2,1)} %w_ref.1) | copy-start | bytes 6291460
  0.6 4.5 %copy-start.1 = (bf16[8,256,256]{2,1,0:T(8,128)(2,1)S(1)}, bf16[8,256,256]{2,1,0:T(8,128)(2,1)}, u32[]{:S(2)}) copy-start(bf16[8,256,256]{2,1,0:T(8,128)(2,1)} %k_ref.1) | copy-start | bytes 3145732
  0.7 4.5 %copy-start.4 = (bf16[8,2,256]{2,1,0:T(2,128)(2,1)S(1)}, bf16[8,2,256]{2,1,0:T(2,128)(2,1)}, u32[]{:S(2)}) copy-start(bf16[8,2,256]{2,1,0:T(2,128)(2,1)} %nv_ref.1) | copy-start | bytes 24580
  0.7 4.5 %copy-start.3 = (bf16[8,2,256]{2,1,0:T(2,128)(2,1)S(1)}, bf16[8,2,256]{2,1,0:T(2,128)(2,1)}, u32[]{:S(2)}) copy-start(bf16[8,2,256]{2,1,0:T(2,128)(2,1)} %nk_ref.1) | copy-start | bytes 24580
  0.7 4.5 %copy-start.2 = (bf16[8,2,256]{2,1,0:T(2,128)(2,1)S(1)}, bf16[8,2,256]{2,1,0:T(2,128)(2,1)}, u32[]{:S(2)}) copy-start(bf16[8,2,256]{2,1,0:T(2,128)(2,1)} %q_ref.1) | copy-start | bytes 24580
  0.7 21.7 %collective-permute-start.6 = (bf16[8,64,1024]{2,1,0:T(8,128)(2,1)}, bf16[8,64,1024]{2,1,0:T(8,128)(2,1)S(1)}, u32[]{:S(2)}, u32[]{:S(2)}) collective-permute-start(bf16[8,64,1024]{2,1,0:T(8,128)(2,1)} %own_hbm.1), channel_id=1, source_target_pairs={{0,8},{8,0},{16,24},{24,16},{32,40},{40,32},{48,56},{56,48},{64,72... | collective-permute-start | bytes 3145736 | tf_op jit(solution)/shard_map/ppermute | solution.py:309
  0.8 7.5 %collective-permute-start.1 = (s32[1,2,8]{2,1,0:T(2,128)}, s32[1,2,8]{2,1,0:T(2,128)S(1)}, u32[]{:S(2)}, u32[]{:S(2)}) collective-permute-start(s32[1,2,8]{2,1,0:T(2,128)} %refs_0_.1), channel_id=1, source_target_pairs={{0,32},{8,40},{16,48},{24,56},{32,0},{40,8},{48,16},{56,24},{64,96... | collective-permute-start | bytes 200 | tf_op jit(solution)/shard_map/ppermute | solution.py:313
  4.1 4.2 %collective-permute-start = (s32[1,2,8]{2,1,0:T(2,128)}, s32[1,2,8]{2,1,0:T(2,128)S(1)}, u32[]{:S(2)}, u32[]{:S(2)}) collective-permute-start(s32[1,2,8]{2,1,0:T(2,128)} %refs_0_.1), channel_id=1, source_target_pairs={{0,16},{8,24},{16,0},{24,8},{32,48},{40,56},{48,32},{56,40},{64,80... | collective-permute-start | bytes 200 | tf_op jit(solution)/shard_map/ppermute | solution.py:313
  4.7 5.0 %collective-permute-start.2 = (s32[1,2,8]{2,1,0:T(2,128)}, s32[1,2,8]{2,1,0:T(2,128)S(1)}, u32[]{:S(2)}, u32[]{:S(2)}) collective-permute-start(s32[1,2,8]{2,1,0:T(2,128)} %refs_0_.1), channel_id=1, source_target_pairs={{0,48},{8,56},{16,32},{24,40},{32,16},{40,24},{48,0},{56,8},{64,11... | collective-permute-start | bytes 200 | tf_op jit(solution)/shard_map/ppermute | solution.py:313
  5.2 4.6 %copy-start.5 = (s32[1,2,8]{2,1,0:T(2,128)S(1)}, s32[1,2,8]{2,1,0:T(2,128)}, u32[]{:S(2)}) copy-start(s32[1,2,8]{2,1,0:T(2,128)} %refs_0_.1) | copy-start | bytes 196
  9.7 12.6 %collective-permute-start.5 = (s32[4,2,8]{2,1,0:T(2,128)S(1)}, s32[4,2,8]{2,1,0:T(2,128)S(1)}, u32[]{:S(2)}, u32[]{:S(2)}) collective-permute-start(s32[4,2,8]{2,1,0:T(2,128)S(1)} %gather.1.refs_0_), channel_id=1, source_target_pairs={{0,192},{8,200},{16,208},{24,216},{32,224},{40,232},{48,240},{56,2... | collective-permute-start | bytes 776 | tf_op jit(solution)/shard_map/ppermute | solution.py:355
  10.3 12.1 %collective-permute-start.4 = (s32[4,2,8]{2,1,0:T(2,128)S(1)}, s32[4,2,8]{2,1,0:T(2,128)S(1)}, u32[]{:S(2)}, u32[]{:S(2)}) collective-permute-start(s32[4,2,8]{2,1,0:T(2,128)S(1)} %gather.1.refs_0_), channel_id=1, source_target_pairs={{0,128},{8,136},{16,144},{24,152},{32,160},{40,168},{48,176},{56,1... | collective-permute-start | bytes 776 | tf_op jit(solution)/shard_map/ppermute | solution.py:355
  13.0 9.3 %collective-permute-start.3 = (s32[4,2,8]{2,1,0:T(2,128)S(1)}, s32[4,2,8]{2,1,0:T(2,128)S(1)}, u32[]{:S(2)}, u32[]{:S(2)}) collective-permute-start(s32[4,2,8]{2,1,0:T(2,128)S(1)} %gather.1.refs_0_), channel_id=1, source_target_pairs={{0,64},{8,72},{16,80},{24,88},{32,96},{40,104},{48,112},{56,120},{... | collective-permute-start | bytes 776 | tf_op jit(solution)/shard_map/ppermute | solution.py:355
  13.8 17.5 %all-to-all-start = ((bf16[8,16,512]{2,1,0:T(8,128)(2,1)}), bf16[8,16,512]{2,1,0:T(8,128)(2,1)S(1)}, u32[]{:S(2)}, u32[]{:S(2)}) async-start(bf16[8,16,512]{2,1,0:T(8,128)(2,1)} %get-tuple-element.15), calls=%async_computation | async-start | bytes 262144 | tf_op jit(solution)/shard_map/all_to_all | solution.py:357
  22.3 5.3 %copy-start.8 = (bf16[512]{0:T(512)(128)(2,1)S(1)}, bf16[512]{0:T(512)(128)(2,1)}, u32[]{:S(2)}) copy-start(bf16[512]{0:T(512)(128)(2,1)} %param.23) | copy-start | bytes 3076
  22.3 9.1 %copy-start.6 = (bf16[8,2,512]{2,1,0:T(2,128)(2,1)S(1)}, bf16[8,2,512]{2,1,0:T(2,128)(2,1)}, u32[]{:S(2)}) copy-start(bf16[8,2,512]{2,1,0:T(2,128)(2,1)} %residual_ref.1) | copy-start | bytes 49156
  23.4 13.6 %copy-start.7 = (bf16[1024]{0:T(1024)(128)(2,1)S(1)}, bf16[1024]{0:T(1024)(128)(2,1)}, u32[]{:S(2)}) copy-start(bf16[1024]{0:T(1024)(128)(2,1)} %param.27) | copy-start | bytes 6148
  23.4 13.6 %collective-permute-start.7 = (bf16[4,16,1024]{2,1,0:T(8,128)(2,1)S(1)}, bf16[4,16,1024]{2,1,0:T(8,128)(2,1)S(1)}, u32[]{:S(2)}, u32[]{:S(2)}) collective-permute-start(bf16[4,16,1024]{2,1,0:T(8,128)(2,1)S(1)} %get-tuple-element.21), channel_id=1, source_target_pairs={{0,128},{8,136},{16,144},{24,152},{32,160},{40,168},{48,176},{56,1... | collective-permute-start | bytes 393224 | tf_op jit(solution)/shard_map/ppermute | solution.py:376
  24.0 13.0 %collective-permute-start.8 = (bf16[4,16,1024]{2,1,0:T(8,128)(2,1)S(1)}, bf16[4,16,1024]{2,1,0:T(8,128)(2,1)S(1)}, u32[]{:S(2)}, u32[]{:S(2)}) collective-permute-start(bf16[4,16,1024]{2,1,0:T(8,128)(2,1)S(1)} %get-tuple-element.22), channel_id=1, source_target_pairs={{0,64},{8,72},{16,80},{24,88},{32,96},{40,104},{48,112},{56,120},{... | collective-permute-start | bytes 393224 | tf_op jit(solution)/shard_map/ppermute | solution.py:376
  26.1 10.9 %collective-permute-start.9 = (bf16[4,16,1024]{2,1,0:T(8,128)(2,1)S(1)}, bf16[4,16,1024]{2,1,0:T(8,128)(2,1)S(1)}, u32[]{:S(2)}, u32[]{:S(2)}) collective-permute-start(bf16[4,16,1024]{2,1,0:T(8,128)(2,1)S(1)} %get-tuple-element.23), channel_id=1, source_target_pairs={{0,192},{8,200},{16,208},{24,216},{32,224},{40,232},{48,240},{56,2... | collective-permute-start | bytes 393224 | tf_op jit(solution)/shard_map/ppermute | solution.py:376
  33.5 11.9 %all-to-all-start.1 = ((f32[8,2,1152]{2,1,0:T(2,128)}), f32[8,2,1152]{2,1,0:T(2,128)S(1)}, u32[]{:S(2)}, u32[]{:S(2)}) async-start(f32[8,2,1152]{2,1,0:T(2,128)} %get-tuple-element.19), calls=%async_computation.1 | async-start | bytes 147456 | tf_op jit(solution)/shard_map/all_to_all | solution.py:410
  37.0 8.4 %collective-permute-start.10 = (bf16[16,1024]{1,0:T(8,128)(2,1)S(1)}, bf16[16,1024]{1,0:T(8,128)(2,1)S(1)}, u32[]{:S(2)}, u32[]{:S(2)}) collective-permute-start(bf16[16,1024]{1,0:T(8,128)(2,1)S(1)} %get-tuple-element.25), channel_id=1, source_target_pairs={{0,32},{8,40},{16,48},{24,56},{32,0},{40,8},{48,16},{56,24},{64,96... | collective-permute-start | bytes 98312 | tf_op jit(solution)/shard_map/ppermute | solution.py:391
  38.8 6.6 %collective-permute-start.11 = (bf16[16,1024]{1,0:T(8,128)(2,1)S(1)}, bf16[16,1024]{1,0:T(8,128)(2,1)S(1)}, u32[]{:S(2)}, u32[]{:S(2)}) collective-permute-start(bf16[16,1024]{1,0:T(8,128)(2,1)S(1)} %get-tuple-element.26), channel_id=1, source_target_pairs={{0,16},{8,24},{16,0},{24,8},{32,48},{40,56},{48,32},{56,40},{64,80... | collective-permute-start | bytes 98312 | tf_op jit(solution)/shard_map/ppermute | solution.py:391
  39.5 5.9 %collective-permute-start.12 = (bf16[16,1024]{1,0:T(8,128)(2,1)S(1)}, bf16[16,1024]{1,0:T(8,128)(2,1)S(1)}, u32[]{:S(2)}, u32[]{:S(2)}) collective-permute-start(bf16[16,1024]{1,0:T(8,128)(2,1)S(1)} %get-tuple-element.27), channel_id=1, source_target_pairs={{0,48},{8,56},{16,32},{24,40},{32,16},{40,24},{48,0},{56,8},{64,11... | collective-permute-start | bytes 98312 | tf_op jit(solution)/shard_map/ppermute | solution.py:391

commit v4 on v3

--- a/solution.py
+++ b/solution.py
@@ -18,6 +18,7 @@
 CORES = 2
 SIDE = 4
 STEPS = (2, 1, 3)
+LATE = 256
 EXTRA = 128
 MIB = 2**20
 LIMIT = 16
@@ -37,8 +38,8 @@
     return lax.broadcasted_iota(jnp.int32, shape, axis)
 
 
-def warm_kernel(out_ref):
-    out_ref[...] = jnp.zeros_like(out_ref)
+def warm_kernel(*refs):
+    refs[-1][...] = jnp.zeros_like(refs[-1])
 
 
 def attend_kernel(
@@ -46,12 +47,18 @@
     lengths_buf, v_buf, small, sent_buf, sems
 ):
     get_lengths = pltpu.make_async_copy(lengths_hbm, lengths_buf, sems.at[0])
-    get_values = pltpu.make_async_copy(v_hbm, v_buf, sems.at[1])
-    get_own = pltpu.make_async_copy(own_hbm, own_ref, sems.at[2])
+    dialogues = q_ref.shape[0]
+    half = dialogues // 2
+    get_values = [
+        pltpu.make_async_copy(
+            v_hbm.at[pl.ds(i * half, half)], v_buf.at[pl.ds(i * half, half)], sems.at[1 + i]
+        )
+        for i in range(2)
+    ]
+    get_own = pltpu.make_async_copy(own_hbm, own_ref, sems.at[3])
     get_lengths.start()
-    get_values.start()
-    get_own.start()
-    dialogues = q_ref.shape[0]
+    get_values[0].start()
+    get_values[1].start()
     width = q_ref.shape[2]
     rows = dialogues * FRAMES
     heads = width // HD
@@ -69,12 +76,12 @@
     ).astype(jnp.bfloat16)
     scale = 1.0 / math.sqrt(HD)
 
-    row = iota((stacked, slots), 0)
     slot = iota((stacked, slots), 1)
-    dialogue = (row % rows) // FRAMES
+    dialogue = (iota((stacked, slots), 0) % rows) // FRAMES
+    of_dialogue = [dialogue == d for d in range(dialogues)]
     scores = jnp.zeros((stacked, slots), jnp.float32)
     for d in range(dialogues):
-        scores = jnp.where(dialogue == d, dot_nt(spread, k_ref[d]), scores)
+        scores = jnp.where(of_dialogue[d], dot_nt(spread, k_ref[d]), scores)
     row_n = iota((stacked, rows), 0) % rows
     col_n = iota((stacked, rows), 1)
     seen = (row_n // FRAMES == col_n // FRAMES) & (col_n <= row_n)
@@ -82,7 +89,7 @@
     get_lengths.wait()
     live = jnp.zeros((stacked, slots), jnp.int32)
     for d in range(dialogues):
-        live = jnp.where(dialogue == d, lengths_buf[d], live)
+        live = jnp.where(of_dialogue[d], lengths_buf[d], live)
     scores = jnp.where(slot < live, scores * scale, -jnp.inf)
     largest = jnp.maximum(
         jnp.max(scores, axis=-1, keepdims=True), jnp.max(fresh, axis=-1, keepdims=True)
@@ -92,13 +99,14 @@
     total = jnp.sum(exp_cache, axis=-1, keepdims=True) + jnp.sum(
         exp_fresh, axis=-1, keepdims=True
     )
-    prob_cache = exp_cache / total
-    prob_fresh = (exp_fresh / total).astype(jnp.bfloat16)
-    mixed = dot_nn(prob_fresh, fresh_value)
-    get_values.wait()
-    for d in range(dialogues):
-        own = jnp.where(dialogue == d, prob_cache, 0.0).astype(jnp.bfloat16)
+    mixed = dot_nn(exp_fresh.astype(jnp.bfloat16), fresh_value)
+    for d in range(dialogues):
+        if d % half == 0:
+            get_values[d // half].wait()
+        own = jnp.where(of_dialogue[d], exp_cache, 0.0).astype(jnp.bfloat16)
         mixed = mixed + dot_nn(own, v_buf[d])
+    get_own.start()
+    mixed = mixed / total
     attended = mixed[:rows]
     for h in range(1, heads):
         attended = jnp.where(head_of == h, mixed[h * rows : (h + 1) * rows], attended)
@@ -109,7 +117,7 @@
         sent_buf[t] = dot_nn(attended, w_ref[:, t * features : (t + 1) * features]).astype(
             jnp.bfloat16
         )
-        sends.append(pltpu.make_async_copy(sent_buf.at[t], out_hbm.at[t], sems.at[3 + t]))
+        sends.append(pltpu.make_async_copy(sent_buf.at[t], out_hbm.at[t], sems.at[4 + t]))
         sends[t].start()
     get_own.wait()
     for send in sends:
@@ -124,7 +132,7 @@
 
 def lookup_kernel(*refs):
     ids_refs, (own_ref, other_ref) = refs[:SIDE], refs[SIDE : SIDE + 2]
-    out_refs, (done_ref, found_buf) = refs[SIDE + 2 : 2 * SIDE + 2], refs[2 * SIDE + 2 :]
+    out_refs, found_buf = refs[SIDE + 2 : 2 * SIDE + 2], refs[-1]
     span = own_ref.shape[1]
     width = own_ref.shape[2]
     entries = LEVELS * span
@@ -159,7 +167,6 @@
     found_buf[...] = found.astype(jnp.bfloat16).reshape(found_buf.shape)
     for s in range(SIDE):
         out_refs[s][...] = found_buf[s * SIDE : (s + 1) * SIDE]
-    done_ref[...] = jnp.zeros_like(done_ref)
 
 
 def collect_kernel(own_ref, *refs):
@@ -171,18 +178,27 @@
         out_refs[s][...] = value
 
 
-def fetch_kernel(w_hbm, order_ref, out_ref, sem):
-    copy = pltpu.make_async_copy(w_hbm, out_ref, sem)
-    copy.start()
-    copy.wait()
+def fetch_kernel(qkv_hbm, o_hbm, order_ref, out_ref, sems):
+    near = qkv_hbm.shape[1] - LATE
+    copies = [
+        pltpu.make_async_copy(qkv_hbm.at[:, pl.ds(0, near)], out_ref.at[:, pl.ds(0, near)], sems.at[0])
+    ]
+    for j in range(o_hbm.shape[1] // LATE):
+        part = pl.ds(j * LATE, LATE)
+        copies.append(
+            pltpu.make_async_copy(
+                o_hbm.at[pl.ds(0, LATE), part], out_ref.at[part, pl.ds(near, LATE)], sems.at[1 + j]
+            )
+        )
+    for copy in copies:
+        copy.start()
+    for copy in copies:
+        copy.wait()
 
 
 def middle_kernel(
-    shares_ref, residual_ref, gain_ref, w_hbm, order_ref, stream_ref, sent_ref,
-    w_ref, rows_buf, sent_buf, sem
+    shares_ref, residual_ref, gain_ref, w_ref, order_ref, stream_ref, sent_ref, rows_buf, sent_buf
 ):
-    get_weight = pltpu.make_async_copy(w_hbm, w_ref, sem)
-    get_weight.start()
     dialogues = residual_ref.shape[0]
     for d in range(dialogues):
         rows_buf[FRAMES * d : FRAMES * (d + 1), :] = residual_ref[d].astype(jnp.float32)
@@ -198,7 +214,6 @@
     sent_buf[:, width:] = jnp.broadcast_to(squares, (hidden.shape[0], EXTRA))
     for d in range(dialogues):
         stream_ref[d] = rows_buf[FRAMES * d : FRAMES * (d + 1), :].astype(jnp.bfloat16)
-    get_weight.wait()
     sent_buf[:, :width] = dot_nn(scaled, w_ref[...])
     for d in range(dialogues):
         sent_ref[d] = sent_buf[FRAMES * d : FRAMES * (d + 1), :]
@@ -208,9 +223,15 @@
     terms_ref, *refs
 ):
     table_refs = refs[:SIDE]
-    gain_ref, qkv_ref, o_hbm, out_ref, o_ref, sem = refs[SIDE:]
-    get_weight = pltpu.make_async_copy(o_hbm, o_ref, sem)
-    get_weight.start()
+    gain_ref, near_ref, qkv_hbm, o_hbm, out_ref, v_buf, o_buf, sems = refs[SIDE:]
+    heads_width = DHEADS * DHD
+    near = 3 * heads_width - LATE
+    get_v = pltpu.make_async_copy(qkv_hbm.at[:, pl.ds(near, LATE)], v_buf, sems.at[0])
+    get_o = pltpu.make_async_copy(
+        o_hbm.at[pl.ds(heads_width - LATE, LATE)], o_buf, sems.at[1]
+    )
+    get_v.start()
+    get_o.start()
     count, width = table_refs[0].shape
     terms = terms_ref[0]
     for t in range(1, terms_ref.shape[0]):
@@ -224,10 +245,9 @@
     depth_input = values + jnp.where(frame == 0, proj[0:1], proj[1:2])
     mean = jnp.sum(depth_input * depth_input, axis=-1, keepdims=True) / width
     normed = (depth_input * lax.rsqrt(mean + 1e-05) * gain_ref[...]).astype(jnp.bfloat16)
-    heads_width = DHEADS * DHD
-    query = dot_nn(normed, qkv_ref[:, :heads_width]).astype(jnp.bfloat16).astype(jnp.float32)
-    key = dot_nn(normed, qkv_ref[:, heads_width : 2 * heads_width]).astype(jnp.bfloat16)
-    value = dot_nn(normed, qkv_ref[:, 2 * heads_width :]).astype(jnp.bfloat16)
+    query = dot_nn(normed, near_ref[:, :heads_width]).astype(jnp.bfloat16).astype(jnp.float32)
+    key = dot_nn(normed, near_ref[:, heads_width : 2 * heads_width]).astype(jnp.bfloat16)
+    value = dot_nn(normed, near_ref[:, 2 * heads_width : near]).astype(jnp.bfloat16)
     head_of = iota((count, heads_width), 1) // DHD
     spread = jnp.concatenate(
         [jnp.where(head_of == h, query, 0.0) for h in range(DHEADS)], axis=0
@@ -238,14 +258,23 @@
     seen = (row // LEVELS == col // LEVELS) & (col <= row)
     exps = jnp.where(seen, jnp.exp(scores), 0.0)
     probs = (exps / jnp.sum(exps, axis=-1, keepdims=True)).astype(jnp.bfloat16)
-    spread_out = dot_nn(probs, value)
+    get_v.wait()
+    late_value = dot_nn(normed, v_buf[...]).astype(jnp.bfloat16)
+    spread_out = dot_nn(probs, jnp.concatenate([value, late_value], axis=1))
     mixed = spread_out[:count]
     for h in range(1, DHEADS):
         mixed = jnp.where(head_of == h, spread_out[h * count : (h + 1) * count], mixed)
-    get_weight.wait()
-    out_ref[...] = (depth_input + dot_nn(mixed.astype(jnp.bfloat16), o_ref[...])).astype(
-        jnp.bfloat16
-    )
+    mixed = mixed.astype(jnp.bfloat16)
+    early = jnp.concatenate(
+        [
+            dot_nn(mixed[:, :LATE], near_ref[j * LATE : (j + 1) * LATE, near:])
+            for j in range(width // LATE)
+        ],
+        axis=1,
+    )
+    get_o.wait()
+    late = dot_nn(mixed[:, LATE:], o_buf[...])
+    out_ref[...] = (depth_input + early + late).astype(jnp.bfloat16)
 
 
 VMEM = pl.BlockSpec(memory_space=pltpu.VMEM)
@@ -306,10 +335,10 @@
     members = batch_size // CORES
     count = FRAMES * LEVELS
 
-    other_tables = lax.ppermute(level_tables, "batch", flipped(batch_size, 1, 1))
     order = call(
         warm_kernel, "warm", pltpu.VMEM((8, 128), f32), [], VMEM, [], LIMIT, WARM_FLOPS, 1
     )()
+    other_tables = lax.ppermute(level_tables, "batch", flipped(batch_size, 1, 1))
     near = [lax.ppermute(tokens, "batch", flipped(batch_size, CORES, s)) for s in STEPS]
     head_terms, own_tables = call(
         attend_kernel,
@@ -325,7 +354,7 @@
             pltpu.VMEM(cache_values.shape, bf16),
             pltpu.VMEM((3, rows, new_queries.shape[2]), f32),
             pltpu.VMEM((tensor_size, rows, features), bf16),
-            pltpu.SemaphoreType.DMA((3 + tensor_size,)),
+            pltpu.SemaphoreType.DMA((4 + tensor_size,)),
         ],
         LIMIT,
         10**8,
@@ -356,15 +385,12 @@
 
     shares = lax.all_to_all(head_terms, "tensor", 0, 0, tiled=True)
 
-    *partial_rows, looked = call(
+    partial_rows = call(
         lookup_kernel,
         "lookup",
-        (
-            *[pltpu.VMEM((SIDE, count, width), bf16)] * SIDE,
-            pltpu.VMEM((8, 128), f32),
-        ),
+        [pltpu.VMEM((SIDE, count, width), bf16)] * SIDE,
         [VMEM] * (SIDE + 2),
-        (VMEM,) * (SIDE + 1),
+        [VMEM] * SIDE,
         [
             pltpu.VMEM((members, count, width), bf16),
         ],
@@ -372,6 +398,10 @@
         10**11,
         1,
     )(column, *sorted_steps(ids), own_tables, other_tables)
+    looked = call(
+        warm_kernel, "warm_in", pltpu.VMEM((8, 128), f32), [VMEM], VMEM, [], LIMIT, WARM_FLOPS, 1
+    )(partial_rows[0])
+    *partial_rows, looked = lax.optimization_barrier((*partial_rows, looked))
     across = [
         lax.ppermute(partial_rows[s], "batch", flipped(batch_size, CORES * SIDE, s))
         for s in STEPS
@@ -395,42 +425,44 @@
         middle_kernel,
         "middle",
         (pltpu.HBM(residual.shape, bf16), pltpu.HBM((held, FRAMES, width + EXTRA), f32)),
-        [VMEM] * 3 + [ANY, VMEM],
+        [VMEM] * 5,
         (VMEM, VMEM),
         [
-            pltpu.VMEM(in_weight.shape, bf16),
             pltpu.VMEM((rows, features), f32),
             pltpu.VMEM((rows, width + EXTRA), f32),
-            pltpu.SemaphoreType.DMA,
         ],
         LIMIT,
         10**9,
         1,
-    )(shares, residual, temporal_gain.astype(f32).reshape(1, features), *hbm(in_weight), looked)
+    )(shares, residual, temporal_gain.astype(f32).reshape(1, features), in_weight, looked)
     terms = lax.all_to_all(sent, "tensor", 0, 0, tiled=True)
 
-    qkv_near = call(
+    near_weights = call(
         fetch_kernel,
         "fetch",
         pltpu.VMEM(depth_qkv.shape, bf16),
-        [ANY, VMEM],
+        [ANY, ANY, VMEM],
         VMEM,
-        [pltpu.SemaphoreType.DMA],
+        [pltpu.SemaphoreType.DMA((1 + width // LATE,))],
         LIMIT,
         10**9,
         1,
-    )(*hbm(depth_qkv), own_rows)
+    )(*hbm(depth_qkv, depth_out), own_rows)
     states = call(
         depth_kernel,
         "depth",
         pltpu.HBM((count, width), bf16),
-        [VMEM] * (SIDE + 3) + [ANY],
+        [VMEM] * (SIDE + 3) + [ANY, ANY],
         VMEM,
-        [pltpu.VMEM(depth_out.shape, bf16), pltpu.SemaphoreType.DMA],
+        [
+            pltpu.VMEM((width, LATE), bf16),
+            pltpu.VMEM((LATE, width), bf16),
+            pltpu.SemaphoreType.DMA((2,)),
+        ],
         LIMIT,
         10**9,
         1,
-    )(terms, own_rows, *along, depth_gain.astype(f32).reshape(1, width), qkv_near, *hbm(depth_out))
+    )(terms, own_rows, *along, depth_gain.astype(f32).reshape(1, width), near_weights, *hbm(depth_qkv, depth_out))
     return (temporal_out, states.reshape(1, FRAMES, LEVELS, width))
 
 

time: 48.4 us -> 46.9 us (0.969)
  Pallas kernels: 10.8 us -> 9.09 us
    pallas_call x1, Pallas kernels: 2.13 us -> 0.9 us  [per_device(): call(middle_kernel, 'middle', (pltpu.HBM(residual.shape, bf16), pltpu.HBM...]
    pallas_call x2 -> x3, Pallas kernels: 2.89 us -> 2.85 us  [the longest x1 1.86 us: per_device(): call(fetch_kernel, 'fetch', pltpu.VMEM(depth_qkv.shape, bf16), [ANY, ANY,...]
  transfers between devices with their start and end apart: 15 -> 15, of which waited for: 3 -> 3; matrix products, arithmetic and copies ran while one was open for 0% -> 0% of each run, Pallas kernels for 17% -> 14%
where the time goes in v4:
time: 46.9 us; the launch traced here: 46.6 us
  starting transfers between devices  28.8 us (61%)
  Pallas kernels  9.09 us (19%)
  waiting for transfers between devices  7.76 us (17%)
  between operations  0.87 us (2%)
    all_to_all x1, starting transfers between devices, per_device(): shares = lax.all_to_all(head_terms, 'tensor', 0, 0, tiled=True)  8.47 us
    ppermute x3, starting transfers between devices, per_device(): lax.ppermute(tokens, 'batch', flipped(batch_size, CORES, s))  4.34 us
    ppermute x3, starting transfers between devices, per_device(): lax.ppermute(side_rows[s - 1], 'batch', flipped(batch_size, CORES, s))  4.18 us
    ppermute x3, starting transfers between devices, per_device(): lax.ppermute(partial_rows[s], 'batch', flipped(batch_size, CORES * SIDE, s))  4.18 us
    ppermute x3, starting transfers between devices, per_device(): lax.ppermute(column, 'batch', flipped(batch_size, CORES * SIDE, s))  4.09 us
    all_to_all x1, waiting for transfers between devices, per_device(): shares = lax.all_to_all(head_terms, 'tensor', 0, 0, tiled=True)  3.8 us
    all_to_all x1, starting transfers between devices, per_device(): terms = lax.all_to_all(sent, 'tensor', 0, 0, tiled=True)  3.42 us
    pallas_call x1, Pallas kernels, per_device(): call(attend_kernel, 'attend', (pltpu.HBM((tensor_size, rows, features), b...  2.94 us
  transfers between devices with their start and end apart: 15, of which 3 were waited for; matrix products, arithmetic and copies ran while one was open for 0% of the time, Pallas kernels for 14%

profile of v4, /device:TPU:4, one launch (start us, length us, event | category | flops | bytes accessed | tf_op | source)
XLA Modules:
  0.0 46.6 jit_solution(10918500686438712763)
XLA Ops:
  0.6 0.0 copy-start
  0.6 0.0 copy-start.1
  0.7 0.0 copy-start.4
  0.7 0.0 copy-start.3
  0.7 0.0 copy-start.2
  0.7 0.1 collective-permute-start.6
  0.8 3.3 %collective-permute-start.1 = (s32[1,2,8]{2,1,0:T(2,128)}, s32[1,2,8]{2,1,0:T(2,128)S(1)}, u32[]{:S(2)}, u32[]{:S(2)}) collective-permute-start(s32[1,2,8]{2,1,0:T(2,128)} %refs_0_.1), channel_id=1, source_target_pairs={{0,32},{8,40},{16,48},{24,56},{32,0},{40,8},{48,16},{56,24},{64,96... | collective-permute-start | bytes 200 | tf_op jit(solution)/shard_map/ppermute | solution.py:342
  4.1 0.7 %collective-permute-start = (s32[1,2,8]{2,1,0:T(2,128)}, s32[1,2,8]{2,1,0:T(2,128)S(1)}, u32[]{:S(2)}, u32[]{:S(2)}) collective-permute-start(s32[1,2,8]{2,1,0:T(2,128)} %refs_0_.1), channel_id=1, source_target_pairs={{0,16},{8,24},{16,0},{24,8},{32,48},{40,56},{48,32},{56,40},{64,80... | collective-permute-start | bytes 200 | tf_op jit(solution)/shard_map/ppermute | solution.py:342
  4.7 0.4 collective-permute-start.2
  5.1 0.0 copy-done
  5.1 0.0 copy-done.1
  5.1 0.0 copy-done.4
  5.1 0.0 copy-done.3
  5.1 0.0 copy-done.2
  5.2 0.0 copy-start.5
  5.2 2.9 %attend.1 = (bf16[8,16,512]{2,1,0:T(8,128)(2,1)}, bf16[8,64,1024]{2,1,0:T(8,128)(2,1)S(1)}) custom-call(s32[8]{0:T(128)} %lengths_hbm.1, bf16[8,2,256]{2,1,0:T(2,128)(2,1)S(1)} %copy-done.2, bf16[8,2,256]{2,1,0:T(2,128)(2,1)S(1)} %copy-done.3, bf16[8,2,256]{2,1,0:T(2,128)(2,1)S(1)} %copy-done.4, bf16[8,256,256]{2,1,0:T(8,128)(2,1)S(1)} %copy-done.1, ...), custom_call_target="tpu_custom_call" | custom-call | flops 100000000 | bytes 4194304 | tf_op jit(solution)/shard_map/attend/pallas_call | solution.py:343
  8.1 0.0 collective-permute-done.1.refs_2_
  8.1 0.0 collective-permute-done.refs_1_
  8.1 1.6 %collective-permute-done.2.refs_3_ = s32[1,2,8]{2,1,0:T(2,128)S(1)} collective-permute-done((s32[1,2,8]{2,1,0:T(2,128)}, s32[1,2,8]{2,1,0:T(2,128)S(1)}, u32[]{:S(2)}, u32[]{:S(2)}) %collective-permute-start.2) | collective-permute-done | bytes 96 | tf_op jit(solution)/shard_map/ppermute | solution.py:342
  9.7 0.0 copy-done.5
  9.7 0.5 %collective-permute-start.5 = (s32[4,2,8]{2,1,0:T(2,128)S(1)}, s32[4,2,8]{2,1,0:T(2,128)S(1)}, u32[]{:S(2)}, u32[]{:S(2)}) collective-permute-start(s32[4,2,8]{2,1,0:T(2,128)S(1)} %gather.1.refs_0_), channel_id=1, source_target_pairs={{0,192},{8,200},{16,208},{24,216},{32,224},{40,232},{48,240},{56,2... | collective-permute-start | bytes 776 | tf_op jit(solution)/shard_map/ppermute | solution.py:384
  10.3 2.7 %collective-permute-start.4 = (s32[4,2,8]{2,1,0:T(2,128)S(1)}, s32[4,2,8]{2,1,0:T(2,128)S(1)}, u32[]{:S(2)}, u32[]{:S(2)}) collective-permute-start(s32[4,2,8]{2,1,0:T(2,128)S(1)} %gather.1.refs_0_), channel_id=1, source_target_pairs={{0,128},{8,136},{16,144},{24,152},{32,160},{40,168},{48,176},{56,1... | collective-permute-start | bytes 776 | tf_op jit(solution)/shard_map/ppermute | solution.py:384
  13.0 0.8 %collective-permute-start.3 = (s32[4,2,8]{2,1,0:T(2,128)S(1)}, s32[4,2,8]{2,1,0:T(2,128)S(1)}, u32[]{:S(2)}, u32[]{:S(2)}) collective-permute-start(s32[4,2,8]{2,1,0:T(2,128)S(1)} %gather.1.refs_0_), channel_id=1, source_target_pairs={{0,64},{8,72},{16,80},{24,88},{32,96},{40,104},{48,112},{56,120},{... | collective-permute-start | bytes 776 | tf_op jit(solution)/shard_map/ppermute | solution.py:384
  13.8 8.5 %all-to-all-start = ((bf16[8,16,512]{2,1,0:T(8,128)(2,1)}), bf16[8,16,512]{2,1,0:T(8,128)(2,1)S(1)}, u32[]{:S(2)}, u32[]{:S(2)}) async-start(bf16[8,16,512]{2,1,0:T(8,128)(2,1)} %get-tuple-element.19), calls=%async_computation | async-start | bytes 262144 | tf_op jit(solution)/shard_map/all_to_all | solution.py:386
  22.3 0.0 collective-permute-done.5.refs_3_
  22.3 0.0 collective-permute-done.4.refs_2_
  22.3 0.0 collective-permute-done.3.refs_1_
  22.3 0.0 collective-permute-done.6.refs_5_
  22.3 1.0 %lookup.1 = (bf16[4,16,1024]{2,1,0:T(8,128)(2,1)S(1)}, bf16[4,16,1024]{2,1,0:T(8,128)(2,1)S(1)}, bf16[4,16,1024]{2,1,0:T(8,128)(2,1)S(1)}, bf16[4,16,1024]{2,1,0:T(8,128)(2,1)S(1)}) custom-call(s32[4,2,8]{2,1,0:T(2,128)S(1)} %gather.1.refs_0_, s32[4,2,8]{2,1,0:T(2,128)S(1)} %collective-permute-done.3.refs_1_, s32[4,2,8]{2,1,0:T(2,128)S(1)} %collective-permute-done.4.refs_2_, ...), custom_call_target="tpu_custom_call" | custom-call | flops 99999997952 | bytes 1 | tf_op jit(solution)/shard_map/lookup/pallas_call | solution.py:388
  23.3 0.0 copy-start.9
  23.4 0.0 copy-start.6
  23.4 0.0 copy-start.7
  23.4 0.0 copy-start.8
  23.4 0.6 %collective-permute-start.7 = (bf16[4,16,1024]{2,1,0:T(8,128)(2,1)S(1)}, bf16[4,16,1024]{2,1,0:T(8,128)(2,1)S(1)}, u32[]{:S(2)}, u32[]{:S(2)}) collective-permute-start(bf16[4,16,1024]{2,1,0:T(8,128)(2,1)S(1)} %get-tuple-element.29), channel_id=1, source_target_pairs={{0,128},{8,136},{16,144},{24,152},{32,160},{40,168},{48,176},{56,1... | collective-permute-start | bytes 393224 | tf_op jit(solution)/shard_map/ppermute | solution.py:406
  24.0 2.1 %collective-permute-start.8 = (bf16[4,16,1024]{2,1,0:T(8,128)(2,1)S(1)}, bf16[4,16,1024]{2,1,0:T(8,128)(2,1)S(1)}, u32[]{:S(2)}, u32[]{:S(2)}) collective-permute-start(bf16[4,16,1024]{2,1,0:T(8,128)(2,1)S(1)} %get-tuple-element.30), channel_id=1, source_target_pairs={{0,64},{8,72},{16,80},{24,88},{32,96},{40,104},{48,112},{56,120},{... | collective-permute-start | bytes 393224 | tf_op jit(solution)/shard_map/ppermute | solution.py:406
  26.1 1.5 %collective-permute-start.9 = (bf16[4,16,1024]{2,1,0:T(8,128)(2,1)S(1)}, bf16[4,16,1024]{2,1,0:T(8,128)(2,1)S(1)}, u32[]{:S(2)}, u32[]{:S(2)}) collective-permute-start(bf16[4,16,1024]{2,1,0:T(8,128)(2,1)S(1)} %get-tuple-element.31), channel_id=1, source_target_pairs={{0,192},{8,200},{16,208},{24,216},{32,224},{40,232},{48,240},{56,2... | collective-permute-start | bytes 393224 | tf_op jit(solution)/shard_map/ppermute | solution.py:406
  27.6 0.0 copy-done.9
  27.6 3.8 %all-to-all-done.shares_ref = bf16[8,16,512]{2,1,0:T(8,128)(2,1)S(1)} async-done(((bf16[8,16,512]{2,1,0:T(8,128)(2,1)}), bf16[8,16,512]{2,1,0:T(8,128)(2,1)S(1)}, u32[]{:S(2)}, u32[]{:S(2)}) %all-to-all-start) | async-done | bytes 131104 | tf_op jit(solution)/shard_map/all_to_all | solution.py:386
  31.4 0.0 copy-done.6
  31.4 0.0 copy-done.7
  31.4 0.9 %middle.1 = (bf16[8,2,512]{2,1,0:T(2,128)(2,1)}, f32[8,2,1152]{2,1,0:T(2,128)}) custom-call(bf16[8,16,512]{2,1,0:T(8,128)(2,1)S(1)} %all-to-all-done.shares_ref, bf16[8,2,512]{2,1,0:T(2,128)(2,1)S(1)} %copy-done.7, f32[1,512]{1,0:T(1,128)S(1)} %bitcast.4, bf16[512,1024]{1,0:T(8,128)(2,1)S(1)} %copy-done.6, f32[8,128]{1,0:T(8,128)S(1)} %warm_in.1.order_ref), custom_call_target="tpu_custom_call" | custom-call | flops 1000000000 | bytes 1 | tf_op jit(solution)/shard_map/middle/pallas_call | solution.py:424
  32.3 3.4 %all-to-all-start.1 = ((f32[8,2,1152]{2,1,0:T(2,128)}), f32[8,2,1152]{2,1,0:T(2,128)S(1)}, u32[]{:S(2)}, u32[]{:S(2)}) async-start(f32[8,2,1152]{2,1,0:T(2,128)} %get-tuple-element.27), calls=%async_computation.1 | async-start | bytes 147456 | tf_op jit(solution)/shard_map/all_to_all | solution.py:438
  35.7 0.0 copy-done.8
  35.7 0.0 collective-permute-done.7.refs_0_
  35.7 0.0 collective-permute-done.8.refs_1_
  35.7 0.0 collective-permute-done.9.refs_2_
  35.8 1.6 %collective-permute-start.10 = (bf16[16,1024]{1,0:T(8,128)(2,1)S(1)}, bf16[16,1024]{1,0:T(8,128)(2,1)S(1)}, u32[]{:S(2)}, u32[]{:S(2)}) collective-permute-start(bf16[16,1024]{1,0:T(8,128)(2,1)S(1)} %get-tuple-element.33), channel_id=1, source_target_pairs={{0,32},{8,40},{16,48},{24,56},{32,0},{40,8},{48,16},{56,24},{64,96... | collective-permute-start | bytes 98312 | tf_op jit(solution)/shard_map/ppermute | solution.py:421
  37.4 0.7 %collective-permute-start.11 = (bf16[16,1024]{1,0:T(8,128)(2,1)S(1)}, bf16[16,1024]{1,0:T(8,128)(2,1)S(1)}, u32[]{:S(2)}, u32[]{:S(2)}) collective-permute-start(bf16[16,1024]{1,0:T(8,128)(2,1)S(1)} %get-tuple-element.34), channel_id=1, source_target_pairs={{0,16},{8,24},{16,0},{24,8},{32,48},{40,56},{48,32},{56,40},{64,80... | collective-permute-start | bytes 98312 | tf_op jit(solution)/shard_map/ppermute | solution.py:421
  38.1 1.9 %collective-permute-start.12 = (bf16[16,1024]{1,0:T(8,128)(2,1)S(1)}, bf16[16,1024]{1,0:T(8,128)(2,1)S(1)}, u32[]{:S(2)}, u32[]{:S(2)}) collective-permute-start(bf16[16,1024]{1,0:T(8,128)(2,1)S(1)} %get-tuple-element.35), channel_id=1, source_target_pairs={{0,48},{8,56},{16,32},{24,40},{32,16},{40,24},{48,0},{56,8},{64,11... | collective-permute-start | bytes 98312 | tf_op jit(solution)/shard_map/ppermute | solution.py:421
  40.0 1.9 %fetch.1.refs_5_ = bf16[1024,1536]{1,0:T(8,128)(2,1)S(1)} custom-call(bf16[1024,1536]{1,0:T(8,128)(2,1)} %refs_6_.1, bf16[512,1024]{1,0:T(8,128)(2,1)} %refs_7_.1, bf16[16,1024]{1,0:T(8,128)(2,1)S(1)} %get-tuple-element.32.order_ref.refs_0_), custom_call_target="tpu_custom_call" | custom-call | flops 1000000000 | bytes 1 | tf_op jit(solution)/shard_map/fetch/pallas_call | solution.py:440
  41.8 2.3 %all-to-all-done.1.terms_ref = f32[8,2,1152]{2,1,0:T(2,128)S(1)} async-done(((f32[8,2,1152]{2,1,0:T(2,128)}), f32[8,2,1152]{2,1,0:T(2,128)S(1)}, u32[]{:S(2)}, u32[]{:S(2)}) %all-to-all-start.1) | async-done | bytes 73760 | tf_op jit(solution)/shard_map/all_to_all | solution.py:438
  44.2 0.0 collective-permute-done.10.refs_1_
  44.2 0.0 collective-permute-done.11.refs_2_
  44.2 0.0 collective-permute-done.12.refs_3_
  44.2 2.4 %depth.1 = bf16[16,1024]{1,0:T(8,128)(2,1)} custom-call(f32[8,2,1152]{2,1,0:T(2,128)S(1)} %all-to-all-done.1.terms_ref, bf16[16,1024]{1,0:T(8,128)(2,1)S(1)} %get-tuple-element.32.order_ref.refs_0_, bf16[16,1024]{1,0:T(8,128)(2,1)S(1)} %collective-permute-done.10.refs_1_, bf16[16,1024]{1,0:T(8,128)(2,1)S(1)} %collective-permute-done.11.refs_2_, ...), custom_call_target="tpu_custom_call" | custom-call | flops 1000000000 | bytes 1 | tf_op jit(solution)/shard_map/depth/pallas_call | solution.py:451
  (6 shorter events, 0.0 us)
Async XLA Ops:
  0.6 4.5 %copy-start = (bf16[256,4096]{1,0:T(8,128)(2,1)S(1)}, bf16[256,4096]{1,0:T(8,128)(2,1)}, u32[]{:S(2)}) copy-start(bf16[256,4096]{1,0:T(8,128)(2,1)} %w_ref.2) | copy-start | bytes 6291460
  0.6 4.5 %copy-start.1 = (bf16[8,256,256]{2,1,0:T(8,128)(2,1)S(1)}, bf16[8,256,256]{2,1,0:T(8,128)(2,1)}, u32[]{:S(2)}) copy-start(bf16[8,256,256]{2,1,0:T(8,128)(2,1)} %k_ref.1) | copy-start | bytes 3145732
  0.7 4.5 %copy-start.4 = (bf16[8,2,256]{2,1,0:T(2,128)(2,1)S(1)}, bf16[8,2,256]{2,1,0:T(2,128)(2,1)}, u32[]{:S(2)}) copy-start(bf16[8,2,256]{2,1,0:T(2,128)(2,1)} %nv_ref.1) | copy-start | bytes 24580
  0.7 4.5 %copy-start.3 = (bf16[8,2,256]{2,1,0:T(2,128)(2,1)S(1)}, bf16[8,2,256]{2,1,0:T(2,128)(2,1)}, u32[]{:S(2)}) copy-start(bf16[8,2,256]{2,1,0:T(2,128)(2,1)} %nk_ref.1) | copy-start | bytes 24580
  0.7 4.5 %copy-start.2 = (bf16[8,2,256]{2,1,0:T(2,128)(2,1)S(1)}, bf16[8,2,256]{2,1,0:T(2,128)(2,1)}, u32[]{:S(2)}) copy-start(bf16[8,2,256]{2,1,0:T(2,128)(2,1)} %q_ref.1) | copy-start | bytes 24580
  0.7 21.7 %collective-permute-start.6 = (bf16[8,64,1024]{2,1,0:T(8,128)(2,1)}, bf16[8,64,1024]{2,1,0:T(8,128)(2,1)S(1)}, u32[]{:S(2)}, u32[]{:S(2)}) collective-permute-start(bf16[8,64,1024]{2,1,0:T(8,128)(2,1)} %own_hbm.1), channel_id=1, source_target_pairs={{0,8},{8,0},{16,24},{24,16},{32,40},{40,32},{48,56},{56,48},{64,72... | collective-permute-start | bytes 3145736 | tf_op jit(solution)/shard_map/ppermute | solution.py:341
  0.8 7.3 %collective-permute-start.1 = (s32[1,2,8]{2,1,0:T(2,128)}, s32[1,2,8]{2,1,0:T(2,128)S(1)}, u32[]{:S(2)}, u32[]{:S(2)}) collective-permute-start(s32[1,2,8]{2,1,0:T(2,128)} %refs_0_.1), channel_id=1, source_target_pairs={{0,32},{8,40},{16,48},{24,56},{32,0},{40,8},{48,16},{56,24},{64,96... | collective-permute-start | bytes 200 | tf_op jit(solution)/shard_map/ppermute | solution.py:342
  4.1 4.1 %collective-permute-start = (s32[1,2,8]{2,1,0:T(2,128)}, s32[1,2,8]{2,1,0:T(2,128)S(1)}, u32[]{:S(2)}, u32[]{:S(2)}) collective-permute-start(s32[1,2,8]{2,1,0:T(2,128)} %refs_0_.1), channel_id=1, source_target_pairs={{0,16},{8,24},{16,0},{24,8},{32,48},{40,56},{48,32},{56,40},{64,80... | collective-permute-start | bytes 200 | tf_op jit(solution)/shard_map/ppermute | solution.py:342
  4.7 5.0 %collective-permute-start.2 = (s32[1,2,8]{2,1,0:T(2,128)}, s32[1,2,8]{2,1,0:T(2,128)S(1)}, u32[]{:S(2)}, u32[]{:S(2)}) collective-permute-start(s32[1,2,8]{2,1,0:T(2,128)} %refs_0_.1), channel_id=1, source_target_pairs={{0,48},{8,56},{16,32},{24,40},{32,16},{40,24},{48,0},{56,8},{64,11... | collective-permute-start | bytes 200 | tf_op jit(solution)/shard_map/ppermute | solution.py:342
  5.2 4.6 %copy-start.5 = (s32[1,2,8]{2,1,0:T(2,128)S(1)}, s32[1,2,8]{2,1,0:T(2,128)}, u32[]{:S(2)}) copy-start(s32[1,2,8]{2,1,0:T(2,128)} %refs_0_.1) | copy-start | bytes 196
  9.7 12.6 %collective-permute-start.5 = (s32[4,2,8]{2,1,0:T(2,128)S(1)}, s32[4,2,8]{2,1,0:T(2,128)S(1)}, u32[]{:S(2)}, u32[]{:S(2)}) collective-permute-start(s32[4,2,8]{2,1,0:T(2,128)S(1)} %gather.1.refs_0_), channel_id=1, source_target_pairs={{0,192},{8,200},{16,208},{24,216},{32,224},{40,232},{48,240},{56,2... | collective-permute-start | bytes 776 | tf_op jit(solution)/shard_map/ppermute | solution.py:384
  10.3 12.0 %collective-permute-start.4 = (s32[4,2,8]{2,1,0:T(2,128)S(1)}, s32[4,2,8]{2,1,0:T(2,128)S(1)}, u32[]{:S(2)}, u32[]{:S(2)}) collective-permute-start(s32[4,2,8]{2,1,0:T(2,128)S(1)} %gather.1.refs_0_), channel_id=1, source_target_pairs={{0,128},{8,136},{16,144},{24,152},{32,160},{40,168},{48,176},{56,1... | collective-permute-start | bytes 776 | tf_op jit(solution)/shard_map/ppermute | solution.py:384
  13.0 9.3 %collective-permute-start.3 = (s32[4,2,8]{2,1,0:T(2,128)S(1)}, s32[4,2,8]{2,1,0:T(2,128)S(1)}, u32[]{:S(2)}, u32[]{:S(2)}) collective-permute-start(s32[4,2,8]{2,1,0:T(2,128)S(1)} %gather.1.refs_0_), channel_id=1, source_target_pairs={{0,64},{8,72},{16,80},{24,88},{32,96},{40,104},{48,112},{56,120},{... | collective-permute-start | bytes 776 | tf_op jit(solution)/shard_map/ppermute | solution.py:384
  13.8 17.5 %all-to-all-start = ((bf16[8,16,512]{2,1,0:T(8,128)(2,1)}), bf16[8,16,512]{2,1,0:T(8,128)(2,1)S(1)}, u32[]{:S(2)}, u32[]{:S(2)}) async-start(bf16[8,16,512]{2,1,0:T(8,128)(2,1)} %get-tuple-element.19), calls=%async_computation | async-start | bytes 262144 | tf_op jit(solution)/shard_map/all_to_all | solution.py:386
  23.3 4.2 %copy-start.9 = (bf16[512]{0:T(512)(128)(2,1)S(1)}, bf16[512]{0:T(512)(128)(2,1)}, u32[]{:S(2)}) copy-start(bf16[512]{0:T(512)(128)(2,1)} %param.23) | copy-start | bytes 3076
  23.4 8.0 %copy-start.6 = (bf16[512,1024]{1,0:T(8,128)(2,1)S(1)}, bf16[512,1024]{1,0:T(8,128)(2,1)}, u32[]{:S(2)}) copy-start(bf16[512,1024]{1,0:T(8,128)(2,1)} %w_ref.3) | copy-start | bytes 3145732
  23.4 8.0 %copy-start.7 = (bf16[8,2,512]{2,1,0:T(2,128)(2,1)S(1)}, bf16[8,2,512]{2,1,0:T(2,128)(2,1)}, u32[]{:S(2)}) copy-start(bf16[8,2,512]{2,1,0:T(2,128)(2,1)} %residual_ref.1) | copy-start | bytes 49156
  23.4 12.3 %copy-start.8 = (bf16[1024]{0:T(1024)(128)(2,1)S(1)}, bf16[1024]{0:T(1024)(128)(2,1)}, u32[]{:S(2)}) copy-start(bf16[1024]{0:T(1024)(128)(2,1)} %param.27) | copy-start | bytes 6148
  23.4 12.3 %collective-permute-start.7 = (bf16[4,16,1024]{2,1,0:T(8,128)(2,1)S(1)}, bf16[4,16,1024]{2,1,0:T(8,128)(2,1)S(1)}, u32[]{:S(2)}, u32[]{:S(2)}) collective-permute-start(bf16[4,16,1024]{2,1,0:T(8,128)(2,1)S(1)} %get-tuple-element.29), channel_id=1, source_target_pairs={{0,128},{8,136},{16,144},{24,152},{32,160},{40,168},{48,176},{56,1... | collective-permute-start | bytes 393224 | tf_op jit(solution)/shard_map/ppermute | solution.py:406
  24.0 11.7 %collective-permute-start.8 = (bf16[4,16,1024]{2,1,0:T(8,128)(2,1)S(1)}, bf16[4,16,1024]{2,1,0:T(8,128)(2,1)S(1)}, u32[]{:S(2)}, u32[]{:S(2)}) collective-permute-start(bf16[4,16,1024]{2,1,0:T(8,128)(2,1)S(1)} %get-tuple-element.30), channel_id=1, source_target_pairs={{0,64},{8,72},{16,80},{24,88},{32,96},{40,104},{48,112},{56,120},{... | collective-permute-start | bytes 393224 | tf_op jit(solution)/shard_map/ppermute | solution.py:406
  26.1 9.7 %collective-permute-start.9 = (bf16[4,16,1024]{2,1,0:T(8,128)(2,1)S(1)}, bf16[4,16,1024]{2,1,0:T(8,128)(2,1)S(1)}, u32[]{:S(2)}, u32[]{:S(2)}) collective-permute-start(bf16[4,16,1024]{2,1,0:T(8,128)(2,1)S(1)} %get-tuple-element.31), channel_id=1, source_target_pairs={{0,192},{8,200},{16,208},{24,216},{32,224},{40,232},{48,240},{56,2... | collective-permute-start | bytes 393224 | tf_op jit(solution)/shard_map/ppermute | solution.py:406
  32.3 11.9 %all-to-all-start.1 = ((f32[8,2,1152]{2,1,0:T(2,128)}), f32[8,2,1152]{2,1,0:T(2,128)S(1)}, u32[]{:S(2)}, u32[]{:S(2)}) async-start(f32[8,2,1152]{2,1,0:T(2,128)} %get-tuple-element.27), calls=%async_computation.1 | async-start | bytes 147456 | tf_op jit(solution)/shard_map/all_to_all | solution.py:438
  35.8 8.4 %collective-permute-start.10 = (bf16[16,1024]{1,0:T(8,128)(2,1)S(1)}, bf16[16,1024]{1,0:T(8,128)(2,1)S(1)}, u32[]{:S(2)}, u32[]{:S(2)}) collective-permute-start(bf16[16,1024]{1,0:T(8,128)(2,1)S(1)} %get-tuple-element.33), channel_id=1, source_target_pairs={{0,32},{8,40},{16,48},{24,56},{32,0},{40,8},{48,16},{56,24},{64,96... | collective-permute-start | bytes 98312 | tf_op jit(solution)/shard_map/ppermute | solution.py:421
  37.4 6.7 %collective-permute-start.11 = (bf16[16,1024]{1,0:T(8,128)(2,1)S(1)}, bf16[16,1024]{1,0:T(8,128)(2,1)S(1)}, u32[]{:S(2)}, u32[]{:S(2)}) collective-permute-start(bf16[16,1024]{1,0:T(8,128)(2,1)S(1)} %get-tuple-element.34), channel_id=1, source_target_pairs={{0,16},{8,24},{16,0},{24,8},{32,48},{40,56},{48,32},{56,40},{64,80... | collective-permute-start | bytes 98312 | tf_op jit(solution)/shard_map/ppermute | solution.py:421
  38.1 6.1 %collective-permute-start.12 = (bf16[16,1024]{1,0:T(8,128)(2,1)S(1)}, bf16[16,1024]{1,0:T(8,128)(2,1)S(1)}, u32[]{:S(2)}, u32[]{:S(2)}) collective-permute-start(bf16[16,1024]{1,0:T(8,128)(2,1)S(1)} %get-tuple-element.35), channel_id=1, source_target_pairs={{0,48},{8,56},{16,32},{24,40},{32,16},{40,24},{48,0},{56,8},{64,11... | collective-permute-start | bytes 98312 | tf_op jit(solution)/shard_map/ppermute | solution.py:421

commit v5 on v4

--- a/solution.py
+++ b/solution.py
@@ -18,11 +18,12 @@
 CORES = 2
 SIDE = 4
 STEPS = (2, 1, 3)
-LATE = 256
+LATE = 128
 EXTRA = 128
 MIB = 2**20
 LIMIT = 16
 WARM_FLOPS = 10**10
+GATHER_FLOPS = 10**10
 NT = (((1,), (1,)), ((), ()))
 
 
@@ -43,22 +44,11 @@
 
 
 def attend_kernel(
-    lengths_hbm, q_ref, nk_ref, nv_ref, k_ref, v_hbm, w_ref, own_hbm, order_ref, out_hbm, own_ref,
-    lengths_buf, v_buf, small, sent_buf, sems
+    lengths_hbm, q_ref, nk_ref, nv_ref, k_ref, v_ref, w_ref, order_ref, out_hbm, lengths_buf, small, sent_buf, sems
 ):
     get_lengths = pltpu.make_async_copy(lengths_hbm, lengths_buf, sems.at[0])
     dialogues = q_ref.shape[0]
-    half = dialogues // 2
-    get_values = [
-        pltpu.make_async_copy(
-            v_hbm.at[pl.ds(i * half, half)], v_buf.at[pl.ds(i * half, half)], sems.at[1 + i]
-        )
-        for i in range(2)
-    ]
-    get_own = pltpu.make_async_copy(own_hbm, own_ref, sems.at[3])
     get_lengths.start()
-    get_values[0].start()
-    get_values[1].start()
     width = q_ref.shape[2]
     rows = dialogues * FRAMES
     heads = width // HD
@@ -101,11 +91,8 @@
     )
     mixed = dot_nn(exp_fresh.astype(jnp.bfloat16), fresh_value)
     for d in range(dialogues):
-        if d % half == 0:
-            get_values[d // half].wait()
         own = jnp.where(of_dialogue[d], exp_cache, 0.0).astype(jnp.bfloat16)
-        mixed = mixed + dot_nn(own, v_buf[d])
-    get_own.start()
+        mixed = mixed + dot_nn(own, v_ref[d])
     mixed = mixed / total
     attended = mixed[:rows]
     for h in range(1, heads):
@@ -117,9 +104,8 @@
         sent_buf[t] = dot_nn(attended, w_ref[:, t * features : (t + 1) * features]).astype(
             jnp.bfloat16
         )
-        sends.append(pltpu.make_async_copy(sent_buf.at[t], out_hbm.at[t], sems.at[4 + t]))
+        sends.append(pltpu.make_async_copy(sent_buf.at[t], out_hbm.at[peers - 1 - t], sems.at[3 + t]))
         sends[t].start()
-    get_own.wait()
     for send in sends:
         send.wait()
 
@@ -216,7 +202,7 @@
         stream_ref[d] = rows_buf[FRAMES * d : FRAMES * (d + 1), :].astype(jnp.bfloat16)
     sent_buf[:, :width] = dot_nn(scaled, w_ref[...])
     for d in range(dialogues):
-        sent_ref[d] = sent_buf[FRAMES * d : FRAMES * (d + 1), :]
+        sent_ref[dialogues - 1 - d] = sent_buf[FRAMES * d : FRAMES * (d + 1), :]
 
 
 def depth_kernel(
@@ -228,7 +214,7 @@
     near = 3 * heads_width - LATE
     get_v = pltpu.make_async_copy(qkv_hbm.at[:, pl.ds(near, LATE)], v_buf, sems.at[0])
     get_o = pltpu.make_async_copy(
-        o_hbm.at[pl.ds(heads_width - LATE, LATE)], o_buf, sems.at[1]
+        o_hbm.at[pl.ds(LATE, heads_width - LATE)], o_buf, sems.at[1]
     )
     get_v.start()
     get_o.start()
@@ -334,27 +320,24 @@
     width = in_weight.shape[1]
     members = batch_size // CORES
     count = FRAMES * LEVELS
+    backward = [list(range(tensor_size))[::-1]]
 
     order = call(
         warm_kernel, "warm", pltpu.VMEM((8, 128), f32), [], VMEM, [], LIMIT, WARM_FLOPS, 1
     )()
     other_tables = lax.ppermute(level_tables, "batch", flipped(batch_size, 1, 1))
     near = [lax.ppermute(tokens, "batch", flipped(batch_size, CORES, s)) for s in STEPS]
-    head_terms, own_tables = call(
+    head_terms = call(
         attend_kernel,
         "attend",
-        (
-            pltpu.HBM((tensor_size, rows, features), bf16),
-            pltpu.VMEM(level_tables.shape, bf16),
-        ),
-        [ANY] + [VMEM] * 4 + [ANY, VMEM, ANY, VMEM],
-        (ANY, VMEM),
+        pltpu.HBM((tensor_size, rows, features), bf16),
+        [ANY] + [VMEM] * 7,
+        ANY,
         [
             pltpu.SMEM((held,), jnp.int32),
-            pltpu.VMEM(cache_values.shape, bf16),
             pltpu.VMEM((3, rows, new_queries.shape[2]), f32),
             pltpu.VMEM((tensor_size, rows, features), bf16),
-            pltpu.SemaphoreType.DMA((4 + tensor_size,)),
+            pltpu.SemaphoreType.DMA((3 + tensor_size,)),
         ],
         LIMIT,
         10**8,
@@ -365,25 +348,26 @@
         new_keys,
         new_values,
         cache_keys,
-        *hbm(cache_values),
+        cache_values,
         out_weight,
-        *hbm(level_tables),
         order,
     )
     column = call(
         gather_kernel,
         "gather",
         pltpu.VMEM((SIDE, FRAMES, LEVELS), jnp.int32),
-        [VMEM] * (SIDE + 1),
+        [VMEM] * SIDE + [ANY],
         VMEM,
         [],
         LIMIT,
-        10**6,
-        1,
-    )(tokens, *sorted_steps(near), own_tables)
+        GATHER_FLOPS,
+        1,
+    )(tokens, *sorted_steps(near), head_terms)
     ids = [lax.ppermute(column, "batch", flipped(batch_size, CORES * SIDE, s)) for s in STEPS]
 
-    shares = lax.all_to_all(head_terms, "tensor", 0, 0, tiled=True)
+    shares = lax.all_to_all(
+        head_terms, "tensor", 0, 0, axis_index_groups=backward, tiled=True
+    )
 
     partial_rows = call(
         lookup_kernel,
@@ -397,7 +381,7 @@
         LIMIT,
         10**11,
         1,
-    )(column, *sorted_steps(ids), own_tables, other_tables)
+    )(column, *sorted_steps(ids), level_tables, other_tables)
     looked = call(
         warm_kernel, "warm_in", pltpu.VMEM((8, 128), f32), [VMEM], VMEM, [], LIMIT, WARM_FLOPS, 1
     )(partial_rows[0])
@@ -435,7 +419,9 @@
         10**9,
         1,
     )(shares, residual, temporal_gain.astype(f32).reshape(1, features), in_weight, looked)
-    terms = lax.all_to_all(sent, "tensor", 0, 0, tiled=True)
+    terms = lax.all_to_all(
+        sent, "tensor", 0, 0, axis_index_groups=backward, tiled=True
+    )
 
     near_weights = call(
         fetch_kernel,
@@ -456,7 +442,7 @@
         VMEM,
         [
             pltpu.VMEM((width, LATE), bf16),
-            pltpu.VMEM((LATE, width), bf16),
+            pltpu.VMEM((depth_out.shape[0] - LATE, width), bf16),
             pltpu.SemaphoreType.DMA((2,)),
         ],
         LIMIT,

time: 46.9 us -> 46.2 us (0.985)
  waiting for transfers between devices: 7.76 us -> 3.59 us
  starting transfers between devices: 28.8 us -> 32.5 us
    all_to_all x2, waiting for transfers between devices: 6.13 us -> 0.64 us  [the longest x1 0.64 us: per_device(): lax.all_to_all(head_terms, 'tensor', 0, 0, axis_index_groups=backward, ti...]
    all_to_all x2, starting transfers between devices: 11.9 us -> 15.7 us  [the longest x1 9.17 us: per_device(): lax.all_to_all(head_terms, 'tensor', 0, 0, axis_index_groups=backward, ti...]
    ppermute x3, waiting for transfers between devices: 0.01 us -> 1.01 us  [per_device(): lax.ppermute(side_rows[s - 1], 'batch', flipped(batch_size, CORES, s))]
where the time goes in v5:
time: 46.2 us; the launch traced here: 45.9 us
  starting transfers between devices  32.5 us (70%)
  Pallas kernels  8.79 us (19%)
  waiting for transfers between devices  3.59 us (8%)
  between operations  0.9 us (2%)
    all_to_all x1, starting transfers between devices, per_device(): lax.all_to_all(head_terms, 'tensor', 0, 0, axis_index_groups=backward, ti...  9.17 us
    all_to_all x1, starting transfers between devices, per_device(): lax.all_to_all(sent, 'tensor', 0, 0, axis_index_groups=backward, tiled=True)  6.57 us
    ppermute x3, starting transfers between devices, per_device(): lax.ppermute(tokens, 'batch', flipped(batch_size, CORES, s))  4.34 us
    ppermute x3, starting transfers between devices, per_device(): lax.ppermute(partial_rows[s], 'batch', flipped(batch_size, CORES * SIDE, s))  4.18 us
    ppermute x3, starting transfers between devices, per_device(): lax.ppermute(side_rows[s - 1], 'batch', flipped(batch_size, CORES, s))  4.18 us
    ppermute x3, starting transfers between devices, per_device(): lax.ppermute(column, 'batch', flipped(batch_size, CORES * SIDE, s))  4.09 us
    pallas_call x1, Pallas kernels, per_device(): call(attend_kernel, 'attend', pltpu.HBM((tensor_size, rows, features), bf...  2.6 us
    pallas_call x1, Pallas kernels, per_device(): call(depth_kernel, 'depth', pltpu.HBM((count, width), bf16), [VMEM] * (SI...  2.35 us
  transfers between devices with their start and end apart: 15, of which 3 were waited for; matrix products, arithmetic and copies ran while one was open for 0% of the time, Pallas kernels for 14%

profile of v5, /device:TPU:4, one launch (start us, length us, event | category | flops | bytes accessed | tf_op | source)
XLA Modules:
  0.0 45.9 jit_solution(16093368086694267806)
XLA Ops:
  0.6 0.0 copy-start
  0.6 0.0 copy-start.2
  0.7 0.0 copy-start.1
  0.7 0.0 copy-start.5
  0.7 0.0 copy-start.4
  0.7 0.0 copy-start.3
  0.7 3.3 %collective-permute-start.1 = (s32[1,2,8]{2,1,0:T(2,128)}, s32[1,2,8]{2,1,0:T(2,128)S(1)}, u32[]{:S(2)}, u32[]{:S(2)}) collective-permute-start(s32[1,2,8]{2,1,0:T(2,128)} %refs_0_.1), channel_id=1, source_target_pairs={{0,32},{8,40},{16,48},{24,56},{32,0},{40,8},{48,16},{56,24},{64,96... | collective-permute-start | bytes 200 | tf_op jit(solution)/shard_map/ppermute | solution.py:329
  4.0 0.7 %collective-permute-start = (s32[1,2,8]{2,1,0:T(2,128)}, s32[1,2,8]{2,1,0:T(2,128)S(1)}, u32[]{:S(2)}, u32[]{:S(2)}) collective-permute-start(s32[1,2,8]{2,1,0:T(2,128)} %refs_0_.1), channel_id=1, source_target_pairs={{0,16},{8,24},{16,0},{24,8},{32,48},{40,56},{48,32},{56,40},{64,80... | collective-permute-start | bytes 200 | tf_op jit(solution)/shard_map/ppermute | solution.py:329
  4.7 0.4 collective-permute-start.2
  5.0 0.0 collective-permute-start.6
  5.0 0.0 copy-done
  5.0 0.0 copy-done.2
  5.0 0.0 copy-done.1
  5.1 0.0 copy-done.5
  5.1 0.0 copy-done.4
  5.1 0.0 copy-done.3
  5.1 0.0 copy-start.9
  5.1 2.6 %attend.1.refs_4_ = bf16[8,16,512]{2,1,0:T(8,128)(2,1)} custom-call(s32[8]{0:T(128)} %lengths_hbm.1, bf16[8,2,256]{2,1,0:T(2,128)(2,1)S(1)} %copy-done.3, bf16[8,2,256]{2,1,0:T(2,128)(2,1)S(1)} %copy-done.4, bf16[8,2,256]{2,1,0:T(2,128)(2,1)S(1)} %copy-done.5, bf16[8,256,256]{2,1,0:T(8,128)(2,1)S(1)} %copy-done.1, bf16[8,256,256]{2,1,0:T(8,128)(2,1)S(1)} %copy-done.2, ...), custom_call_target="tpu_custom_call" | custom-call | flops 100000000 | bytes 4194304 | tf_op jit(solution)/shard_map/attend/pallas_call | solution.py:330
  7.7 0.0 copy-start.6
  7.7 0.0 collective-permute-done.1.refs_2_
  7.7 0.0 collective-permute-done.refs_1_
  7.8 1.9 %collective-permute-done.2.refs_3_ = s32[1,2,8]{2,1,0:T(2,128)S(1)} collective-permute-done((s32[1,2,8]{2,1,0:T(2,128)}, s32[1,2,8]{2,1,0:T(2,128)S(1)}, u32[]{:S(2)}, u32[]{:S(2)}) %collective-permute-start.2) | collective-permute-done | bytes 96 | tf_op jit(solution)/shard_map/ppermute | solution.py:329
  9.6 0.0 copy-done.9
  9.6 0.5 %collective-permute-start.5 = (s32[4,2,8]{2,1,0:T(2,128)S(1)}, s32[4,2,8]{2,1,0:T(2,128)S(1)}, u32[]{:S(2)}, u32[]{:S(2)}) collective-permute-start(s32[4,2,8]{2,1,0:T(2,128)S(1)} %gather.1.refs_0_), channel_id=1, source_target_pairs={{0,192},{8,200},{16,208},{24,216},{32,224},{40,232},{48,240},{56,2... | collective-permute-start | bytes 776 | tf_op jit(solution)/shard_map/ppermute | solution.py:366
  10.2 2.7 %collective-permute-start.4 = (s32[4,2,8]{2,1,0:T(2,128)S(1)}, s32[4,2,8]{2,1,0:T(2,128)S(1)}, u32[]{:S(2)}, u32[]{:S(2)}) collective-permute-start(s32[4,2,8]{2,1,0:T(2,128)S(1)} %gather.1.refs_0_), channel_id=1, source_target_pairs={{0,128},{8,136},{16,144},{24,152},{32,160},{40,168},{48,176},{56,1... | collective-permute-start | bytes 776 | tf_op jit(solution)/shard_map/ppermute | solution.py:366
  12.9 0.8 %collective-permute-start.3 = (s32[4,2,8]{2,1,0:T(2,128)S(1)}, s32[4,2,8]{2,1,0:T(2,128)S(1)}, u32[]{:S(2)}, u32[]{:S(2)}) collective-permute-start(s32[4,2,8]{2,1,0:T(2,128)S(1)} %gather.1.refs_0_), channel_id=1, source_target_pairs={{0,64},{8,72},{16,80},{24,88},{32,96},{40,104},{48,112},{56,120},{... | collective-permute-start | bytes 776 | tf_op jit(solution)/shard_map/ppermute | solution.py:366
  13.7 9.2 %all-to-all-start = ((bf16[8,16,512]{2,1,0:T(8,128)(2,1)}), bf16[8,16,512]{2,1,0:T(8,128)(2,1)S(1)}, u32[]{:S(2)}, u32[]{:S(2)}) async-start(bf16[8,16,512]{2,1,0:T(8,128)(2,1)} %attend.1.refs_4_), calls=%async_computation | async-start | bytes 262144 | tf_op jit(solution)/shard_map/all_to_all | solution.py:368
  22.9 0.0 collective-permute-done.5.refs_3_
  22.9 0.0 collective-permute-done.4.refs_2_
  22.9 0.0 collective-permute-done.3.refs_1_
  22.9 0.0 collective-permute-done.6.refs_5_
  22.9 0.0 copy-done.6
  23.0 1.0 %lookup.1 = (bf16[4,16,1024]{2,1,0:T(8,128)(2,1)S(1)}, bf16[4,16,1024]{2,1,0:T(8,128)(2,1)S(1)}, bf16[4,16,1024]{2,1,0:T(8,128)(2,1)S(1)}, bf16[4,16,1024]{2,1,0:T(8,128)(2,1)S(1)}) custom-call(s32[4,2,8]{2,1,0:T(2,128)S(1)} %gather.1.refs_0_, s32[4,2,8]{2,1,0:T(2,128)S(1)} %collective-permute-done.3.refs_1_, s32[4,2,8]{2,1,0:T(2,128)S(1)} %collective-permute-done.4.refs_2_, ...), custom_call_target="tpu_custom_call" | custom-call | flops 99999997952 | bytes 1 | tf_op jit(solution)/shard_map/lookup/pallas_call | solution.py:372
  23.9 0.0 copy-start.11
  24.0 0.0 copy-start.7
  24.0 0.0 copy-start.8
  24.0 0.0 copy-start.10
  24.0 0.6 %collective-permute-start.7 = (bf16[4,16,1024]{2,1,0:T(8,128)(2,1)S(1)}, bf16[4,16,1024]{2,1,0:T(8,128)(2,1)S(1)}, u32[]{:S(2)}, u32[]{:S(2)}) collective-permute-start(bf16[4,16,1024]{2,1,0:T(8,128)(2,1)S(1)} %get-tuple-element.25), channel_id=1, source_target_pairs={{0,128},{8,136},{16,144},{24,152},{32,160},{40,168},{48,176},{56,1... | collective-permute-start | bytes 393224 | tf_op jit(solution)/shard_map/ppermute | solution.py:390
  24.6 2.1 %collective-permute-start.8 = (bf16[4,16,1024]{2,1,0:T(8,128)(2,1)S(1)}, bf16[4,16,1024]{2,1,0:T(8,128)(2,1)S(1)}, u32[]{:S(2)}, u32[]{:S(2)}) collective-permute-start(bf16[4,16,1024]{2,1,0:T(8,128)(2,1)S(1)} %get-tuple-element.26), channel_id=1, source_target_pairs={{0,64},{8,72},{16,80},{24,88},{32,96},{40,104},{48,112},{56,120},{... | collective-permute-start | bytes 393224 | tf_op jit(solution)/shard_map/ppermute | solution.py:390
  26.7 1.5 %collective-permute-start.9 = (bf16[4,16,1024]{2,1,0:T(8,128)(2,1)S(1)}, bf16[4,16,1024]{2,1,0:T(8,128)(2,1)S(1)}, u32[]{:S(2)}, u32[]{:S(2)}) collective-permute-start(bf16[4,16,1024]{2,1,0:T(8,128)(2,1)S(1)} %get-tuple-element.27), channel_id=1, source_target_pairs={{0,192},{8,200},{16,208},{24,216},{32,224},{40,232},{48,240},{56,2... | collective-permute-start | bytes 393224 | tf_op jit(solution)/shard_map/ppermute | solution.py:390
  28.2 0.0 copy-done.11
  28.2 0.6 %all-to-all-done.shares_ref = bf16[8,16,512]{2,1,0:T(8,128)(2,1)S(1)} async-done(((bf16[8,16,512]{2,1,0:T(8,128)(2,1)}), bf16[8,16,512]{2,1,0:T(8,128)(2,1)S(1)}, u32[]{:S(2)}, u32[]{:S(2)}) %all-to-all-start) | async-done | bytes 131104 | tf_op jit(solution)/shard_map/all_to_all | solution.py:368
  28.8 0.0 copy-done.7
  28.8 0.0 copy-done.8
  28.8 0.9 %middle.1 = (bf16[8,2,512]{2,1,0:T(2,128)(2,1)}, f32[8,2,1152]{2,1,0:T(2,128)}) custom-call(bf16[8,16,512]{2,1,0:T(8,128)(2,1)S(1)} %all-to-all-done.shares_ref, bf16[8,2,512]{2,1,0:T(2,128)(2,1)S(1)} %copy-done.8, f32[1,512]{1,0:T(1,128)S(1)} %bitcast.4, bf16[512,1024]{1,0:T(8,128)(2,1)S(1)} %copy-done.7, f32[8,128]{1,0:T(8,128)S(1)} %warm_in.1.order_ref), custom_call_target="tpu_custom_call" | custom-call | flops 1000000000 | bytes 1 | tf_op jit(solution)/shard_map/middle/pallas_call | solution.py:408
  29.8 6.6 %all-to-all-start.1 = ((f32[8,2,1152]{2,1,0:T(2,128)}), f32[8,2,1152]{2,1,0:T(2,128)S(1)}, u32[]{:S(2)}, u32[]{:S(2)}) async-start(f32[8,2,1152]{2,1,0:T(2,128)} %get-tuple-element.23), calls=%async_computation.1 | async-start | bytes 147456 | tf_op jit(solution)/shard_map/all_to_all | solution.py:422
  36.3 0.0 copy-done.10
  36.3 0.0 collective-permute-done.7.refs_0_
  36.3 0.0 collective-permute-done.8.refs_1_
  36.4 0.0 collective-permute-done.9.refs_2_
  36.4 1.3 %collective-permute-start.10 = (bf16[16,1024]{1,0:T(8,128)(2,1)S(1)}, bf16[16,1024]{1,0:T(8,128)(2,1)S(1)}, u32[]{:S(2)}, u32[]{:S(2)}) collective-permute-start(bf16[16,1024]{1,0:T(8,128)(2,1)S(1)} %get-tuple-element.29), channel_id=1, source_target_pairs={{0,32},{8,40},{16,48},{24,56},{32,0},{40,8},{48,16},{56,24},{64,96... | collective-permute-start | bytes 98312 | tf_op jit(solution)/shard_map/ppermute | solution.py:405
  37.7 0.7 %collective-permute-start.11 = (bf16[16,1024]{1,0:T(8,128)(2,1)S(1)}, bf16[16,1024]{1,0:T(8,128)(2,1)S(1)}, u32[]{:S(2)}, u32[]{:S(2)}) collective-permute-start(bf16[16,1024]{1,0:T(8,128)(2,1)S(1)} %get-tuple-element.30), channel_id=1, source_target_pairs={{0,16},{8,24},{16,0},{24,8},{32,48},{40,56},{48,32},{56,40},{64,80... | collective-permute-start | bytes 98312 | tf_op jit(solution)/shard_map/ppermute | solution.py:405
  38.4 2.2 %collective-permute-start.12 = (bf16[16,1024]{1,0:T(8,128)(2,1)S(1)}, bf16[16,1024]{1,0:T(8,128)(2,1)S(1)}, u32[]{:S(2)}, u32[]{:S(2)}) collective-permute-start(bf16[16,1024]{1,0:T(8,128)(2,1)S(1)} %get-tuple-element.31), channel_id=1, source_target_pairs={{0,48},{8,56},{16,32},{24,40},{32,16},{40,24},{48,0},{56,8},{64,11... | collective-permute-start | bytes 98312 | tf_op jit(solution)/shard_map/ppermute | solution.py:405
  40.6 1.9 %fetch.1.refs_5_ = bf16[1024,1536]{1,0:T(8,128)(2,1)S(1)} custom-call(bf16[1024,1536]{1,0:T(8,128)(2,1)} %refs_6_.1, bf16[512,1024]{1,0:T(8,128)(2,1)} %refs_7_.1, bf16[16,1024]{1,0:T(8,128)(2,1)S(1)} %get-tuple-element.28.order_ref.refs_0_), custom_call_target="tpu_custom_call" | custom-call | flops 1000000000 | bytes 1 | tf_op jit(solution)/shard_map/fetch/pallas_call | solution.py:426
  42.5 0.0 all-to-all-done.1.terms_ref
  42.5 0.0 collective-permute-done.10.refs_1_
  42.5 0.0 collective-permute-done.11.refs_2_
  42.5 1.0 %collective-permute-done.12.refs_3_ = bf16[16,1024]{1,0:T(8,128)(2,1)S(1)} collective-permute-done((bf16[16,1024]{1,0:T(8,128)(2,1)S(1)}, bf16[16,1024]{1,0:T(8,128)(2,1)S(1)}, u32[]{:S(2)}, u32[]{:S(2)}) %collective-permute-start.12) | collective-permute-done | bytes 32800 | tf_op jit(solution)/shard_map/ppermute | solution.py:405
  43.5 2.3 %depth.1 = bf16[16,1024]{1,0:T(8,128)(2,1)} custom-call(f32[8,2,1152]{2,1,0:T(2,128)S(1)} %all-to-all-done.1.terms_ref, bf16[16,1024]{1,0:T(8,128)(2,1)S(1)} %get-tuple-element.28.order_ref.refs_0_, bf16[16,1024]{1,0:T(8,128)(2,1)S(1)} %collective-permute-done.10.refs_1_, bf16[16,1024]{1,0:T(8,128)(2,1)S(1)} %collective-permute-done.11.refs_2_, ...), custom_call_target="tpu_custom_call" | custom-call | flops 1000000000 | bytes 1 | tf_op jit(solution)/shard_map/depth/pallas_call | solution.py:437
  (6 shorter events, 0.0 us)
Async XLA Ops:
  0.6 4.4 %copy-start = (bf16[256,4096]{1,0:T(8,128)(2,1)S(1)}, bf16[256,4096]{1,0:T(8,128)(2,1)}, u32[]{:S(2)}) copy-start(bf16[256,4096]{1,0:T(8,128)(2,1)} %w_ref.2) | copy-start | bytes 6291460
  0.6 4.4 %copy-start.2 = (bf16[8,256,256]{2,1,0:T(8,128)(2,1)S(1)}, bf16[8,256,256]{2,1,0:T(8,128)(2,1)}, u32[]{:S(2)}) copy-start(bf16[8,256,256]{2,1,0:T(8,128)(2,1)} %v_ref.1) | copy-start | bytes 3145732
  0.7 4.4 %copy-start.1 = (bf16[8,256,256]{2,1,0:T(8,128)(2,1)S(1)}, bf16[8,256,256]{2,1,0:T(8,128)(2,1)}, u32[]{:S(2)}) copy-start(bf16[8,256,256]{2,1,0:T(8,128)(2,1)} %k_ref.1) | copy-start | bytes 3145732
  0.7 4.4 %copy-start.5 = (bf16[8,2,256]{2,1,0:T(2,128)(2,1)S(1)}, bf16[8,2,256]{2,1,0:T(2,128)(2,1)}, u32[]{:S(2)}) copy-start(bf16[8,2,256]{2,1,0:T(2,128)(2,1)} %nv_ref.1) | copy-start | bytes 24580
  0.7 4.4 %copy-start.4 = (bf16[8,2,256]{2,1,0:T(2,128)(2,1)S(1)}, bf16[8,2,256]{2,1,0:T(2,128)(2,1)}, u32[]{:S(2)}) copy-start(bf16[8,2,256]{2,1,0:T(2,128)(2,1)} %nk_ref.1) | copy-start | bytes 24580
  0.7 4.4 %copy-start.3 = (bf16[8,2,256]{2,1,0:T(2,128)(2,1)S(1)}, bf16[8,2,256]{2,1,0:T(2,128)(2,1)}, u32[]{:S(2)}) copy-start(bf16[8,2,256]{2,1,0:T(2,128)(2,1)} %q_ref.1) | copy-start | bytes 24580
  0.7 7.0 %collective-permute-start.1 = (s32[1,2,8]{2,1,0:T(2,128)}, s32[1,2,8]{2,1,0:T(2,128)S(1)}, u32[]{:S(2)}, u32[]{:S(2)}) collective-permute-start(s32[1,2,8]{2,1,0:T(2,128)} %refs_0_.1), channel_id=1, source_target_pairs={{0,32},{8,40},{16,48},{24,56},{32,0},{40,8},{48,16},{56,24},{64,96... | collective-permute-start | bytes 200 | tf_op jit(solution)/shard_map/ppermute | solution.py:329
  4.0 3.8 %collective-permute-start = (s32[1,2,8]{2,1,0:T(2,128)}, s32[1,2,8]{2,1,0:T(2,128)S(1)}, u32[]{:S(2)}, u32[]{:S(2)}) collective-permute-start(s32[1,2,8]{2,1,0:T(2,128)} %refs_0_.1), channel_id=1, source_target_pairs={{0,16},{8,24},{16,0},{24,8},{32,48},{40,56},{48,32},{56,40},{64,80... | collective-permute-start | bytes 200 | tf_op jit(solution)/shard_map/ppermute | solution.py:329
  4.7 5.0 %collective-permute-start.2 = (s32[1,2,8]{2,1,0:T(2,128)}, s32[1,2,8]{2,1,0:T(2,128)S(1)}, u32[]{:S(2)}, u32[]{:S(2)}) collective-permute-start(s32[1,2,8]{2,1,0:T(2,128)} %refs_0_.1), channel_id=1, source_target_pairs={{0,48},{8,56},{16,32},{24,40},{32,16},{40,24},{48,0},{56,8},{64,11... | collective-permute-start | bytes 200 | tf_op jit(solution)/shard_map/ppermute | solution.py:329
  5.0 17.9 %collective-permute-start.6 = (bf16[8,64,1024]{2,1,0:T(8,128)(2,1)}, bf16[8,64,1024]{2,1,0:T(8,128)(2,1)S(1)}, u32[]{:S(2)}, u32[]{:S(2)}) collective-permute-start(bf16[8,64,1024]{2,1,0:T(8,128)(2,1)} %refs_4_.1), channel_id=1, source_target_pairs={{0,8},{8,0},{16,24},{24,16},{32,40},{40,32},{48,56},{56,48},{64,72... | collective-permute-start | bytes 3145736 | tf_op jit(solution)/shard_map/ppermute | solution.py:328
  5.1 4.6 %copy-start.9 = (s32[1,2,8]{2,1,0:T(2,128)S(1)}, s32[1,2,8]{2,1,0:T(2,128)}, u32[]{:S(2)}) copy-start(s32[1,2,8]{2,1,0:T(2,128)} %refs_0_.1) | copy-start | bytes 196
  7.7 15.2 %copy-start.6 = (bf16[8,64,1024]{2,1,0:T(8,128)(2,1)S(1)}, bf16[8,64,1024]{2,1,0:T(8,128)(2,1)}, u32[]{:S(2)}) copy-start(bf16[8,64,1024]{2,1,0:T(8,128)(2,1)} %refs_4_.1) | copy-start | bytes 3145732
  9.6 13.3 %collective-permute-start.5 = (s32[4,2,8]{2,1,0:T(2,128)S(1)}, s32[4,2,8]{2,1,0:T(2,128)S(1)}, u32[]{:S(2)}, u32[]{:S(2)}) collective-permute-start(s32[4,2,8]{2,1,0:T(2,128)S(1)} %gather.1.refs_0_), channel_id=1, source_target_pairs={{0,192},{8,200},{16,208},{24,216},{32,224},{40,232},{48,240},{56,2... | collective-permute-start | bytes 776 | tf_op jit(solution)/shard_map/ppermute | solution.py:366
  10.2 12.7 %collective-permute-start.4 = (s32[4,2,8]{2,1,0:T(2,128)S(1)}, s32[4,2,8]{2,1,0:T(2,128)S(1)}, u32[]{:S(2)}, u32[]{:S(2)}) collective-permute-start(s32[4,2,8]{2,1,0:T(2,128)S(1)} %gather.1.refs_0_), channel_id=1, source_target_pairs={{0,128},{8,136},{16,144},{24,152},{32,160},{40,168},{48,176},{56,1... | collective-permute-start | bytes 776 | tf_op jit(solution)/shard_map/ppermute | solution.py:366
  12.9 10.0 %collective-permute-start.3 = (s32[4,2,8]{2,1,0:T(2,128)S(1)}, s32[4,2,8]{2,1,0:T(2,128)S(1)}, u32[]{:S(2)}, u32[]{:S(2)}) collective-permute-start(s32[4,2,8]{2,1,0:T(2,128)S(1)} %gather.1.refs_0_), channel_id=1, source_target_pairs={{0,64},{8,72},{16,80},{24,88},{32,96},{40,104},{48,112},{56,120},{... | collective-permute-start | bytes 776 | tf_op jit(solution)/shard_map/ppermute | solution.py:366
  13.7 15.1 %all-to-all-start = ((bf16[8,16,512]{2,1,0:T(8,128)(2,1)}), bf16[8,16,512]{2,1,0:T(8,128)(2,1)S(1)}, u32[]{:S(2)}, u32[]{:S(2)}) async-start(bf16[8,16,512]{2,1,0:T(8,128)(2,1)} %attend.1.refs_4_), calls=%async_computation | async-start | bytes 262144 | tf_op jit(solution)/shard_map/all_to_all | solution.py:368
  23.9 4.2 %copy-start.11 = (bf16[512]{0:T(512)(128)(2,1)S(1)}, bf16[512]{0:T(512)(128)(2,1)}, u32[]{:S(2)}) copy-start(bf16[512]{0:T(512)(128)(2,1)} %param.23) | copy-start | bytes 3076
  24.0 4.9 %copy-start.7 = (bf16[512,1024]{1,0:T(8,128)(2,1)S(1)}, bf16[512,1024]{1,0:T(8,128)(2,1)}, u32[]{:S(2)}) copy-start(bf16[512,1024]{1,0:T(8,128)(2,1)} %w_ref.3) | copy-start | bytes 3145732
  24.0 4.9 %copy-start.8 = (bf16[8,2,512]{2,1,0:T(2,128)(2,1)S(1)}, bf16[8,2,512]{2,1,0:T(2,128)(2,1)}, u32[]{:S(2)}) copy-start(bf16[8,2,512]{2,1,0:T(2,128)(2,1)} %residual_ref.1) | copy-start | bytes 49156
  24.0 12.3 %copy-start.10 = (bf16[1024]{0:T(1024)(128)(2,1)S(1)}, bf16[1024]{0:T(1024)(128)(2,1)}, u32[]{:S(2)}) copy-start(bf16[1024]{0:T(1024)(128)(2,1)} %param.27) | copy-start | bytes 6148
  24.0 12.3 %collective-permute-start.7 = (bf16[4,16,1024]{2,1,0:T(8,128)(2,1)S(1)}, bf16[4,16,1024]{2,1,0:T(8,128)(2,1)S(1)}, u32[]{:S(2)}, u32[]{:S(2)}) collective-permute-start(bf16[4,16,1024]{2,1,0:T(8,128)(2,1)S(1)} %get-tuple-element.25), channel_id=1, source_target_pairs={{0,128},{8,136},{16,144},{24,152},{32,160},{40,168},{48,176},{56,1... | collective-permute-start | bytes 393224 | tf_op jit(solution)/shard_map/ppermute | solution.py:390
  24.6 11.7 %collective-permute-start.8 = (bf16[4,16,1024]{2,1,0:T(8,128)(2,1)S(1)}, bf16[4,16,1024]{2,1,0:T(8,128)(2,1)S(1)}, u32[]{:S(2)}, u32[]{:S(2)}) collective-permute-start(bf16[4,16,1024]{2,1,0:T(8,128)(2,1)S(1)} %get-tuple-element.26), channel_id=1, source_target_pairs={{0,64},{8,72},{16,80},{24,88},{32,96},{40,104},{48,112},{56,120},{... | collective-permute-start | bytes 393224 | tf_op jit(solution)/shard_map/ppermute | solution.py:390
  26.7 9.7 %collective-permute-start.9 = (bf16[4,16,1024]{2,1,0:T(8,128)(2,1)S(1)}, bf16[4,16,1024]{2,1,0:T(8,128)(2,1)S(1)}, u32[]{:S(2)}, u32[]{:S(2)}) collective-permute-start(bf16[4,16,1024]{2,1,0:T(8,128)(2,1)S(1)} %get-tuple-element.27), channel_id=1, source_target_pairs={{0,192},{8,200},{16,208},{24,216},{32,224},{40,232},{48,240},{56,2... | collective-permute-start | bytes 393224 | tf_op jit(solution)/shard_map/ppermute | solution.py:390
  29.8 12.7 %all-to-all-start.1 = ((f32[8,2,1152]{2,1,0:T(2,128)}), f32[8,2,1152]{2,1,0:T(2,128)S(1)}, u32[]{:S(2)}, u32[]{:S(2)}) async-start(f32[8,2,1152]{2,1,0:T(2,128)} %get-tuple-element.23), calls=%async_computation.1 | async-start | bytes 147456 | tf_op jit(solution)/shard_map/all_to_all | solution.py:422
  36.4 6.1 %collective-permute-start.10 = (bf16[16,1024]{1,0:T(8,128)(2,1)S(1)}, bf16[16,1024]{1,0:T(8,128)(2,1)S(1)}, u32[]{:S(2)}, u32[]{:S(2)}) collective-permute-start(bf16[16,1024]{1,0:T(8,128)(2,1)S(1)} %get-tuple-element.29), channel_id=1, source_target_pairs={{0,32},{8,40},{16,48},{24,56},{32,0},{40,8},{48,16},{56,24},{64,96... | collective-permute-start | bytes 98312 | tf_op jit(solution)/shard_map/ppermute | solution.py:405
  37.7 4.8 %collective-permute-start.11 = (bf16[16,1024]{1,0:T(8,128)(2,1)S(1)}, bf16[16,1024]{1,0:T(8,128)(2,1)S(1)}, u32[]{:S(2)}, u32[]{:S(2)}) collective-permute-start(bf16[16,1024]{1,0:T(8,128)(2,1)S(1)} %get-tuple-element.30), channel_id=1, source_target_pairs={{0,16},{8,24},{16,0},{24,8},{32,48},{40,56},{48,32},{56,40},{64,80... | collective-permute-start | bytes 98312 | tf_op jit(solution)/shard_map/ppermute | solution.py:405
  38.4 5.1 %collective-permute-start.12 = (bf16[16,1024]{1,0:T(8,128)(2,1)S(1)}, bf16[16,1024]{1,0:T(8,128)(2,1)S(1)}, u32[]{:S(2)}, u32[]{:S(2)}) collective-permute-start(bf16[16,1024]{1,0:T(8,128)(2,1)S(1)} %get-tuple-element.31), channel_id=1, source_target_pairs={{0,48},{8,56},{16,32},{24,40},{32,16},{40,24},{48,0},{56,8},{64,11... | collective-permute-start | bytes 98312 | tf_op jit(solution)/shard_map/ppermute | solution.py:405

commit v6 on v5

--- a/solution.py
+++ b/solution.py
@@ -44,11 +44,9 @@
 
 
 def attend_kernel(
-    lengths_hbm, q_ref, nk_ref, nv_ref, k_ref, v_ref, w_ref, order_ref, out_hbm, lengths_buf, small, sent_buf, sems
+    lengths_ref, q_ref, nk_ref, nv_ref, k_ref, v_ref, w_ref, order_ref, out_hbm, small, sent_buf, sems
 ):
-    get_lengths = pltpu.make_async_copy(lengths_hbm, lengths_buf, sems.at[0])
     dialogues = q_ref.shape[0]
-    get_lengths.start()
     width = q_ref.shape[2]
     rows = dialogues * FRAMES
     heads = width // HD
@@ -76,10 +74,12 @@
     col_n = iota((stacked, rows), 1)
     seen = (row_n // FRAMES == col_n // FRAMES) & (col_n <= row_n)
     fresh = jnp.where(seen, dot_nt(spread, fresh_key) * scale, -jnp.inf)
-    get_lengths.wait()
-    live = jnp.zeros((stacked, slots), jnp.int32)
-    for d in range(dialogues):
-        live = jnp.where(of_dialogue[d], lengths_buf[d], live)
+    row_d = (iota((stacked, dialogues), 0) % rows) // FRAMES
+    live = jnp.sum(
+        jnp.where(row_d == iota((stacked, dialogues), 1), lengths_ref[...].astype(jnp.float32), 0.0),
+        axis=-1,
+        keepdims=True,
+    ).astype(jnp.int32)
     scores = jnp.where(slot < live, scores * scale, -jnp.inf)
     largest = jnp.maximum(
         jnp.max(scores, axis=-1, keepdims=True), jnp.max(fresh, axis=-1, keepdims=True)
@@ -331,10 +331,9 @@
         attend_kernel,
         "attend",
         pltpu.HBM((tensor_size, rows, features), bf16),
-        [ANY] + [VMEM] * 7,
+        [VMEM] * 8,
         ANY,
         [
-            pltpu.SMEM((held,), jnp.int32),
             pltpu.VMEM((3, rows, new_queries.shape[2]), f32),
             pltpu.VMEM((tensor_size, rows, features), bf16),
             pltpu.SemaphoreType.DMA((3 + tensor_size,)),
@@ -343,7 +342,7 @@
         10**8,
         4 * 2**20,
     )(
-        *hbm(lengths),
+        lengths.reshape(1, held),
         new_queries,
         new_keys,
         new_values,

time: 46.2 us -> 45.7 us (0.989)
  Pallas kernels: 8.79 us -> 8.27 us
    pallas_call x1, Pallas kernels: 2.6 us -> 2.08 us  [per_device(): call(attend_kernel, 'attend', pltpu.HBM((tensor_size, rows, features), bf...]
    ppermute x3, waiting for transfers between devices: 1.91 us -> 2.43 us  [per_device(): lax.ppermute(tokens, 'batch', flipped(batch_size, CORES, s))]
    ppermute x3, waiting for transfers between devices: 1.01 us -> 0.5 us  [per_device(): lax.ppermute(side_rows[s - 1], 'batch', flipped(batch_size, CORES, s))]
  transfers between devices with their start and end apart: 15 -> 15, of which waited for: 3 -> 4; matrix products, arithmetic and copies ran while one was open for 0% -> 0% of each run, Pallas kernels for 14% -> 13%
where the time goes in v6:
time: 45.7 us; the launch traced here: 45.4 us
  starting transfers between devices  32.8 us (72%)
  Pallas kernels  8.27 us (18%)
  waiting for transfers between devices  3.35 us (7%)
  between operations  0.92 us (2%)
    all_to_all x1, starting transfers between devices, per_device(): lax.all_to_all(head_terms, 'tensor', 0, 0, axis_index_groups=backward, ti...  9.17 us
    all_to_all x1, starting transfers between devices, per_device(): lax.all_to_all(sent, 'tensor', 0, 0, axis_index_groups=backward, tiled=True)  6.81 us
    ppermute x3, starting transfers between devices, per_device(): lax.ppermute(tokens, 'batch', flipped(batch_size, CORES, s))  4.34 us
    ppermute x3, starting transfers between devices, per_device(): lax.ppermute(partial_rows[s], 'batch', flipped(batch_size, CORES * SIDE, s))  4.18 us
    ppermute x3, starting transfers between devices, per_device(): lax.ppermute(side_rows[s - 1], 'batch', flipped(batch_size, CORES, s))  4.18 us
    ppermute x3, starting transfers between devices, per_device(): lax.ppermute(column, 'batch', flipped(batch_size, CORES * SIDE, s))  4.09 us
    ppermute x3, waiting for transfers between devices, per_device(): lax.ppermute(tokens, 'batch', flipped(batch_size, CORES, s))  2.43 us
    pallas_call x1, Pallas kernels, per_device(): call(depth_kernel, 'depth', pltpu.HBM((count, width), bf16), [VMEM] * (SI...  2.35 us
  transfers between devices with their start and end apart: 15, of which 4 were waited for; matrix products, arithmetic and copies ran while one was open for 0% of the time, Pallas kernels for 13%

profile of v6, /device:TPU:4, one launch (start us, length us, event | category | flops | bytes accessed | tf_op | source)
XLA Modules:
  0.0 45.4 jit_solution(5619154822923068452)
XLA Ops:
  0.6 0.0 copy-start
  0.6 0.0 copy-start.6
  0.7 0.0 copy-start.2
  0.7 0.0 copy-start.1
  0.7 0.0 copy-start.5
  0.7 0.0 copy-start.4
  0.7 0.0 copy-start.3
  0.7 3.3 %collective-permute-start.1 = (s32[1,2,8]{2,1,0:T(2,128)}, s32[1,2,8]{2,1,0:T(2,128)S(1)}, u32[]{:S(2)}, u32[]{:S(2)}) collective-permute-start(s32[1,2,8]{2,1,0:T(2,128)} %refs_0_.1), channel_id=1, source_target_pairs={{0,32},{8,40},{16,48},{24,56},{32,0},{40,8},{48,16},{56,24},{64,96... | collective-permute-start | bytes 200 | tf_op jit(solution)/shard_map/ppermute | solution.py:329
  4.0 0.7 %collective-permute-start = (s32[1,2,8]{2,1,0:T(2,128)}, s32[1,2,8]{2,1,0:T(2,128)S(1)}, u32[]{:S(2)}, u32[]{:S(2)}) collective-permute-start(s32[1,2,8]{2,1,0:T(2,128)} %refs_0_.1), channel_id=1, source_target_pairs={{0,16},{8,24},{16,0},{24,8},{32,48},{40,56},{48,32},{56,40},{64,80... | collective-permute-start | bytes 200 | tf_op jit(solution)/shard_map/ppermute | solution.py:329
  4.7 0.4 collective-permute-start.2
  5.0 0.0 collective-permute-start.6
  5.0 0.0 copy-start.10
  5.0 0.0 copy-done
  5.1 0.0 copy-done.6
  5.1 0.0 copy-done.2
  5.1 0.0 copy-done.1
  5.1 0.0 copy-done.5
  5.1 0.0 copy-done.4
  5.1 0.0 copy-done.3
  5.1 2.1 %attend.1.refs_4_ = bf16[8,16,512]{2,1,0:T(8,128)(2,1)} custom-call(s32[1,8]{1,0:T(1,128)S(1)} %bitcast.6, bf16[8,2,256]{2,1,0:T(2,128)(2,1)S(1)} %copy-done.3, bf16[8,2,256]{2,1,0:T(2,128)(2,1)S(1)} %copy-done.4, bf16[8,2,256]{2,1,0:T(2,128)(2,1)S(1)} %copy-done.5, bf16[8,256,256]{2,1,0:T(8,128)(2,1)S(1)} %copy-done.1, bf16[8,256,256]{2,1,0:T(8,128)(2,1)S(1)} %copy-done.2, ...), custom_call_target="tpu_custom_call" | custom-call | flops 100000000 | bytes 4194304 | tf_op jit(solution)/shard_map/attend/pallas_call | solution.py:330
  7.2 0.0 copy-start.7
  7.2 0.0 collective-permute-done.1.refs_2_
  7.2 0.5 %collective-permute-done.refs_1_ = s32[1,2,8]{2,1,0:T(2,128)S(1)} collective-permute-done((s32[1,2,8]{2,1,0:T(2,128)}, s32[1,2,8]{2,1,0:T(2,128)S(1)}, u32[]{:S(2)}, u32[]{:S(2)}) %collective-permute-start) | collective-permute-done | bytes 96 | tf_op jit(solution)/shard_map/ppermute | solution.py:329
  7.8 1.9 %collective-permute-done.2.refs_3_ = s32[1,2,8]{2,1,0:T(2,128)S(1)} collective-permute-done((s32[1,2,8]{2,1,0:T(2,128)}, s32[1,2,8]{2,1,0:T(2,128)S(1)}, u32[]{:S(2)}, u32[]{:S(2)}) %collective-permute-start.2) | collective-permute-done | bytes 96 | tf_op jit(solution)/shard_map/ppermute | solution.py:329
  9.7 0.0 copy-done.10
  9.7 0.5 %collective-permute-start.5 = (s32[4,2,8]{2,1,0:T(2,128)S(1)}, s32[4,2,8]{2,1,0:T(2,128)S(1)}, u32[]{:S(2)}, u32[]{:S(2)}) collective-permute-start(s32[4,2,8]{2,1,0:T(2,128)S(1)} %gather.1.refs_0_), channel_id=1, source_target_pairs={{0,192},{8,200},{16,208},{24,216},{32,224},{40,232},{48,240},{56,2... | collective-permute-start | bytes 776 | tf_op jit(solution)/shard_map/ppermute | solution.py:365
  10.2 2.7 %collective-permute-start.4 = (s32[4,2,8]{2,1,0:T(2,128)S(1)}, s32[4,2,8]{2,1,0:T(2,128)S(1)}, u32[]{:S(2)}, u32[]{:S(2)}) collective-permute-start(s32[4,2,8]{2,1,0:T(2,128)S(1)} %gather.1.refs_0_), channel_id=1, source_target_pairs={{0,128},{8,136},{16,144},{24,152},{32,160},{40,168},{48,176},{56,1... | collective-permute-start | bytes 776 | tf_op jit(solution)/shard_map/ppermute | solution.py:365
  12.9 0.8 %collective-permute-start.3 = (s32[4,2,8]{2,1,0:T(2,128)S(1)}, s32[4,2,8]{2,1,0:T(2,128)S(1)}, u32[]{:S(2)}, u32[]{:S(2)}) collective-permute-start(s32[4,2,8]{2,1,0:T(2,128)S(1)} %gather.1.refs_0_), channel_id=1, source_target_pairs={{0,64},{8,72},{16,80},{24,88},{32,96},{40,104},{48,112},{56,120},{... | collective-permute-start | bytes 776 | tf_op jit(solution)/shard_map/ppermute | solution.py:365
  13.8 9.2 %all-to-all-start = ((bf16[8,16,512]{2,1,0:T(8,128)(2,1)}), bf16[8,16,512]{2,1,0:T(8,128)(2,1)S(1)}, u32[]{:S(2)}, u32[]{:S(2)}) async-start(bf16[8,16,512]{2,1,0:T(8,128)(2,1)} %attend.1.refs_4_), calls=%async_computation | async-start | bytes 262144 | tf_op jit(solution)/shard_map/all_to_all | solution.py:367
  22.9 0.0 collective-permute-done.5.refs_3_
  22.9 0.0 collective-permute-done.4.refs_2_
  22.9 0.0 collective-permute-done.3.refs_1_
  22.9 0.0 collective-permute-done.6.refs_5_
  23.0 0.0 copy-done.7
  23.0 1.0 %lookup.1 = (bf16[4,16,1024]{2,1,0:T(8,128)(2,1)S(1)}, bf16[4,16,1024]{2,1,0:T(8,128)(2,1)S(1)}, bf16[4,16,1024]{2,1,0:T(8,128)(2,1)S(1)}, bf16[4,16,1024]{2,1,0:T(8,128)(2,1)S(1)}) custom-call(s32[4,2,8]{2,1,0:T(2,128)S(1)} %gather.1.refs_0_, s32[4,2,8]{2,1,0:T(2,128)S(1)} %collective-permute-done.3.refs_1_, s32[4,2,8]{2,1,0:T(2,128)S(1)} %collective-permute-done.4.refs_2_, ...), custom_call_target="tpu_custom_call" | custom-call | flops 99999997952 | bytes 1 | tf_op jit(solution)/shard_map/lookup/pallas_call | solution.py:371
  24.0 0.0 copy-start.12
  24.0 0.0 copy-start.8
  24.0 0.0 copy-start.9
  24.0 0.0 copy-start.11
  24.0 0.6 %collective-permute-start.7 = (bf16[4,16,1024]{2,1,0:T(8,128)(2,1)S(1)}, bf16[4,16,1024]{2,1,0:T(8,128)(2,1)S(1)}, u32[]{:S(2)}, u32[]{:S(2)}) collective-permute-start(bf16[4,16,1024]{2,1,0:T(8,128)(2,1)S(1)} %get-tuple-element.25), channel_id=1, source_target_pairs={{0,128},{8,136},{16,144},{24,152},{32,160},{40,168},{48,176},{56,1... | collective-permute-start | bytes 393224 | tf_op jit(solution)/shard_map/ppermute | solution.py:389
  24.6 2.1 %collective-permute-start.8 = (bf16[4,16,1024]{2,1,0:T(8,128)(2,1)S(1)}, bf16[4,16,1024]{2,1,0:T(8,128)(2,1)S(1)}, u32[]{:S(2)}, u32[]{:S(2)}) collective-permute-start(bf16[4,16,1024]{2,1,0:T(8,128)(2,1)S(1)} %get-tuple-element.26), channel_id=1, source_target_pairs={{0,64},{8,72},{16,80},{24,88},{32,96},{40,104},{48,112},{56,120},{... | collective-permute-start | bytes 393224 | tf_op jit(solution)/shard_map/ppermute | solution.py:389
  26.7 1.5 %collective-permute-start.9 = (bf16[4,16,1024]{2,1,0:T(8,128)(2,1)S(1)}, bf16[4,16,1024]{2,1,0:T(8,128)(2,1)S(1)}, u32[]{:S(2)}, u32[]{:S(2)}) collective-permute-start(bf16[4,16,1024]{2,1,0:T(8,128)(2,1)S(1)} %get-tuple-element.27), channel_id=1, source_target_pairs={{0,192},{8,200},{16,208},{24,216},{32,224},{40,232},{48,240},{56,2... | collective-permute-start | bytes 393224 | tf_op jit(solution)/shard_map/ppermute | solution.py:389
  28.2 0.0 copy-done.12
  28.2 0.4 all-to-all-done.shares_ref
  28.6 0.0 copy-done.8
  28.6 0.0 copy-done.9
  28.6 0.9 %middle.1 = (bf16[8,2,512]{2,1,0:T(2,128)(2,1)}, f32[8,2,1152]{2,1,0:T(2,128)}) custom-call(bf16[8,16,512]{2,1,0:T(8,128)(2,1)S(1)} %all-to-all-done.shares_ref, bf16[8,2,512]{2,1,0:T(2,128)(2,1)S(1)} %copy-done.9, f32[1,512]{1,0:T(1,128)S(1)} %bitcast.5, bf16[512,1024]{1,0:T(8,128)(2,1)S(1)} %copy-done.8, f32[8,128]{1,0:T(8,128)S(1)} %warm_in.1.order_ref), custom_call_target="tpu_custom_call" | custom-call | flops 1000000000 | bytes 1 | tf_op jit(solution)/shard_map/middle/pallas_call | solution.py:407
  29.5 6.8 %all-to-all-start.1 = ((f32[8,2,1152]{2,1,0:T(2,128)}), f32[8,2,1152]{2,1,0:T(2,128)S(1)}, u32[]{:S(2)}, u32[]{:S(2)}) async-start(f32[8,2,1152]{2,1,0:T(2,128)} %get-tuple-element.23), calls=%async_computation.1 | async-start | bytes 147456 | tf_op jit(solution)/shard_map/all_to_all | solution.py:421
  36.3 0.0 copy-done.11
  36.3 0.0 collective-permute-done.7.refs_0_
  36.4 0.0 collective-permute-done.8.refs_1_
  36.4 0.0 collective-permute-done.9.refs_2_
  36.4 0.8 %collective-permute-start.10 = (bf16[16,1024]{1,0:T(8,128)(2,1)S(1)}, bf16[16,1024]{1,0:T(8,128)(2,1)S(1)}, u32[]{:S(2)}, u32[]{:S(2)}) collective-permute-start(bf16[16,1024]{1,0:T(8,128)(2,1)S(1)} %get-tuple-element.29), channel_id=1, source_target_pairs={{0,32},{8,40},{16,48},{24,56},{32,0},{40,8},{48,16},{56,24},{64,96... | collective-permute-start | bytes 98312 | tf_op jit(solution)/shard_map/ppermute | solution.py:404
  37.2 0.7 %collective-permute-start.11 = (bf16[16,1024]{1,0:T(8,128)(2,1)S(1)}, bf16[16,1024]{1,0:T(8,128)(2,1)S(1)}, u32[]{:S(2)}, u32[]{:S(2)}) collective-permute-start(bf16[16,1024]{1,0:T(8,128)(2,1)S(1)} %get-tuple-element.30), channel_id=1, source_target_pairs={{0,16},{8,24},{16,0},{24,8},{32,48},{40,56},{48,32},{56,40},{64,80... | collective-permute-start | bytes 98312 | tf_op jit(solution)/shard_map/ppermute | solution.py:404
  37.9 2.7 %collective-permute-start.12 = (bf16[16,1024]{1,0:T(8,128)(2,1)S(1)}, bf16[16,1024]{1,0:T(8,128)(2,1)S(1)}, u32[]{:S(2)}, u32[]{:S(2)}) collective-permute-start(bf16[16,1024]{1,0:T(8,128)(2,1)S(1)} %get-tuple-element.31), channel_id=1, source_target_pairs={{0,48},{8,56},{16,32},{24,40},{32,16},{40,24},{48,0},{56,8},{64,11... | collective-permute-start | bytes 98312 | tf_op jit(solution)/shard_map/ppermute | solution.py:404
  40.6 1.9 %fetch.1.refs_5_ = bf16[1024,1536]{1,0:T(8,128)(2,1)S(1)} custom-call(bf16[1024,1536]{1,0:T(8,128)(2,1)} %refs_6_.1, bf16[512,1024]{1,0:T(8,128)(2,1)} %refs_7_.1, bf16[16,1024]{1,0:T(8,128)(2,1)S(1)} %get-tuple-element.28.order_ref.refs_0_), custom_call_target="tpu_custom_call" | custom-call | flops 1000000000 | bytes 1 | tf_op jit(solution)/shard_map/fetch/pallas_call | solution.py:425
  42.5 0.0 all-to-all-done.1.terms_ref
  42.5 0.0 collective-permute-done.10.refs_1_
  42.5 0.0 collective-permute-done.11.refs_2_
  42.5 0.5 %collective-permute-done.12.refs_3_ = bf16[16,1024]{1,0:T(8,128)(2,1)S(1)} collective-permute-done((bf16[16,1024]{1,0:T(8,128)(2,1)S(1)}, bf16[16,1024]{1,0:T(8,128)(2,1)S(1)}, u32[]{:S(2)}, u32[]{:S(2)}) %collective-permute-start.12) | collective-permute-done | bytes 32800 | tf_op jit(solution)/shard_map/ppermute | solution.py:404
  43.0 2.3 %depth.1 = bf16[16,1024]{1,0:T(8,128)(2,1)} custom-call(f32[8,2,1152]{2,1,0:T(2,128)S(1)} %all-to-all-done.1.terms_ref, bf16[16,1024]{1,0:T(8,128)(2,1)S(1)} %get-tuple-element.28.order_ref.refs_0_, bf16[16,1024]{1,0:T(8,128)(2,1)S(1)} %collective-permute-done.10.refs_1_, bf16[16,1024]{1,0:T(8,128)(2,1)S(1)} %collective-permute-done.11.refs_2_, ...), custom_call_target="tpu_custom_call" | custom-call | flops 1000000000 | bytes 1 | tf_op jit(solution)/shard_map/depth/pallas_call | solution.py:436
  (6 shorter events, 0.0 us)
Async XLA Ops:
  0.6 4.4 %copy-start = (bf16[256,4096]{1,0:T(8,128)(2,1)S(1)}, bf16[256,4096]{1,0:T(8,128)(2,1)}, u32[]{:S(2)}) copy-start(bf16[256,4096]{1,0:T(8,128)(2,1)} %w_ref.2) | copy-start | bytes 6291460
  0.6 4.4 %copy-start.6 = (s32[8]{0:T(128)S(1)}, s32[8]{0:T(128)}, u32[]{:S(2)}) copy-start(s32[8]{0:T(128)} %param.21) | copy-start | bytes 100
  0.7 4.4 %copy-start.2 = (bf16[8,256,256]{2,1,0:T(8,128)(2,1)S(1)}, bf16[8,256,256]{2,1,0:T(8,128)(2,1)}, u32[]{:S(2)}) copy-start(bf16[8,256,256]{2,1,0:T(8,128)(2,1)} %v_ref.1) | copy-start | bytes 3145732
  0.7 4.4 %copy-start.1 = (bf16[8,256,256]{2,1,0:T(8,128)(2,1)S(1)}, bf16[8,256,256]{2,1,0:T(8,128)(2,1)}, u32[]{:S(2)}) copy-start(bf16[8,256,256]{2,1,0:T(8,128)(2,1)} %k_ref.1) | copy-start | bytes 3145732
  0.7 4.4 %copy-start.5 = (bf16[8,2,256]{2,1,0:T(2,128)(2,1)S(1)}, bf16[8,2,256]{2,1,0:T(2,128)(2,1)}, u32[]{:S(2)}) copy-start(bf16[8,2,256]{2,1,0:T(2,128)(2,1)} %nv_ref.1) | copy-start | bytes 24580
  0.7 4.4 %copy-start.4 = (bf16[8,2,256]{2,1,0:T(2,128)(2,1)S(1)}, bf16[8,2,256]{2,1,0:T(2,128)(2,1)}, u32[]{:S(2)}) copy-start(bf16[8,2,256]{2,1,0:T(2,128)(2,1)} %nk_ref.1) | copy-start | bytes 24580
  0.7 4.4 %copy-start.3 = (bf16[8,2,256]{2,1,0:T(2,128)(2,1)S(1)}, bf16[8,2,256]{2,1,0:T(2,128)(2,1)}, u32[]{:S(2)}) copy-start(bf16[8,2,256]{2,1,0:T(2,128)(2,1)} %q_ref.1) | copy-start | bytes 24580
  0.7 6.5 %collective-permute-start.1 = (s32[1,2,8]{2,1,0:T(2,128)}, s32[1,2,8]{2,1,0:T(2,128)S(1)}, u32[]{:S(2)}, u32[]{:S(2)}) collective-permute-start(s32[1,2,8]{2,1,0:T(2,128)} %refs_0_.1), channel_id=1, source_target_pairs={{0,32},{8,40},{16,48},{24,56},{32,0},{40,8},{48,16},{56,24},{64,96... | collective-permute-start | bytes 200 | tf_op jit(solution)/shard_map/ppermute | solution.py:329
  4.0 3.8 %collective-permute-start = (s32[1,2,8]{2,1,0:T(2,128)}, s32[1,2,8]{2,1,0:T(2,128)S(1)}, u32[]{:S(2)}, u32[]{:S(2)}) collective-permute-start(s32[1,2,8]{2,1,0:T(2,128)} %refs_0_.1), channel_id=1, source_target_pairs={{0,16},{8,24},{16,0},{24,8},{32,48},{40,56},{48,32},{56,40},{64,80... | collective-permute-start | bytes 200 | tf_op jit(solution)/shard_map/ppermute | solution.py:329
  4.7 5.0 %collective-permute-start.2 = (s32[1,2,8]{2,1,0:T(2,128)}, s32[1,2,8]{2,1,0:T(2,128)S(1)}, u32[]{:S(2)}, u32[]{:S(2)}) collective-permute-start(s32[1,2,8]{2,1,0:T(2,128)} %refs_0_.1), channel_id=1, source_target_pairs={{0,48},{8,56},{16,32},{24,40},{32,16},{40,24},{48,0},{56,8},{64,11... | collective-permute-start | bytes 200 | tf_op jit(solution)/shard_map/ppermute | solution.py:329
  5.0 17.9 %collective-permute-start.6 = (bf16[8,64,1024]{2,1,0:T(8,128)(2,1)}, bf16[8,64,1024]{2,1,0:T(8,128)(2,1)S(1)}, u32[]{:S(2)}, u32[]{:S(2)}) collective-permute-start(bf16[8,64,1024]{2,1,0:T(8,128)(2,1)} %refs_4_.1), channel_id=1, source_target_pairs={{0,8},{8,0},{16,24},{24,16},{32,40},{40,32},{48,56},{56,48},{64,72... | collective-permute-start | bytes 3145736 | tf_op jit(solution)/shard_map/ppermute | solution.py:328
  5.0 4.6 %copy-start.10 = (s32[1,2,8]{2,1,0:T(2,128)S(1)}, s32[1,2,8]{2,1,0:T(2,128)}, u32[]{:S(2)}) copy-start(s32[1,2,8]{2,1,0:T(2,128)} %refs_0_.1) | copy-start | bytes 196
  7.2 15.8 %copy-start.7 = (bf16[8,64,1024]{2,1,0:T(8,128)(2,1)S(1)}, bf16[8,64,1024]{2,1,0:T(8,128)(2,1)}, u32[]{:S(2)}) copy-start(bf16[8,64,1024]{2,1,0:T(8,128)(2,1)} %refs_4_.1) | copy-start | bytes 3145732
  9.7 13.3 %collective-permute-start.5 = (s32[4,2,8]{2,1,0:T(2,128)S(1)}, s32[4,2,8]{2,1,0:T(2,128)S(1)}, u32[]{:S(2)}, u32[]{:S(2)}) collective-permute-start(s32[4,2,8]{2,1,0:T(2,128)S(1)} %gather.1.refs_0_), channel_id=1, source_target_pairs={{0,192},{8,200},{16,208},{24,216},{32,224},{40,232},{48,240},{56,2... | collective-permute-start | bytes 776 | tf_op jit(solution)/shard_map/ppermute | solution.py:365
  10.2 12.7 %collective-permute-start.4 = (s32[4,2,8]{2,1,0:T(2,128)S(1)}, s32[4,2,8]{2,1,0:T(2,128)S(1)}, u32[]{:S(2)}, u32[]{:S(2)}) collective-permute-start(s32[4,2,8]{2,1,0:T(2,128)S(1)} %gather.1.refs_0_), channel_id=1, source_target_pairs={{0,128},{8,136},{16,144},{24,152},{32,160},{40,168},{48,176},{56,1... | collective-permute-start | bytes 776 | tf_op jit(solution)/shard_map/ppermute | solution.py:365
  12.9 10.0 %collective-permute-start.3 = (s32[4,2,8]{2,1,0:T(2,128)S(1)}, s32[4,2,8]{2,1,0:T(2,128)S(1)}, u32[]{:S(2)}, u32[]{:S(2)}) collective-permute-start(s32[4,2,8]{2,1,0:T(2,128)S(1)} %gather.1.refs_0_), channel_id=1, source_target_pairs={{0,64},{8,72},{16,80},{24,88},{32,96},{40,104},{48,112},{56,120},{... | collective-permute-start | bytes 776 | tf_op jit(solution)/shard_map/ppermute | solution.py:365
  13.8 14.8 %all-to-all-start = ((bf16[8,16,512]{2,1,0:T(8,128)(2,1)}), bf16[8,16,512]{2,1,0:T(8,128)(2,1)S(1)}, u32[]{:S(2)}, u32[]{:S(2)}) async-start(bf16[8,16,512]{2,1,0:T(8,128)(2,1)} %attend.1.refs_4_), calls=%async_computation | async-start | bytes 262144 | tf_op jit(solution)/shard_map/all_to_all | solution.py:367
  24.0 4.2 %copy-start.12 = (bf16[512]{0:T(512)(128)(2,1)S(1)}, bf16[512]{0:T(512)(128)(2,1)}, u32[]{:S(2)}) copy-start(bf16[512]{0:T(512)(128)(2,1)} %param.23) | copy-start | bytes 3076
  24.0 4.6 %copy-start.8 = (bf16[512,1024]{1,0:T(8,128)(2,1)S(1)}, bf16[512,1024]{1,0:T(8,128)(2,1)}, u32[]{:S(2)}) copy-start(bf16[512,1024]{1,0:T(8,128)(2,1)} %w_ref.3) | copy-start | bytes 3145732
  24.0 4.6 %copy-start.9 = (bf16[8,2,512]{2,1,0:T(2,128)(2,1)S(1)}, bf16[8,2,512]{2,1,0:T(2,128)(2,1)}, u32[]{:S(2)}) copy-start(bf16[8,2,512]{2,1,0:T(2,128)(2,1)} %residual_ref.1) | copy-start | bytes 49156
  24.0 12.3 %copy-start.11 = (bf16[1024]{0:T(1024)(128)(2,1)S(1)}, bf16[1024]{0:T(1024)(128)(2,1)}, u32[]{:S(2)}) copy-start(bf16[1024]{0:T(1024)(128)(2,1)} %param.27) | copy-start | bytes 6148
  24.0 12.3 %collective-permute-start.7 = (bf16[4,16,1024]{2,1,0:T(8,128)(2,1)S(1)}, bf16[4,16,1024]{2,1,0:T(8,128)(2,1)S(1)}, u32[]{:S(2)}, u32[]{:S(2)}) collective-permute-start(bf16[4,16,1024]{2,1,0:T(8,128)(2,1)S(1)} %get-tuple-element.25), channel_id=1, source_target_pairs={{0,128},{8,136},{16,144},{24,152},{32,160},{40,168},{48,176},{56,1... | collective-permute-start | bytes 393224 | tf_op jit(solution)/shard_map/ppermute | solution.py:389
  24.6 11.7 %collective-permute-start.8 = (bf16[4,16,1024]{2,1,0:T(8,128)(2,1)S(1)}, bf16[4,16,1024]{2,1,0:T(8,128)(2,1)S(1)}, u32[]{:S(2)}, u32[]{:S(2)}) collective-permute-start(bf16[4,16,1024]{2,1,0:T(8,128)(2,1)S(1)} %get-tuple-element.26), channel_id=1, source_target_pairs={{0,64},{8,72},{16,80},{24,88},{32,96},{40,104},{48,112},{56,120},{... | collective-permute-start | bytes 393224 | tf_op jit(solution)/shard_map/ppermute | solution.py:389
  26.7 9.7 %collective-permute-start.9 = (bf16[4,16,1024]{2,1,0:T(8,128)(2,1)S(1)}, bf16[4,16,1024]{2,1,0:T(8,128)(2,1)S(1)}, u32[]{:S(2)}, u32[]{:S(2)}) collective-permute-start(bf16[4,16,1024]{2,1,0:T(8,128)(2,1)S(1)} %get-tuple-element.27), channel_id=1, source_target_pairs={{0,192},{8,200},{16,208},{24,216},{32,224},{40,232},{48,240},{56,2... | collective-permute-start | bytes 393224 | tf_op jit(solution)/shard_map/ppermute | solution.py:389
  29.5 13.0 %all-to-all-start.1 = ((f32[8,2,1152]{2,1,0:T(2,128)}), f32[8,2,1152]{2,1,0:T(2,128)S(1)}, u32[]{:S(2)}, u32[]{:S(2)}) async-start(f32[8,2,1152]{2,1,0:T(2,128)} %get-tuple-element.23), calls=%async_computation.1 | async-start | bytes 147456 | tf_op jit(solution)/shard_map/all_to_all | solution.py:421
  36.4 6.1 %collective-permute-start.10 = (bf16[16,1024]{1,0:T(8,128)(2,1)S(1)}, bf16[16,1024]{1,0:T(8,128)(2,1)S(1)}, u32[]{:S(2)}, u32[]{:S(2)}) collective-permute-start(bf16[16,1024]{1,0:T(8,128)(2,1)S(1)} %get-tuple-element.29), channel_id=1, source_target_pairs={{0,32},{8,40},{16,48},{24,56},{32,0},{40,8},{48,16},{56,24},{64,96... | collective-permute-start | bytes 98312 | tf_op jit(solution)/shard_map/ppermute | solution.py:404
  37.2 5.3 %collective-permute-start.11 = (bf16[16,1024]{1,0:T(8,128)(2,1)S(1)}, bf16[16,1024]{1,0:T(8,128)(2,1)S(1)}, u32[]{:S(2)}, u32[]{:S(2)}) collective-permute-start(bf16[16,1024]{1,0:T(8,128)(2,1)S(1)} %get-tuple-element.30), channel_id=1, source_target_pairs={{0,16},{8,24},{16,0},{24,8},{32,48},{40,56},{48,32},{56,40},{64,80... | collective-permute-start | bytes 98312 | tf_op jit(solution)/shard_map/ppermute | solution.py:404
  37.9 5.1 %collective-permute-start.12 = (bf16[16,1024]{1,0:T(8,128)(2,1)S(1)}, bf16[16,1024]{1,0:T(8,128)(2,1)S(1)}, u32[]{:S(2)}, u32[]{:S(2)}) collective-permute-start(bf16[16,1024]{1,0:T(8,128)(2,1)S(1)} %get-tuple-element.31), channel_id=1, source_target_pairs={{0,48},{8,56},{16,32},{24,40},{32,16},{40,24},{48,0},{56,8},{64,11... | collective-permute-start | bytes 98312 | tf_op jit(solution)/shard_map/ppermute | solution.py:404

commit v7 on v6

--- a/solution.py
+++ b/solution.py
@@ -326,7 +326,7 @@
         warm_kernel, "warm", pltpu.VMEM((8, 128), f32), [], VMEM, [], LIMIT, WARM_FLOPS, 1
     )()
     other_tables = lax.ppermute(level_tables, "batch", flipped(batch_size, 1, 1))
-    near = [lax.ppermute(tokens, "batch", flipped(batch_size, CORES, s)) for s in STEPS]
+    near = [lax.ppermute(tokens, "batch", flipped(batch_size, CORES, s)) for s in range(1, SIDE)]
     head_terms = call(
         attend_kernel,
         "attend",
@@ -361,7 +361,7 @@
         LIMIT,
         GATHER_FLOPS,
         1,
-    )(tokens, *sorted_steps(near), head_terms)
+    )(tokens, *near, head_terms)
     ids = [lax.ppermute(column, "batch", flipped(batch_size, CORES * SIDE, s)) for s in STEPS]
 
     shares = lax.all_to_all(

time: 45.7 us -> 45.7 us (level)
  no operation moved by 1% of the time
where the time goes in v7:
time: 45.7 us; the launch traced here: 45.4 us
  starting transfers between devices  32.8 us (72%)
  Pallas kernels  8.27 us (18%)
  waiting for transfers between devices  3.35 us (7%)
  between operations  0.92 us (2%)
    all_to_all x1, starting transfers between devices, per_device(): lax.all_to_all(head_terms, 'tensor', 0, 0, axis_index_groups=backward, ti...  9.17 us
    all_to_all x1, starting transfers between devices, per_device(): lax.all_to_all(sent, 'tensor', 0, 0, axis_index_groups=backward, tiled=True)  6.81 us
    ppermute x3, starting transfers between devices, per_device(): lax.ppermute(tokens, 'batch', flipped(batch_size, CORES, s))  4.34 us
    ppermute x3, starting transfers between devices, per_device(): lax.ppermute(partial_rows[s], 'batch', flipped(batch_size, CORES * SIDE, s))  4.18 us
    ppermute x3, starting transfers between devices, per_device(): lax.ppermute(side_rows[s - 1], 'batch', flipped(batch_size, CORES, s))  4.18 us
    ppermute x3, starting transfers between devices, per_device(): lax.ppermute(column, 'batch', flipped(batch_size, CORES * SIDE, s))  4.09 us
    ppermute x3, waiting for transfers between devices, per_device(): lax.ppermute(tokens, 'batch', flipped(batch_size, CORES, s))  2.43 us
    pallas_call x1, Pallas kernels, per_device(): call(depth_kernel, 'depth', pltpu.HBM((count, width), bf16), [VMEM] * (SI...  2.35 us
  transfers between devices with their start and end apart: 15, of which 4 were waited for; matrix products, arithmetic and copies ran while one was open for 0% of the time, Pallas kernels for 13%

profile of v7, /device:TPU:4, one launch (start us, length us, event | category | flops | bytes accessed | tf_op | source)
XLA Modules:
  0.0 45.4 jit_solution(5619154822923068452)
XLA Ops:
  0.6 0.0 copy-start
  0.6 0.0 copy-start.6
  0.7 0.0 copy-start.2
  0.7 0.0 copy-start.1
  0.7 0.0 copy-start.5
  0.7 0.0 copy-start.4
  0.7 0.0 copy-start.3
  0.7 3.3 %collective-permute-start.1 = (s32[1,2,8]{2,1,0:T(2,128)}, s32[1,2,8]{2,1,0:T(2,128)S(1)}, u32[]{:S(2)}, u32[]{:S(2)}) collective-permute-start(s32[1,2,8]{2,1,0:T(2,128)} %refs_0_.1), channel_id=1, source_target_pairs={{0,32},{8,40},{16,48},{24,56},{32,0},{40,8},{48,16},{56,24},{64,96... | collective-permute-start | bytes 200 | tf_op jit(solution)/shard_map/ppermute | solution.py:329
  4.0 0.7 %collective-permute-start = (s32[1,2,8]{2,1,0:T(2,128)}, s32[1,2,8]{2,1,0:T(2,128)S(1)}, u32[]{:S(2)}, u32[]{:S(2)}) collective-permute-start(s32[1,2,8]{2,1,0:T(2,128)} %refs_0_.1), channel_id=1, source_target_pairs={{0,16},{8,24},{16,0},{24,8},{32,48},{40,56},{48,32},{56,40},{64,80... | collective-permute-start | bytes 200 | tf_op jit(solution)/shard_map/ppermute | solution.py:329
  4.7 0.4 collective-permute-start.2
  5.0 0.0 collective-permute-start.6
  5.0 0.0 copy-start.10
  5.0 0.0 copy-done
  5.1 0.0 copy-done.6
  5.1 0.0 copy-done.2
  5.1 0.0 copy-done.1
  5.1 0.0 copy-done.5
  5.1 0.0 copy-done.4
  5.1 0.0 copy-done.3
  5.1 2.1 %attend.1.refs_4_ = bf16[8,16,512]{2,1,0:T(8,128)(2,1)} custom-call(s32[1,8]{1,0:T(1,128)S(1)} %bitcast.6, bf16[8,2,256]{2,1,0:T(2,128)(2,1)S(1)} %copy-done.3, bf16[8,2,256]{2,1,0:T(2,128)(2,1)S(1)} %copy-done.4, bf16[8,2,256]{2,1,0:T(2,128)(2,1)S(1)} %copy-done.5, bf16[8,256,256]{2,1,0:T(8,128)(2,1)S(1)} %copy-done.1, bf16[8,256,256]{2,1,0:T(8,128)(2,1)S(1)} %copy-done.2, ...), custom_call_target="tpu_custom_call" | custom-call | flops 100000000 | bytes 4194304 | tf_op jit(solution)/shard_map/attend/pallas_call | solution.py:330
  7.2 0.0 copy-start.7
  7.2 0.0 collective-permute-done.1.refs_2_
  7.2 0.5 %collective-permute-done.refs_1_ = s32[1,2,8]{2,1,0:T(2,128)S(1)} collective-permute-done((s32[1,2,8]{2,1,0:T(2,128)}, s32[1,2,8]{2,1,0:T(2,128)S(1)}, u32[]{:S(2)}, u32[]{:S(2)}) %collective-permute-start) | collective-permute-done | bytes 96 | tf_op jit(solution)/shard_map/ppermute | solution.py:329
  7.8 1.9 %collective-permute-done.2.refs_3_ = s32[1,2,8]{2,1,0:T(2,128)S(1)} collective-permute-done((s32[1,2,8]{2,1,0:T(2,128)}, s32[1,2,8]{2,1,0:T(2,128)S(1)}, u32[]{:S(2)}, u32[]{:S(2)}) %collective-permute-start.2) | collective-permute-done | bytes 96 | tf_op jit(solution)/shard_map/ppermute | solution.py:329
  9.7 0.0 copy-done.10
  9.7 0.5 %collective-permute-start.5 = (s32[4,2,8]{2,1,0:T(2,128)S(1)}, s32[4,2,8]{2,1,0:T(2,128)S(1)}, u32[]{:S(2)}, u32[]{:S(2)}) collective-permute-start(s32[4,2,8]{2,1,0:T(2,128)S(1)} %gather.1.refs_0_), channel_id=1, source_target_pairs={{0,192},{8,200},{16,208},{24,216},{32,224},{40,232},{48,240},{56,2... | collective-permute-start | bytes 776 | tf_op jit(solution)/shard_map/ppermute | solution.py:365
  10.2 2.7 %collective-permute-start.4 = (s32[4,2,8]{2,1,0:T(2,128)S(1)}, s32[4,2,8]{2,1,0:T(2,128)S(1)}, u32[]{:S(2)}, u32[]{:S(2)}) collective-permute-start(s32[4,2,8]{2,1,0:T(2,128)S(1)} %gather.1.refs_0_), channel_id=1, source_target_pairs={{0,128},{8,136},{16,144},{24,152},{32,160},{40,168},{48,176},{56,1... | collective-permute-start | bytes 776 | tf_op jit(solution)/shard_map/ppermute | solution.py:365
  12.9 0.8 %collective-permute-start.3 = (s32[4,2,8]{2,1,0:T(2,128)S(1)}, s32[4,2,8]{2,1,0:T(2,128)S(1)}, u32[]{:S(2)}, u32[]{:S(2)}) collective-permute-start(s32[4,2,8]{2,1,0:T(2,128)S(1)} %gather.1.refs_0_), channel_id=1, source_target_pairs={{0,64},{8,72},{16,80},{24,88},{32,96},{40,104},{48,112},{56,120},{... | collective-permute-start | bytes 776 | tf_op jit(solution)/shard_map/ppermute | solution.py:365
  13.8 9.2 %all-to-all-start = ((bf16[8,16,512]{2,1,0:T(8,128)(2,1)}), bf16[8,16,512]{2,1,0:T(8,128)(2,1)S(1)}, u32[]{:S(2)}, u32[]{:S(2)}) async-start(bf16[8,16,512]{2,1,0:T(8,128)(2,1)} %attend.1.refs_4_), calls=%async_computation | async-start | bytes 262144 | tf_op jit(solution)/shard_map/all_to_all | solution.py:367
  22.9 0.0 collective-permute-done.5.refs_3_
  22.9 0.0 collective-permute-done.4.refs_2_
  22.9 0.0 collective-permute-done.3.refs_1_
  22.9 0.0 collective-permute-done.6.refs_5_
  23.0 0.0 copy-done.7
  23.0 1.0 %lookup.1 = (bf16[4,16,1024]{2,1,0:T(8,128)(2,1)S(1)}, bf16[4,16,1024]{2,1,0:T(8,128)(2,1)S(1)}, bf16[4,16,1024]{2,1,0:T(8,128)(2,1)S(1)}, bf16[4,16,1024]{2,1,0:T(8,128)(2,1)S(1)}) custom-call(s32[4,2,8]{2,1,0:T(2,128)S(1)} %gather.1.refs_0_, s32[4,2,8]{2,1,0:T(2,128)S(1)} %collective-permute-done.3.refs_1_, s32[4,2,8]{2,1,0:T(2,128)S(1)} %collective-permute-done.4.refs_2_, ...), custom_call_target="tpu_custom_call" | custom-call | flops 99999997952 | bytes 1 | tf_op jit(solution)/shard_map/lookup/pallas_call | solution.py:371
  24.0 0.0 copy-start.12
  24.0 0.0 copy-start.8
  24.0 0.0 copy-start.9
  24.0 0.0 copy-start.11
  24.0 0.6 %collective-permute-start.7 = (bf16[4,16,1024]{2,1,0:T(8,128)(2,1)S(1)}, bf16[4,16,1024]{2,1,0:T(8,128)(2,1)S(1)}, u32[]{:S(2)}, u32[]{:S(2)}) collective-permute-start(bf16[4,16,1024]{2,1,0:T(8,128)(2,1)S(1)} %get-tuple-element.25), channel_id=1, source_target_pairs={{0,128},{8,136},{16,144},{24,152},{32,160},{40,168},{48,176},{56,1... | collective-permute-start | bytes 393224 | tf_op jit(solution)/shard_map/ppermute | solution.py:389
  24.6 2.1 %collective-permute-start.8 = (bf16[4,16,1024]{2,1,0:T(8,128)(2,1)S(1)}, bf16[4,16,1024]{2,1,0:T(8,128)(2,1)S(1)}, u32[]{:S(2)}, u32[]{:S(2)}) collective-permute-start(bf16[4,16,1024]{2,1,0:T(8,128)(2,1)S(1)} %get-tuple-element.26), channel_id=1, source_target_pairs={{0,64},{8,72},{16,80},{24,88},{32,96},{40,104},{48,112},{56,120},{... | collective-permute-start | bytes 393224 | tf_op jit(solution)/shard_map/ppermute | solution.py:389
  26.7 1.5 %collective-permute-start.9 = (bf16[4,16,1024]{2,1,0:T(8,128)(2,1)S(1)}, bf16[4,16,1024]{2,1,0:T(8,128)(2,1)S(1)}, u32[]{:S(2)}, u32[]{:S(2)}) collective-permute-start(bf16[4,16,1024]{2,1,0:T(8,128)(2,1)S(1)} %get-tuple-element.27), channel_id=1, source_target_pairs={{0,192},{8,200},{16,208},{24,216},{32,224},{40,232},{48,240},{56,2... | collective-permute-start | bytes 393224 | tf_op jit(solution)/shard_map/ppermute | solution.py:389
  28.2 0.0 copy-done.12
  28.2 0.4 all-to-all-done.shares_ref
  28.6 0.0 copy-done.8
  28.6 0.0 copy-done.9
  28.6 0.9 %middle.1 = (bf16[8,2,512]{2,1,0:T(2,128)(2,1)}, f32[8,2,1152]{2,1,0:T(2,128)}) custom-call(bf16[8,16,512]{2,1,0:T(8,128)(2,1)S(1)} %all-to-all-done.shares_ref, bf16[8,2,512]{2,1,0:T(2,128)(2,1)S(1)} %copy-done.9, f32[1,512]{1,0:T(1,128)S(1)} %bitcast.5, bf16[512,1024]{1,0:T(8,128)(2,1)S(1)} %copy-done.8, f32[8,128]{1,0:T(8,128)S(1)} %warm_in.1.order_ref), custom_call_target="tpu_custom_call" | custom-call | flops 1000000000 | bytes 1 | tf_op jit(solution)/shard_map/middle/pallas_call | solution.py:407
  29.5 6.8 %all-to-all-start.1 = ((f32[8,2,1152]{2,1,0:T(2,128)}), f32[8,2,1152]{2,1,0:T(2,128)S(1)}, u32[]{:S(2)}, u32[]{:S(2)}) async-start(f32[8,2,1152]{2,1,0:T(2,128)} %get-tuple-element.23), calls=%async_computation.1 | async-start | bytes 147456 | tf_op jit(solution)/shard_map/all_to_all | solution.py:421
  36.3 0.0 copy-done.11
  36.3 0.0 collective-permute-done.7.refs_0_
  36.4 0.0 collective-permute-done.8.refs_1_
  36.4 0.0 collective-permute-done.9.refs_2_
  36.4 0.8 %collective-permute-start.10 = (bf16[16,1024]{1,0:T(8,128)(2,1)S(1)}, bf16[16,1024]{1,0:T(8,128)(2,1)S(1)}, u32[]{:S(2)}, u32[]{:S(2)}) collective-permute-start(bf16[16,1024]{1,0:T(8,128)(2,1)S(1)} %get-tuple-element.29), channel_id=1, source_target_pairs={{0,32},{8,40},{16,48},{24,56},{32,0},{40,8},{48,16},{56,24},{64,96... | collective-permute-start | bytes 98312 | tf_op jit(solution)/shard_map/ppermute | solution.py:404
  37.2 0.7 %collective-permute-start.11 = (bf16[16,1024]{1,0:T(8,128)(2,1)S(1)}, bf16[16,1024]{1,0:T(8,128)(2,1)S(1)}, u32[]{:S(2)}, u32[]{:S(2)}) collective-permute-start(bf16[16,1024]{1,0:T(8,128)(2,1)S(1)} %get-tuple-element.30), channel_id=1, source_target_pairs={{0,16},{8,24},{16,0},{24,8},{32,48},{40,56},{48,32},{56,40},{64,80... | collective-permute-start | bytes 98312 | tf_op jit(solution)/shard_map/ppermute | solution.py:404
  37.9 2.7 %collective-permute-start.12 = (bf16[16,1024]{1,0:T(8,128)(2,1)S(1)}, bf16[16,1024]{1,0:T(8,128)(2,1)S(1)}, u32[]{:S(2)}, u32[]{:S(2)}) collective-permute-start(bf16[16,1024]{1,0:T(8,128)(2,1)S(1)} %get-tuple-element.31), channel_id=1, source_target_pairs={{0,48},{8,56},{16,32},{24,40},{32,16},{40,24},{48,0},{56,8},{64,11... | collective-permute-start | bytes 98312 | tf_op jit(solution)/shard_map/ppermute | solution.py:404
  40.6 1.9 %fetch.1.refs_5_ = bf16[1024,1536]{1,0:T(8,128)(2,1)S(1)} custom-call(bf16[1024,1536]{1,0:T(8,128)(2,1)} %refs_6_.1, bf16[512,1024]{1,0:T(8,128)(2,1)} %refs_7_.1, bf16[16,1024]{1,0:T(8,128)(2,1)S(1)} %get-tuple-element.28.order_ref.refs_0_), custom_call_target="tpu_custom_call" | custom-call | flops 1000000000 | bytes 1 | tf_op jit(solution)/shard_map/fetch/pallas_call | solution.py:425
  42.5 0.0 all-to-all-done.1.terms_ref
  42.5 0.0 collective-permute-done.10.refs_1_
  42.5 0.0 collective-permute-done.11.refs_2_
  42.5 0.5 %collective-permute-done.12.refs_3_ = bf16[16,1024]{1,0:T(8,128)(2,1)S(1)} collective-permute-done((bf16[16,1024]{1,0:T(8,128)(2,1)S(1)}, bf16[16,1024]{1,0:T(8,128)(2,1)S(1)}, u32[]{:S(2)}, u32[]{:S(2)}) %collective-permute-start.12) | collective-permute-done | bytes 32800 | tf_op jit(solution)/shard_map/ppermute | solution.py:404
  43.0 2.3 %depth.1 = bf16[16,1024]{1,0:T(8,128)(2,1)} custom-call(f32[8,2,1152]{2,1,0:T(2,128)S(1)} %all-to-all-done.1.terms_ref, bf16[16,1024]{1,0:T(8,128)(2,1)S(1)} %get-tuple-element.28.order_ref.refs_0_, bf16[16,1024]{1,0:T(8,128)(2,1)S(1)} %collective-permute-done.10.refs_1_, bf16[16,1024]{1,0:T(8,128)(2,1)S(1)} %collective-permute-done.11.refs_2_, ...), custom_call_target="tpu_custom_call" | custom-call | flops 1000000000 | bytes 1 | tf_op jit(solution)/shard_map/depth/pallas_call | solution.py:436
  (6 shorter events, 0.0 us)
Async XLA Ops:
  0.6 4.4 %copy-start = (bf16[256,4096]{1,0:T(8,128)(2,1)S(1)}, bf16[256,4096]{1,0:T(8,128)(2,1)}, u32[]{:S(2)}) copy-start(bf16[256,4096]{1,0:T(8,128)(2,1)} %w_ref.2) | copy-start | bytes 6291460
  0.6 4.4 %copy-start.6 = (s32[8]{0:T(128)S(1)}, s32[8]{0:T(128)}, u32[]{:S(2)}) copy-start(s32[8]{0:T(128)} %param.21) | copy-start | bytes 100
  0.7 4.4 %copy-start.2 = (bf16[8,256,256]{2,1,0:T(8,128)(2,1)S(1)}, bf16[8,256,256]{2,1,0:T(8,128)(2,1)}, u32[]{:S(2)}) copy-start(bf16[8,256,256]{2,1,0:T(8,128)(2,1)} %v_ref.1) | copy-start | bytes 3145732
  0.7 4.4 %copy-start.1 = (bf16[8,256,256]{2,1,0:T(8,128)(2,1)S(1)}, bf16[8,256,256]{2,1,0:T(8,128)(2,1)}, u32[]{:S(2)}) copy-start(bf16[8,256,256]{2,1,0:T(8,128)(2,1)} %k_ref.1) | copy-start | bytes 3145732
  0.7 4.4 %copy-start.5 = (bf16[8,2,256]{2,1,0:T(2,128)(2,1)S(1)}, bf16[8,2,256]{2,1,0:T(2,128)(2,1)}, u32[]{:S(2)}) copy-start(bf16[8,2,256]{2,1,0:T(2,128)(2,1)} %nv_ref.1) | copy-start | bytes 24580
  0.7 4.4 %copy-start.4 = (bf16[8,2,256]{2,1,0:T(2,128)(2,1)S(1)}, bf16[8,2,256]{2,1,0:T(2,128)(2,1)}, u32[]{:S(2)}) copy-start(bf16[8,2,256]{2,1,0:T(2,128)(2,1)} %nk_ref.1) | copy-start | bytes 24580
  0.7 4.4 %copy-start.3 = (bf16[8,2,256]{2,1,0:T(2,128)(2,1)S(1)}, bf16[8,2,256]{2,1,0:T(2,128)(2,1)}, u32[]{:S(2)}) copy-start(bf16[8,2,256]{2,1,0:T(2,128)(2,1)} %q_ref.1) | copy-start | bytes 24580
  0.7 6.5 %collective-permute-start.1 = (s32[1,2,8]{2,1,0:T(2,128)}, s32[1,2,8]{2,1,0:T(2,128)S(1)}, u32[]{:S(2)}, u32[]{:S(2)}) collective-permute-start(s32[1,2,8]{2,1,0:T(2,128)} %refs_0_.1), channel_id=1, source_target_pairs={{0,32},{8,40},{16,48},{24,56},{32,0},{40,8},{48,16},{56,24},{64,96... | collective-permute-start | bytes 200 | tf_op jit(solution)/shard_map/ppermute | solution.py:329
  4.0 3.8 %collective-permute-start = (s32[1,2,8]{2,1,0:T(2,128)}, s32[1,2,8]{2,1,0:T(2,128)S(1)}, u32[]{:S(2)}, u32[]{:S(2)}) collective-permute-start(s32[1,2,8]{2,1,0:T(2,128)} %refs_0_.1), channel_id=1, source_target_pairs={{0,16},{8,24},{16,0},{24,8},{32,48},{40,56},{48,32},{56,40},{64,80... | collective-permute-start | bytes 200 | tf_op jit(solution)/shard_map/ppermute | solution.py:329
  4.7 5.0 %collective-permute-start.2 = (s32[1,2,8]{2,1,0:T(2,128)}, s32[1,2,8]{2,1,0:T(2,128)S(1)}, u32[]{:S(2)}, u32[]{:S(2)}) collective-permute-start(s32[1,2,8]{2,1,0:T(2,128)} %refs_0_.1), channel_id=1, source_target_pairs={{0,48},{8,56},{16,32},{24,40},{32,16},{40,24},{48,0},{56,8},{64,11... | collective-permute-start | bytes 200 | tf_op jit(solution)/shard_map/ppermute | solution.py:329
  5.0 17.9 %collective-permute-start.6 = (bf16[8,64,1024]{2,1,0:T(8,128)(2,1)}, bf16[8,64,1024]{2,1,0:T(8,128)(2,1)S(1)}, u32[]{:S(2)}, u32[]{:S(2)}) collective-permute-start(bf16[8,64,1024]{2,1,0:T(8,128)(2,1)} %refs_4_.1), channel_id=1, source_target_pairs={{0,8},{8,0},{16,24},{24,16},{32,40},{40,32},{48,56},{56,48},{64,72... | collective-permute-start | bytes 3145736 | tf_op jit(solution)/shard_map/ppermute | solution.py:328
  5.0 4.6 %copy-start.10 = (s32[1,2,8]{2,1,0:T(2,128)S(1)}, s32[1,2,8]{2,1,0:T(2,128)}, u32[]{:S(2)}) copy-start(s32[1,2,8]{2,1,0:T(2,128)} %refs_0_.1) | copy-start | bytes 196
  7.2 15.8 %copy-start.7 = (bf16[8,64,1024]{2,1,0:T(8,128)(2,1)S(1)}, bf16[8,64,1024]{2,1,0:T(8,128)(2,1)}, u32[]{:S(2)}) copy-start(bf16[8,64,1024]{2,1,0:T(8,128)(2,1)} %refs_4_.1) | copy-start | bytes 3145732
  9.7 13.3 %collective-permute-start.5 = (s32[4,2,8]{2,1,0:T(2,128)S(1)}, s32[4,2,8]{2,1,0:T(2,128)S(1)}, u32[]{:S(2)}, u32[]{:S(2)}) collective-permute-start(s32[4,2,8]{2,1,0:T(2,128)S(1)} %gather.1.refs_0_), channel_id=1, source_target_pairs={{0,192},{8,200},{16,208},{24,216},{32,224},{40,232},{48,240},{56,2... | collective-permute-start | bytes 776 | tf_op jit(solution)/shard_map/ppermute | solution.py:365
  10.2 12.7 %collective-permute-start.4 = (s32[4,2,8]{2,1,0:T(2,128)S(1)}, s32[4,2,8]{2,1,0:T(2,128)S(1)}, u32[]{:S(2)}, u32[]{:S(2)}) collective-permute-start(s32[4,2,8]{2,1,0:T(2,128)S(1)} %gather.1.refs_0_), channel_id=1, source_target_pairs={{0,128},{8,136},{16,144},{24,152},{32,160},{40,168},{48,176},{56,1... | collective-permute-start | bytes 776 | tf_op jit(solution)/shard_map/ppermute | solution.py:365
  12.9 10.0 %collective-permute-start.3 = (s32[4,2,8]{2,1,0:T(2,128)S(1)}, s32[4,2,8]{2,1,0:T(2,128)S(1)}, u32[]{:S(2)}, u32[]{:S(2)}) collective-permute-start(s32[4,2,8]{2,1,0:T(2,128)S(1)} %gather.1.refs_0_), channel_id=1, source_target_pairs={{0,64},{8,72},{16,80},{24,88},{32,96},{40,104},{48,112},{56,120},{... | collective-permute-start | bytes 776 | tf_op jit(solution)/shard_map/ppermute | solution.py:365
  13.8 14.8 %all-to-all-start = ((bf16[8,16,512]{2,1,0:T(8,128)(2,1)}), bf16[8,16,512]{2,1,0:T(8,128)(2,1)S(1)}, u32[]{:S(2)}, u32[]{:S(2)}) async-start(bf16[8,16,512]{2,1,0:T(8,128)(2,1)} %attend.1.refs_4_), calls=%async_computation | async-start | bytes 262144 | tf_op jit(solution)/shard_map/all_to_all | solution.py:367
  24.0 4.2 %copy-start.12 = (bf16[512]{0:T(512)(128)(2,1)S(1)}, bf16[512]{0:T(512)(128)(2,1)}, u32[]{:S(2)}) copy-start(bf16[512]{0:T(512)(128)(2,1)} %param.23) | copy-start | bytes 3076
  24.0 4.6 %copy-start.8 = (bf16[512,1024]{1,0:T(8,128)(2,1)S(1)}, bf16[512,1024]{1,0:T(8,128)(2,1)}, u32[]{:S(2)}) copy-start(bf16[512,1024]{1,0:T(8,128)(2,1)} %w_ref.3) | copy-start | bytes 3145732
  24.0 4.6 %copy-start.9 = (bf16[8,2,512]{2,1,0:T(2,128)(2,1)S(1)}, bf16[8,2,512]{2,1,0:T(2,128)(2,1)}, u32[]{:S(2)}) copy-start(bf16[8,2,512]{2,1,0:T(2,128)(2,1)} %residual_ref.1) | copy-start | bytes 49156
  24.0 12.3 %copy-start.11 = (bf16[1024]{0:T(1024)(128)(2,1)S(1)}, bf16[1024]{0:T(1024)(128)(2,1)}, u32[]{:S(2)}) copy-start(bf16[1024]{0:T(1024)(128)(2,1)} %param.27) | copy-start | bytes 6148
  24.0 12.3 %collective-permute-start.7 = (bf16[4,16,1024]{2,1,0:T(8,128)(2,1)S(1)}, bf16[4,16,1024]{2,1,0:T(8,128)(2,1)S(1)}, u32[]{:S(2)}, u32[]{:S(2)}) collective-permute-start(bf16[4,16,1024]{2,1,0:T(8,128)(2,1)S(1)} %get-tuple-element.25), channel_id=1, source_target_pairs={{0,128},{8,136},{16,144},{24,152},{32,160},{40,168},{48,176},{56,1... | collective-permute-start | bytes 393224 | tf_op jit(solution)/shard_map/ppermute | solution.py:389
  24.6 11.7 %collective-permute-start.8 = (bf16[4,16,1024]{2,1,0:T(8,128)(2,1)S(1)}, bf16[4,16,1024]{2,1,0:T(8,128)(2,1)S(1)}, u32[]{:S(2)}, u32[]{:S(2)}) collective-permute-start(bf16[4,16,1024]{2,1,0:T(8,128)(2,1)S(1)} %get-tuple-element.26), channel_id=1, source_target_pairs={{0,64},{8,72},{16,80},{24,88},{32,96},{40,104},{48,112},{56,120},{... | collective-permute-start | bytes 393224 | tf_op jit(solution)/shard_map/ppermute | solution.py:389
  26.7 9.7 %collective-permute-start.9 = (bf16[4,16,1024]{2,1,0:T(8,128)(2,1)S(1)}, bf16[4,16,1024]{2,1,0:T(8,128)(2,1)S(1)}, u32[]{:S(2)}, u32[]{:S(2)}) collective-permute-start(bf16[4,16,1024]{2,1,0:T(8,128)(2,1)S(1)} %get-tuple-element.27), channel_id=1, source_target_pairs={{0,192},{8,200},{16,208},{24,216},{32,224},{40,232},{48,240},{56,2... | collective-permute-start | bytes 393224 | tf_op jit(solution)/shard_map/ppermute | solution.py:389
  29.5 13.0 %all-to-all-start.1 = ((f32[8,2,1152]{2,1,0:T(2,128)}), f32[8,2,1152]{2,1,0:T(2,128)S(1)}, u32[]{:S(2)}, u32[]{:S(2)}) async-start(f32[8,2,1152]{2,1,0:T(2,128)} %get-tuple-element.23), calls=%async_computation.1 | async-start | bytes 147456 | tf_op jit(solution)/shard_map/all_to_all | solution.py:421
  36.4 6.1 %collective-permute-start.10 = (bf16[16,1024]{1,0:T(8,128)(2,1)S(1)}, bf16[16,1024]{1,0:T(8,128)(2,1)S(1)}, u32[]{:S(2)}, u32[]{:S(2)}) collective-permute-start(bf16[16,1024]{1,0:T(8,128)(2,1)S(1)} %get-tuple-element.29), channel_id=1, source_target_pairs={{0,32},{8,40},{16,48},{24,56},{32,0},{40,8},{48,16},{56,24},{64,96... | collective-permute-start | bytes 98312 | tf_op jit(solution)/shard_map/ppermute | solution.py:404
  37.2 5.3 %collective-permute-start.11 = (bf16[16,1024]{1,0:T(8,128)(2,1)S(1)}, bf16[16,1024]{1,0:T(8,128)(2,1)S(1)}, u32[]{:S(2)}, u32[]{:S(2)}) collective-permute-start(bf16[16,1024]{1,0:T(8,128)(2,1)S(1)} %get-tuple-element.30), channel_id=1, source_target_pairs={{0,16},{8,24},{16,0},{24,8},{32,48},{40,56},{48,32},{56,40},{64,80... | collective-permute-start | bytes 98312 | tf_op jit(solution)/shard_map/ppermute | solution.py:404
  37.9 5.1 %collective-permute-start.12 = (bf16[16,1024]{1,0:T(8,128)(2,1)S(1)}, bf16[16,1024]{1,0:T(8,128)(2,1)S(1)}, u32[]{:S(2)}, u32[]{:S(2)}) collective-permute-start(bf16[16,1024]{1,0:T(8,128)(2,1)S(1)} %get-tuple-element.31), channel_id=1, source_target_pairs={{0,48},{8,56},{16,32},{24,40},{32,16},{40,24},{48,0},{56,8},{64,11... | collective-permute-start | bytes 98312 | tf_op jit(solution)/shard_map/ppermute | solution.py:404
